TPU v7x, 128 devices: a whole 4x4x4 slice. The times are simulated.
128 devices in a mesh: ctx: 64 (over z, y_hi, x, core), head: 2 (over y_lo).
Axes of the slice: x: 4, y: 4 (y_hi: 2, y_lo: 2; y = y_hi * 2 + y_lo), z: 4, core: 2. Of those that a mesh axis runs over, the one named last changes fastest.
Arguments:
- tokens: bfloat16 [49152, 1024], P('ctx')
- qkv_weight: bfloat16 [1024, 3, 1024], P('ctx', None, 'head'), may hold values from -0.1875 to 0.1875
- grad_attn: bfloat16 [49152, 1024], P('ctx', 'head'), may hold values from -6 to 6
- positions: int32 [49152], P('ctx'), may hold values from 0 to 3145727, as said below
- slopes: float32 [16], P('head'), may hold values from 0.03 to 0.6
Outputs:
- d_tokens: bfloat16 [49152, 1024], P('ctx')
- d_weight: float32 [1024, 3, 1024], P('ctx', None, 'head')
Inputs may be any that keep to these rules, and one draw needn't show every extreme that they name: positions rise strictly along the sequence, start at 0 and end at 3145727; neighbours differ by 1 to 127.
All inputs are finite; a program needn't handle non-finite values.
Results may differ from a plain program's by a relative error of at most 0.006.
The roundings to bfloat16 on the way count: a program that leaves them out, or rounds other values in their place, can miss the bound.
Values may be sent and summed in bfloat16 or wider, within the bound.
No kernel may reach another device: no remote copies, remote signals or barrier semaphores. Data moves between devices by JAX's collectives and lax.ppermute only.
A program may use at most 128 MiB of HBM per device.

v0:
```python
import jax
import jax.numpy as jnp
from jax import lax
from jax.sharding import PartitionSpec as P


def from_partner(value, axis, apart):
    mask = 2**apart
    pairs = [(source, source ^ mask) for source in range(lax.axis_size(axis))]
    return lax.ppermute(value, axis, pairs)


def one_head_grads(items, logd, scale):
    q_head, k_head, v_head, g_head, slope = items
    score = (
        jnp.einsum("qe,ke->qk", q_head, k_head, preferred_element_type=jnp.float32) * scale
        - slope * logd
    )
    top = jnp.max(score, axis=-1, keepdims=True)
    expd = jnp.exp(score - top)
    prob = expd / jnp.sum(expd, axis=-1, keepdims=True)
    prob_round = prob.astype(jnp.bfloat16)
    outv = jnp.dot(prob_round, v_head, preferred_element_type=jnp.float32)
    delta = jnp.sum(g_head.astype(jnp.float32) * outv, axis=-1, keepdims=True)
    dprob = jnp.einsum("qe,ke->qk", g_head, v_head, preferred_element_type=jnp.float32)
    dscore = (prob * (dprob - delta) * scale).astype(jnp.bfloat16)
    dq = jnp.dot(dscore, k_head, preferred_element_type=jnp.float32).astype(jnp.bfloat16)
    dk = jnp.einsum("qk,qe->ke", dscore, q_head, preferred_element_type=jnp.float32)
    dv = jnp.einsum("qk,qe->ke", prob_round, g_head, preferred_element_type=jnp.float32)
    return (dq, dk, dv)


def on_device(tokens, qkv_weight, grad_attn, positions, slopes):
    rows = tokens.shape[0]
    heads_local = slopes.shape[0]
    local_width = qkv_weight.shape[2]
    head_size = local_width // heads_local
    scale = head_size ** (-0.5)
    full_weight = lax.all_gather(qkv_weight, "ctx", axis=0, tiled=True)
    qkv = jnp.einsum("sd,dcf->scf", tokens, full_weight, preferred_element_type=jnp.float32).astype(
        jnp.bfloat16
    )

    def split_heads(array):
        return array.reshape(rows, heads_local, head_size).transpose(1, 0, 2)

    def merge_heads(array):
        return array.transpose(1, 0, 2).reshape(rows, local_width)

    top_bit = lax.axis_size("ctx").bit_length() - 2
    far_keys, far_values, far_pos = from_partner((qkv[:, 1], qkv[:, 2], positions), "ctx", top_bit)
    keys_all = jnp.concatenate([split_heads(qkv[:, 1]), split_heads(far_keys)], 1)
    values_all = jnp.concatenate([split_heads(qkv[:, 2]), split_heads(far_values)], 1)
    pos_all = jnp.concatenate([positions, far_pos], 0)
    logd = jnp.log1p(jnp.abs(positions[:, None] - pos_all[None, :]).astype(jnp.float32))

    def per_head(items):
        return one_head_grads(items, logd, scale)

    dq, dk_all, dv_all = lax.map(
        per_head, (split_heads(qkv[:, 0]), keys_all, values_all, split_heads(grad_attn), slopes)
    )
    back_keys, back_values = from_partner((dk_all[:, rows:], dv_all[:, rows:]), "ctx", top_bit)
    dk = (dk_all[:, :rows] + back_keys).astype(jnp.bfloat16)
    dv = (dv_all[:, :rows] + back_values).astype(jnp.bfloat16)
    dqkv = jnp.stack([merge_heads(dq), merge_heads(dk), merge_heads(dv)], 1)
    partial_rows = jnp.einsum("scf,dcf->sd", dqkv, full_weight, preferred_element_type=jnp.float32)
    d_tokens = lax.psum(partial_rows, "head").astype(jnp.bfloat16)
    term = jnp.einsum("sd,scf->dcf", tokens, dqkv, preferred_element_type=jnp.float32)
    d_weight = lax.psum_scatter(term, "ctx", scatter_dimension=0, tiled=True)
    return (d_tokens, d_weight)


def solution(mesh):
    placed = (P("ctx", None), P("ctx", None, "head"), P("ctx", "head"), P("ctx"), P("head"))
    return jax.shard_map(
        on_device,
        mesh=mesh,
        in_specs=placed,
        out_specs=(P("ctx", None), P("ctx", None, "head")),
        check_vma=False,
    )
```

profile of v0, /device:TPU:0, one launch (start us, length us, event | category | flops | bytes accessed | tf_op | source)
XLA Modules:
  0.0 1035.6 jit_solution(3913822468340966411)
XLA Ops:
  8.0 75.9 %all-gather.2.cloned.1.call-done = bf16[1024,3,512]{2,0,1:T(8,128)(2,1)} async-done(((bf16[16,3,512]{2,0,1:T(8,128)(2,1)}), bf16[1024,3,512]{2,0,1:T(8,128)(2,1)}) %all-gather.2.cloned.1.call-update) | async-done | bytes 3145744 | tf_op jit(solution)/shard_map/all_gather | solution.py:39
  83.8 4.5 convolution_convert_fusion.1
  91.6 2.1 collective-permute-start
  96.6 32.0 %collective-permute-done.1 = s32[768]{0:T(1024)S(1)} collective-permute-done((s32[768]{0:T(1024)S(1)}, s32[768]{0:T(1024)S(1)}, u32[]{:S(2)}, u32[]{:S(2)}) %collective-permute-start.1) | collective-permute-done | bytes 3104 | tf_op jit(solution)/shard_map/ppermute | solution.py:10
  128.6 2.5 copy.33
  131.0 2.5 copy.30
  135.0 2.5 copy.34
  137.5 2.5 copy.31
  139.9 5.2 pad_maximum_fusion
  145.1 131.1 %while.15 = (s32[]{:T(128)}, bf16[8,768,64]{1,2,0:T(8,128)(2,1)S(1)}, f32[8,1536,64]{1,2,0:T(8,128)}, f32[8,1536,64]{1,2,0:T(8,128)}, bf16[8,768,64]{2,1,0:T(8,1...) while((s32[]{:T(128)}, ...), condition=%wide.region_4.5_spmd.clone, body=%wide.region_0.4_spmd.clone.sunk | while | flops 926217984 | bytes 43292288 | solution.py:60
  145.7 4.6 fusion.77
  153.9 2.1 multiply_convert_fusion.2
  156.1 2.3 fusion.82
  162.0 4.6 fusion.77
  168.4 1.9 fusion.80
  170.3 2.1 multiply_convert_fusion.2
  172.4 2.3 fusion.82
  178.4 4.6 fusion.77
  186.7 2.1 multiply_convert_fusion.2
  188.8 2.3 fusion.82
  194.8 4.6 fusion.77
  201.2 1.9 fusion.80
  203.1 2.1 multiply_convert_fusion.2
  205.2 2.3 fusion.82
  211.2 4.6 fusion.77
  219.4 2.1 multiply_convert_fusion.2
  221.6 2.3 fusion.82
  227.6 4.6 fusion.77
  235.8 2.1 multiply_convert_fusion.2
  238.0 2.3 fusion.82
  244.0 4.6 fusion.77
  252.2 2.1 multiply_convert_fusion.2
  254.3 2.3 fusion.82
  260.4 4.6 fusion.77
  268.6 2.1 multiply_convert_fusion.2
  270.7 2.3 fusion.82
  280.2 2.7 slice.29
  282.8 2.1 collective-permute-start.4
  284.9 2.3 copy.35
  287.2 30.4 %collective-permute-done.3 = f32[8,768,64]{1,2,0:T(8,128)} collective-permute-done((f32[8,768,64]{1,2,0:T(8,128)S(1)}, f32[8,768,64]{1,2,0:T(8,128)}, u32[]{:S(2)}, u32[]{:S(2)}) %collective-permute-start.3) | collective-permute-done | bytes 1572896 | tf_op jit(solution)/shard_map/ppermute | solution.py:10
  317.7 2.0 add_convert_fusion.1
  320.9 29.0 %collective-permute-done.4 = f32[8,768,64]{1,2,0:T(8,128)} collective-permute-done((f32[8,768,64]{1,2,0:T(8,128)}, f32[8,768,64]{1,2,0:T(8,128)}, u32[]{:S(2)}, u32[]{:S(2)}) %collective-permute-start.4) | collective-permute-done | bytes 1572896 | tf_op jit(solution)/shard_map/ppermute | solution.py:10
  349.8 2.0 add_convert_fusion
  353.0 6.0 convolution_bitcast_fusion.2
  359.0 9.4 copy.39
  370.3 6.5 convolution_bitcast_fusion.3
  376.8 87.9 %all-reduce.5 = bf16[768,1024]{1,0:T(8,128)(2,1)} all-reduce(f32[768,1024]{1,0:T(8,128)} %convolution_bitcast_fusion.3), channel_id=1, replica_groups=mesh['ctx'=64,'head'=2] {'head'}, use_global_device_ids=true, to_apply=%region_5.6 | all-reduce | flops 786432 | bytes 4718592 | tf_op jit(solution)/shard_map/psum | solution.py:68
  464.7 562.5 %all-reduce.4.cloned.1.call-done = f32[1024,3,512]{2,1,0:T(4,128)} async-done(((f32[1024,3,512]{2,1,0:T(4,128)}), f32[1024,3,512]{2,1,0:T(4,128)}) %all-reduce.4.cloned.1.call-update) | async-done | bytes 6291472
  (84 shorter events, 72.5 us)
Async XLA Ops:
  7.2 76.7 %copy-start = (bf16[768,1024]{1,0:T(8,128)(2,1)S(1)}, bf16[768,1024]{1,0:T(8,128)(2,1)}, u32[]{:S(2)}) copy-start(bf16[768,1024]{1,0:T(8,128)(2,1)} %param.7) | copy-start | bytes 4718596
  7.2 76.6 %all-gather.2.cloned.1.call-start = ((), (), s32[]{:S(2)}) async-start(), calls=%async_computation | async-start | bytes 3194880 | tf_op jit(solution)/shard_map/all_gather | solution.py:39
  7.9 1019.3 %all-reduce.4.cloned.1.call-start = ((), (), s32[]{:S(2)}) async-start(), calls=%async_computation.1 | async-start | bytes 16777216
  88.4 5.3 copy-start.5
  90.2 44.9 %collective-permute-start.2 = (bf16[768,512]{0,1:T(8,128)(2,1)}, bf16[768,512]{0,1:T(8,128)(2,1)}, u32[]{:S(2)}, u32[]{:S(2)}) collective-permute-start(bf16[768,512]{0,1:T(8,128)(2,1)} %get-tuple-element.117), channel_id=1, source_target_pairs={{0,64},{2,66},{4,68},{6,70},{8,72},{10,74},{12,76},{14,78},{16,80}... | collective-permute-start | bytes 2359304 | tf_op jit(solution)/shard_map/ppermute | solution.py:10
  91.6 45.9 %collective-permute-start = (bf16[768,512]{0,1:T(8,128)(2,1)}, bf16[768,512]{0,1:T(8,128)(2,1)}, u32[]{:S(2)}, u32[]{:S(2)}) collective-permute-start(bf16[768,512]{0,1:T(8,128)(2,1)} %get-tuple-element.116), channel_id=1, source_target_pairs={{0,64},{2,66},{4,68},{6,70},{8,72},{10,74},{12,76},{14,78},{16,80}... | collective-permute-start | bytes 2359304 | tf_op jit(solution)/shard_map/ppermute | solution.py:10
  93.7 34.9 %collective-permute-start.1 = (s32[768]{0:T(1024)S(1)}, s32[768]{0:T(1024)S(1)}, u32[]{:S(2)}, u32[]{:S(2)}) collective-permute-start(s32[768]{0:T(1024)S(1)} %copy-done.5), channel_id=1, source_target_pairs={{0,64},{2,66},{4,68},{6,70},{8,72},{10,74},{12,76},{14,78},{16,80}... | collective-permute-start | bytes 9224 | tf_op jit(solution)/shard_map/ppermute | solution.py:10
  139.9 5.2 copy-start.2
  139.9 5.2 copy-start.6
  276.2 0.9 copy-start.3
  278.6 39.0 %collective-permute-start.3 = (f32[8,768,64]{1,2,0:T(8,128)S(1)}, f32[8,768,64]{1,2,0:T(8,128)}, u32[]{:S(2)}, u32[]{:S(2)}) collective-permute-start(f32[8,768,64]{1,2,0:T(8,128)S(1)} %slice.27), channel_id=1, source_target_pairs={{0,64},{2,66},{4,68},{6,70},{8,72},{10,74},{12,76},{14,78},{16,80}... | collective-permute-start | bytes 4718600 | tf_op jit(solution)/shard_map/ppermute | solution.py:10
  282.8 67.0 %collective-permute-start.4 = (f32[8,768,64]{1,2,0:T(8,128)}, f32[8,768,64]{1,2,0:T(8,128)}, u32[]{:S(2)}, u32[]{:S(2)}) collective-permute-start(f32[8,768,64]{1,2,0:T(8,128)} %slice.29), channel_id=1, source_target_pairs={{0,64},{2,66},{4,68},{6,70},{8,72},{10,74},{12,76},{14,78},{16,80}... | collective-permute-start | bytes 4718600 | tf_op jit(solution)/shard_map/ppermute | solution.py:10
  320.9 32.1 %copy-start.1 = (bf16[768,1,512]{2,0,1:T(8,128)(2,1)S(1)}, bf16[768,1,512]{2,0,1:T(8,128)(2,1)}, u32[]{:S(2)}) copy-start(bf16[768,1,512]{2,0,1:T(8,128)(2,1)} %copy.35) | copy-start | bytes 2359300
  368.4 0.7 copy-start.7
  368.4 1.9 copy-start.4
Sparse Core Ops, SparseCore 0:
  11.2 72.5 all-gather.1
  368.6 658.5 all-reduce.3
where the time goes:
time: 1040 us
  waiting for transfers between devices  730 us (70%)
  matrix products  129 us (12%)
  blocking collectives  87.9 us (8%)
  local copies, waits for them, and re-layouts  40.9 us (4%)
  other arithmetic  23.2 us (2%)
  between operations  14.8 us (1%)
    unnamed x3, waiting for transfers between devices  563 us
    ppermute x5, waiting for transfers between devices, from_partner(): return lax.ppermute(value, axis, pairs)  91.4 us
    psum x1, blocking collectives, on_device(): d_tokens = lax.psum(partial_rows, 'head').astype(jnp.bfloat16)  87.9 us
    all_gather x1, waiting for transfers between devices, on_device(): full_weight = lax.all_gather(qkv_weight, 'ctx', axis=0, tiled=True)  75.9 us
    dot_general x8, matrix products, one_head_grads(): jnp.einsum('qe,ke->qk', q_head, k_head, preferred_element_type=jnp.float32)  36.9 us
  transfers between devices with their start and end apart: 7, of which 5 were waited for; matrix products, arithmetic and copies ran while one was open for 2% of the time, Pallas kernels for 0%

commit v1 on v0

v1 whole, which is shorter than its diff:
```python
import jax
import jax.numpy as jnp
from jax import lax
from jax.experimental import pallas as pl
from jax.experimental.pallas import tpu as pltpu
from jax.sharding import PartitionSpec as P

BF = jnp.bfloat16
F32 = jnp.float32
TILE = 256


def swap(value, axis):
    return lax.ppermute(value, axis, [(0, 1), (1, 0)])


def dot(a, b, dims=((1,), (0,))):
    return lax.dot_general(a, b, (dims, ((), ())), preferred_element_type=F32)


def attention_kernel(
    slopes_ref, qo, qf, ko, kf, vo, vf, go, gf, logd_ref, near_ref, far_ref,
    q_s, k_s, v_s, g_s, kt_s, dk_s, dv_s, s_s, dp_s,
):
    step = pl.program_id(0)
    rows = qo.shape[0]
    total = 2 * rows
    chunks = total // TILE

    @pl.when(step == 0)
    def _():
        for scratch, near, far in ((q_s, qo, qf), (k_s, ko, kf), (v_s, vo, vf), (g_s, go, gf)):
            scratch[:rows] = near[...]
            scratch[rows:] = far[...]
        kt_s[...] = k_s[...].astype(F32).T.astype(BF)
        dk_s[...] = jnp.zeros_like(dk_s)
        dv_s[...] = jnp.zeros_like(dv_s)

    here = pl.ds(pl.multiple_of(step * TILE, TILE), TILE)
    q = (q_s[here].astype(F32) * 0.125)
    g = g_s[here].astype(F32)
    q_t, g_t = q.T, g.T
    upper = lax.broadcasted_iota(jnp.int32, (128, TILE), 0) < 64
    left = lax.broadcasted_iota(jnp.int32, (TILE, 128), 1) < 64
    zero = jnp.float32(0)
    qts = [jnp.where(upper, q_t, zero).astype(BF), jnp.where(upper, zero, q_t).astype(BF)]
    gts = [jnp.where(upper, g_t, zero).astype(BF), jnp.where(upper, zero, g_t).astype(BF)]
    qs = [jnp.where(left, q, zero).astype(BF), jnp.where(left, zero, q).astype(BF)]
    gs = [jnp.where(left, g, zero).astype(BF), jnp.where(left, zero, g).astype(BF)]
    for h in range(2):
        slope = slopes_ref[h]
        top = None
        for c in range(chunks):
            part = slice(c * TILE, (c + 1) * TILE)
            score = dot(k_s[part], qts[h]) - slope * logd_ref[part]
            s_s[h, part] = score
            peak = jnp.max(score, axis=0, keepdims=True)
            top = peak if top is None else jnp.maximum(top, peak)
        norm = jnp.zeros((1, TILE), F32)
        delta = jnp.zeros((1, TILE), F32)
        for c in range(chunks):
            part = slice(c * TILE, (c + 1) * TILE)
            e = jnp.exp(s_s[h, part] - top)
            s_s[h, part] = e
            dp = dot(v_s[part], gts[h])
            dp_s[h, part] = dp
            norm += jnp.sum(e, axis=0, keepdims=True)
            delta += jnp.sum(e * dp, axis=0, keepdims=True)
        inverse = 1.0 / norm
        delta = delta * inverse
        dq_t = jnp.zeros((64, TILE), F32)
        for c in range(chunks):
            part = slice(c * TILE, (c + 1) * TILE)
            p = s_s[h, part] * inverse
            ds = (p * (dp_s[h, part] - delta)).astype(BF)
            dv_s[part] += dot(p.astype(BF), gs[h])
            dk_s[part] += dot(ds, qs[h])
            dq_t += dot(kt_s[h * 64 : (h + 1) * 64, part], ds)
        s_s[h, :64] = dq_t
    dq = jnp.concatenate([s_s[0, :64], s_s[1, :64]], 0).T * 0.125
    local = pl.ds(pl.multiple_of(lax.rem(step, chunks // 2) * TILE, TILE), TILE)

    @pl.when(step < chunks // 2)
    def _():
        near_ref[local, :128] = dq.astype(BF)

    @pl.when(step >= chunks // 2)
    def _():
        far_ref[local, :128] = dq.astype(BF)

    @pl.when(step == chunks - 1)
    def _():
        near_ref[:, 128:256] = dk_s[:rows].astype(BF)
        near_ref[:, 256:384] = dv_s[:rows].astype(BF)
        far_ref[:, 128:256] = dk_s[rows:].astype(BF)
        far_ref[:, 256:384] = dv_s[rows:].astype(BF)


def attention(slopes, near, far, g_near, g_far, logd, pair):
    rows = near.shape[0]
    total = 2 * rows

    def column(block):
        return pl.BlockSpec((rows, 128), lambda t: (0, block))

    specs = []
    for c in range(3):
        specs += [column(3 * pair + c)] * 2
    return pl.pallas_call(
        attention_kernel,
        grid=(total // TILE,),
        in_specs=[pl.BlockSpec(memory_space=pltpu.SMEM)]
        + specs
        + [column(pair)] * 2
        + [pl.BlockSpec((total, TILE), lambda t: (0, t))],
        out_specs=[pl.BlockSpec((rows, 384), lambda t: (0, 0))] * 2,
        out_shape=[jax.ShapeDtypeStruct((rows, 384), BF)] * 2,
        scratch_shapes=[pltpu.VMEM((total, 128), BF)] * 4
        + [pltpu.VMEM((128, total), BF)]
        + [pltpu.VMEM((total, 128), F32)] * 2
        + [pltpu.VMEM((2, total, TILE), F32)] * 2,
        compiler_params=pltpu.CompilerParams(vmem_limit_bytes=32 * 2**20),
        cost_estimate=pl.CostEstimate(
            flops=2 * 5 * 2 * total * total * 256, bytes_accessed=4 * total * total, transcendentals=2 * total * total
        ),
    )(slopes, near, far, near, far, near, far, g_near, g_far, logd)


def by_core(own, other, core):
    stack = jnp.where(core == 0, jnp.stack([own, other], 1), jnp.stack([other, own], 1))
    return stack.reshape(1024, own.shape[2])


def own_core_first(array, core):
    split = array.reshape(32, 2, 16, array.shape[1])
    first, second = split[:, 0], split[:, 1]
    first, second = jnp.where(core == 0, first, second), jnp.where(core == 0, second, first)
    return jnp.concatenate([first.reshape(512, -1), second.reshape(512, -1)], 0)


def on_device(tokens, qkv_weight, grad_attn, positions, slopes):
    z_hi, core, head = lax.axis_index("zh"), lax.axis_index("c"), lax.axis_index("h")
    rows = tokens.shape[0]
    half, quarter = rows // 2, rows // 4

    with jax.named_scope("tokens"):
        send = [lax.dynamic_slice_in_dim(tokens, head * half + i * quarter, quarter, 0) for i in range(2)]
        got = [swap(part, "zh") for part in send]
        other = [swap(part, "h") for part in got]
        far_tokens = jnp.where(
            head == 0, jnp.concatenate(got + other, 0), jnp.concatenate(other + got, 0)
        )

    with jax.named_scope("weights"):
        w = qkv_weight.reshape(16, 3, 2, 2, 128).transpose(2, 0, 3, 1, 4).reshape(2, 1, 16, 768)
        w = jnp.broadcast_to(w, (2, 16, 16, 768)).reshape(32, 16, 768)
        w = lax.all_to_all(w, ("zh", "zl", "yh", "x"), 0, 0)
        w = by_core(w, swap(w, "c"), core)

    with jax.named_scope("bias"):
        g_near = lax.dynamic_slice_in_dim(grad_attn, z_hi * 256, 256, 1)
        g_far = swap(lax.dynamic_slice_in_dim(grad_attn, (1 - z_hi) * 256, 256, 1), "zh")
        pos = jnp.concatenate([positions, swap(positions, "zh")], 0)
        logd = jnp.log((1 + jnp.abs(pos[:, None] - pos[None, :])).astype(F32))
        slopes = lax.dynamic_slice_in_dim(slopes, z_hi * 4, 4, 0)

    with jax.named_scope("transposed"):
        near_t = own_core_first(tokens.T, core)
        far_t = own_core_first(far_tokens.T, core)
        near_t, far_t = lax.optimization_barrier((near_t, far_t))

    with jax.named_scope("projection"):
        near = dot(tokens, w).astype(BF)
        far = dot(far_tokens, w).astype(BF)
    with jax.named_scope("attention"):
        grads = [attention(slopes[2 * p : 2 * p + 2], near, far, g_near, g_far, logd, p) for p in range(2)]

    with jax.named_scope("d_tokens"):
        w_other = swap(w, "zh")
        total = 0.0
        for p in range(2):
            part = slice(384 * p, 384 * (p + 1))
            back = swap(grads[p][1], "zh")
            total = total + dot(grads[p][0], w[:, part], ((1,), (1,)))
            total = total + dot(back, w_other[:, part], ((1,), (1,)))
        total = total.astype(BF)
        outs = []
        for i in range(2):
            mine = total[i * half : (i + 1) * half]
            outs.append((mine.astype(F32) + swap(mine, "h").astype(F32)).astype(BF))
        d_tokens = jnp.concatenate(outs, 0)

    with jax.named_scope("d_weight"):
        terms = []
        for p in range(2):
            term = dot(near_t, grads[p][0]) + dot(far_t, grads[p][1])
            terms.append((term[:512] + swap(term[512:], "c")).astype(BF))
        term = jnp.concatenate(terms, 1).reshape(32, 16, 768)
        term = lax.all_to_all(term, ("zh", "zl", "yh", "x"), 0, 0)
        term = jnp.sum(term.reshape(2, 16, 16, 768).astype(F32), axis=1)
        d_weight = term.reshape(2, 16, 2, 3, 128).transpose(1, 3, 0, 2, 4).reshape(16, 3, 512)
    return d_tokens, d_weight


def solution(mesh):
    mesh = jax.sharding.Mesh(mesh.devices.reshape(2, 2, 2, 4, 2, 2), ("zh", "zl", "yh", "x", "c", "h"))
    ctx = ("zh", "zl", "yh", "x", "c")
    return jax.shard_map(
        on_device,
        mesh=mesh,
        in_specs=(P(ctx, None), P(ctx, None, "h"), P(ctx, "h"), P(ctx), P("h")),
        out_specs=(P(ctx, None), P(ctx, None, "h")),
        check_vma=False,
    )
```

time: 1040 us -> 198 us (0.19)
  waiting for transfers between devices: 730 us -> 72.8 us
  matrix products: 129 us -> 17.3 us
  blocking collectives: 87.9 us -> 0 us
  Pallas kernels: 0 us -> 42.9 us
  local copies, waits for them, and re-layouts: 40.9 us -> 11.7 us
  starting transfers between devices: 8.68 us -> 37 us
  between operations: 14.8 us -> 1.03 us
    unnamed x3 -> x0, waiting for transfers between devices: 563 us -> none
    dot_general x51 -> x10, matrix products: 129 us -> 17.3 us  [dot(): return lax.dot_general(a, b, (dims, ((), ())), preferred_element_type=F32)]
    psum x1 -> x0, blocking collectives: 87.9 us -> none  [on_device(): d_tokens = lax.psum(partial_rows, 'head').astype(jnp.bfloat16)]
    all_gather x1 -> x0, waiting for transfers between devices: 75.9 us -> none  [on_device(): full_weight = lax.all_gather(qkv_weight, 'ctx', axis=0, tiled=True)]
    pallas_call x0 -> x2, Pallas kernels: none -> 42.9 us  [attention(): pl.pallas_call(attention_kernel, grid=(total // TILE,), in_specs=[pl.Bloc...]
    ppermute x5 -> x14, waiting for transfers between devices: 91.4 us -> 66.3 us  [swap(): return lax.ppermute(value, axis, [(0, 1), (1, 0)])]
    all_to_all x0 -> x2, starting transfers between devices: none -> 15.7 us  [the longest x1 7.91 us: on_device(): term = lax.all_to_all(term, ('zh', 'zl', 'yh', 'x'), 0, 0)]
    ppermute x5 -> x14, starting transfers between devices: 8.6 us -> 21.3 us  [swap(): return lax.ppermute(value, axis, [(0, 1), (1, 0)])]
  transfers between devices with their start and end apart: 7 -> 16, of which waited for: 5 -> 6; matrix products, arithmetic and copies ran while one was open for 2% -> 19% of each run, Pallas kernels for 0% -> 22%
where the time goes in v1:
time: 198 us; the launch traced here: 196 us
  waiting for transfers between devices  72.8 us (37%)
  Pallas kernels  42.9 us (22%)
  starting transfers between devices  37 us (19%)
  matrix products  17.3 us (9%)
  other arithmetic  13.3 us (7%)
  local copies, waits for them, and re-layouts  11.7 us (6%)
    ppermute x14, waiting for transfers between devices, swap(): return lax.ppermute(value, axis, [(0, 1), (1, 0)])  66.3 us
    pallas_call x2, Pallas kernels, attention(): pl.pallas_call(attention_kernel, grid=(total // TILE,), in_specs=[pl.Bloc...  42.9 us
    ppermute x14, starting transfers between devices, swap(): return lax.ppermute(value, axis, [(0, 1), (1, 0)])  21.3 us
    dot_general x10, matrix products, dot(): return lax.dot_general(a, b, (dims, ((), ())), preferred_element_type=F32)  17.3 us
    all_to_all x1, starting transfers between devices, on_device(): term = lax.all_to_all(term, ('zh', 'zl', 'yh', 'x'), 0, 0)  7.91 us
    all_to_all x1, starting transfers between devices, on_device(): w = lax.all_to_all(w, ('zh', 'zl', 'yh', 'x'), 0, 0)  7.78 us
    all_to_all x1, waiting for transfers between devices, on_device(): term = lax.all_to_all(term, ('zh', 'zl', 'yh', 'x'), 0, 0)  6.53 us
    log x1, other arithmetic, on_device(): logd = jnp.log((1 + jnp.abs(pos[:, None] - pos[None, :])).astype(F32))  5.02 us
  transfers between devices with their start and end apart: 16, of which 6 were waited for; matrix products, arithmetic and copies ran while one was open for 19% of the time, Pallas kernels for 22%

profile of v1, /device:TPU:0, one launch (start us, length us, event | category | flops | bytes accessed | tf_op | source)
XLA Modules:
  0.0 196.1 jit_solution(17765360119021039577)
XLA Ops:
  0.6 4.0 %collective-permute-start.6 = (s32[768]{0:T(1024)}, s32[768]{0:T(1024)S(1)}, u32[]{:S(2)}, u32[]{:S(2)}) collective-permute-start(s32[768]{0:T(1024)} %param.8), channel_id=1, source_target_pairs={{0,64},{64,0},{1,65},{65,1},{2,66},{66,2},{3,67},{67,3},{4,68},{68... | collective-permute-start | bytes 9224 | tf_op jit(solution)/shard_map/bias/ppermute | solution.py:14
  4.7 0.8 reshape.57
  5.6 0.9 broadcast_in_dim.10
  6.5 7.8 %all-to-all-start = ((bf16[32,16,768]{2,1,0:T(8,128)(2,1)}), bf16[32,16,768]{2,1,0:T(8,128)(2,1)S(1)}, u32[]{:S(2)}, u32[]{:S(2)}) async-start(bf16[32,16,768]{2,1,0:T(8,128)(2,1)} %bitcast.1), calls=%async_computation | async-start | bytes 1572864 | tf_op jit(solution)/shard_map/weights/all_to_all | solution.py:157
  14.3 0.8 constant_dynamic-slice_fusion
  15.1 3.3 %collective-permute-start.5 = (bf16[768,256]{1,0:T(8,128)(2,1)}, bf16[768,256]{1,0:T(8,128)(2,1)S(1)}, u32[]{:S(2)}, u32[]{:S(2)}) collective-permute-start(bf16[768,256]{1,0:T(8,128)(2,1)} %get-tuple-element.24), channel_id=1, source_target_pairs={{0,64},{64,0},{1,65},{65,1},{2,66},{66,2},{3,67},{67,3},{4,68},{68... | collective-permute-start | bytes 1179656 | tf_op jit(solution)/shard_map/bias/ppermute | solution.py:14
  18.4 1.7 copy.16
  20.2 1.4 constant_dynamic-slice_fusion.3
  21.6 0.2 collective-permute-start.1
  21.9 3.3 %collective-permute-start.2 = (bf16[192,1024]{0,1:T(8,128)(2,1)}, bf16[192,1024]{0,1:T(8,128)(2,1)}, u32[]{:S(2)}, u32[]{:S(2)}) collective-permute-start(bf16[192,1024]{0,1:T(8,128)(2,1)} %get-tuple-element.23), channel_id=1, source_target_pairs={{0,64},{64,0},{1,65},{65,1},{2,66},{66,2},{3,67},{67,3},{4,68},{68... | collective-permute-start | bytes 1179656 | tf_op jit(solution)/shard_map/tokens/ppermute | solution.py:14
  25.3 22.1 %collective-permute-done.1 = bf16[192,1024]{0,1:T(8,128)(2,1)} collective-permute-done((bf16[192,1024]{0,1:T(8,128)(2,1)}, bf16[192,1024]{0,1:T(8,128)(2,1)}, u32[]{:S(2)}, u32[]{:S(2)}) %collective-permute-start.1) | collective-permute-done | bytes 393248 | tf_op jit(solution)/shard_map/tokens/ppermute | solution.py:14
  47.5 0.7 collective-permute-start.3
  48.1 9.5 %collective-permute-done.2 = bf16[192,1024]{0,1:T(8,128)(2,1)} collective-permute-done((bf16[192,1024]{0,1:T(8,128)(2,1)}, bf16[192,1024]{0,1:T(8,128)(2,1)}, u32[]{:S(2)}, u32[]{:S(2)}) %collective-permute-start.2) | collective-permute-done | bytes 393248 | tf_op jit(solution)/shard_map/tokens/ppermute | solution.py:14
  57.6 0.7 collective-permute-start.4
  58.3 5.0 %convert_log_fusion.logd_ref = f32[1536,1536]{1,0:T(8,128)} fusion(s32[1536]{0:T(1024)S(1)} %constant_dynamic-update-slice_fusion), kind=kLoop, calls=%fused_computation | loop fusion | flops 9437184 | bytes 9443328 | tf_op jit(solution)/shard_map/bias/log | solution.py:164
  63.3 7.5 %collective-permute-done.4 = bf16[192,1024]{0,1:T(8,128)(2,1)} collective-permute-done((bf16[192,1024]{0,1:T(8,128)(2,1)}, bf16[192,1024]{0,1:T(8,128)(2,1)}, u32[]{:S(2)}, u32[]{:S(2)}) %collective-permute-start.4) | collective-permute-done | bytes 393248 | tf_op jit(solution)/shard_map/tokens/ppermute | solution.py:14
  70.8 4.2 %maximum_select_fusion.1 = bf16[768,1024]{0,1:T(8,128)(2,1)S(1)} fusion(bf16[192,1024]{0,1:T(8,128)(2,1)} %collective-permute-done.4, bf16[192,1024]{0,1:T(8,128)(2,1)} %collective-permute-done.3, bf16[192,1024]{0,1:T(8,128)(2,1)} %collective-permute-done.2, bf16[192,1024]{0,1:T(8,128)(2,1)} %collective-permute-done.1, pred[]{:T(512)S(6)} %eq.5), kind=kLoop, calls=%fused_computation.3 | loop fusion | flops 13369344 | bytes 3145729 | tf_op jit(solution)/shard_map/tokens/jit(_where)/select_n | solution.py:150
  75.0 0.2 broadcast_select_fusion.1
  75.5 1.0 copy-done.2
  76.6 1.3 copy-done.3
  77.9 1.4 fusion.qo.ko.vo
  79.3 2.5 %collective-permute-start.8 = (bf16[1024,768]{1,0:T(8,128)(2,1)S(1)}, bf16[1024,768]{1,0:T(8,128)(2,1)}, u32[]{:S(2)}, u32[]{:S(2)}) collective-permute-start(bf16[1024,768]{1,0:T(8,128)(2,1)S(1)} %bitcast.49), channel_id=1, source_target_pairs={{0,64},{64,0},{1,65},{65,1},{2,66},{66,2},{3,67},{67,3},{4,68},{68... | collective-permute-start | bytes 4718600 | tf_op jit(solution)/shard_map/d_tokens/ppermute | solution.py:14
  81.8 1.5 convolution_convert_fusion.1.qf.kf.vf
  83.3 21.5 %attention.3 = (bf16[768,384]{1,0:T(8,128)(2,1)S(1)}, bf16[768,384]{1,0:T(8,128)(2,1)S(1)}) custom-call(f32[2]{0:T(128)S(1)} %get-tuple-element.27.slopes_ref, bf16[768,768]{1,0:T(8,128)(2,1)S(1)} %fusion.qo.ko.vo, bf16[768,768]{1,0:T(8,128)(2,1)S(1)} %convolution_convert_fusion.1.qf.kf.vf, bf16[768,768]{1,0:T(8,128)(2,1)S(1)} %fusion.qo.ko.vo, ...), custom_call_target="tpu_custom_call" | custom-call | flops 12079595520 | bytes 9437184 | tf_op jit(solution)/shard_map/attention/pallas_call | solution.py:109
  104.8 1.3 collective-permute-start.9
  106.1 21.4 %attention.2 = (bf16[768,384]{1,0:T(8,128)(2,1)S(1)}, bf16[768,384]{1,0:T(8,128)(2,1)S(1)}) custom-call(f32[2]{0:T(128)S(1)} %get-tuple-element.26.slopes_ref, bf16[768,768]{1,0:T(8,128)(2,1)S(1)} %fusion.qo.ko.vo, bf16[768,768]{1,0:T(8,128)(2,1)S(1)} %convolution_convert_fusion.1.qf.kf.vf, bf16[768,768]{1,0:T(8,128)(2,1)S(1)} %fusion.qo.ko.vo, ...), custom_call_target="tpu_custom_call" | custom-call | flops 12079595520 | bytes 9437184 | tf_op jit(solution)/shard_map/attention/pallas_call | solution.py:109
  127.6 2.6 %collective-permute-start.7 = (bf16[768,384]{1,0:T(8,128)(2,1)S(1)}, bf16[768,384]{1,0:T(8,128)(2,1)}, u32[]{:S(2)}, u32[]{:S(2)}) collective-permute-start(bf16[768,384]{1,0:T(8,128)(2,1)S(1)} %get-tuple-element.9), channel_id=1, source_target_pairs={{0,64},{64,0},{1,65},{65,1},{2,66},{66,2},{3,67},{67,3},{4,68},{68... | collective-permute-start | bytes 1769480 | tf_op jit(solution)/shard_map/d_tokens/ppermute | solution.py:14
  130.2 0.8 fusion.16
  131.0 0.8 fusion.15
  131.8 0.8 convolution_add_fusion.1
  132.8 0.8 convolution_add_fusion
  133.7 0.6 collective-permute-start.13
  134.3 2.7 %fusion.7 = f32[768,1024]{1,0:T(8,128)} fusion(bf16[768,384]{1,0:T(8,128)(2,1)S(1)} %get-tuple-element.10, bf16[1024,768]{1,0:T(8,128)(2,1)S(1)} %bitcast.51), kind=kOutput, calls=%fused_computation.21 | convolution fusion | flops 603979776 | bytes 4521984 | tf_op jit(solution)/shard_map/d_tokens/dot_general | solution.py:18
  137.0 2.6 %fusion.11 = f32[768,1024]{1,0:T(8,128)} fusion(bf16[768,384]{1,0:T(8,128)(2,1)S(1)} %get-tuple-element.8, bf16[1024,768]{1,0:T(8,128)(2,1)S(1)} %bitcast.52), kind=kOutput, calls=%fused_computation.25 | convolution fusion | flops 603979776 | bytes 4521984 | tf_op jit(solution)/shard_map/d_tokens/dot_general | solution.py:18
  140.1 1.2 copy.19
  141.3 7.9 %all-to-all-start.1 = ((bf16[32,16,768]{2,1,0:T(8,128)(2,1)}), bf16[32,16,768]{2,1,0:T(8,128)(2,1)}, u32[]{:S(2)}, u32[]{:S(2)}) async-start(bf16[32,16,768]{2,1,0:T(8,128)(2,1)} %bitcast.16), calls=%async_computation.1 | async-start | bytes 1572864 | tf_op jit(solution)/shard_map/d_weight/all_to_all | solution.py:199
  149.2 2.5 %fusion.9 = f32[768,1024]{1,0:T(8,128)S(1)} fusion(bf16[768,384]{1,0:T(8,128)(2,1)} %collective-permute-done.7, bf16[1024,768]{1,0:T(8,128)(2,1)} %collective-permute-done.8), kind=kOutput, calls=%fused_computation.23 | convolution fusion | flops 603979776 | bytes 4521984 | tf_op jit(solution)/shard_map/d_tokens/dot_general | solution.py:18
  151.7 3.3 %add_convert_fusion = bf16[768,1024]{1,0:T(8,128)(2,1)S(1)} fusion(f32[768,1024]{1,0:T(8,128)S(1)} %copy-done, f32[768,1024]{1,0:T(8,128)} %fusion.11, f32[768,1024]{1,0:T(8,128)S(1)} %fusion.9, bf16[768,384]{1,0:T(8,128)(2,1)} %collective-permute-done.9, bf16[1024,768]{1,0:T(8,128)(2,1)} %collective-permute-done.8), kind=kOutput, calls=%fused_computation.1 | convolution fusion | flops 607125504 | bytes 12386304 | tf_op jit(solution)/shard_map/d_tokens/dot_general | solution.py:18
  155.1 1.3 fusion.13
  156.3 0.7 collective-permute-start.10
  157.0 1.3 collective-permute-start.11
  158.4 6.5 %all-to-all-done.1 = bf16[32,16,768]{2,1,0:T(8,128)(2,1)} async-done(((bf16[32,16,768]{2,1,0:T(8,128)(2,1)}), bf16[32,16,768]{2,1,0:T(8,128)(2,1)}, u32[]{:S(2)}, u32[]{:S(2)}) %all-to-all-start.1) | async-done | bytes 786464 | tf_op jit(solution)/shard_map/d_weight/all_to_all | solution.py:199
  164.9 1.2 convert_reduce_fusion
  166.3 0.7 reshape.63
  167.0 10.5 %collective-permute-done.10 = bf16[384,1024]{1,0:T(8,128)(2,1)S(1)} collective-permute-done((bf16[384,1024]{1,0:T(8,128)(2,1)}, bf16[384,1024]{1,0:T(8,128)(2,1)S(1)}, u32[]{:S(2)}, u32[]{:S(2)}) %collective-permute-start.10) | collective-permute-done | bytes 786464 | tf_op jit(solution)/shard_map/d_tokens/ppermute | solution.py:14
  177.5 16.7 %collective-permute-done.11 = bf16[384,1024]{1,0:T(8,128)(2,1)S(1)} collective-permute-done((bf16[384,1024]{1,0:T(8,128)(2,1)}, bf16[384,1024]{1,0:T(8,128)(2,1)S(1)}, u32[]{:S(2)}, u32[]{:S(2)}) %collective-permute-start.11) | collective-permute-done | bytes 786464 | tf_op jit(solution)/shard_map/d_tokens/ppermute | solution.py:14
  194.2 0.7 add_convert_fusion.2
  194.9 1.3 pad_maximum_fusion
  (48 shorter events, 1.4 us)
Async XLA Ops:
  0.6 13.7 %copy-start.4 = (bf16[768,512]{1,0:T(8,128)(2,1)S(1)}, bf16[768,512]{1,0:T(8,128)(2,1)}, u32[]{:S(2)}) copy-start(bf16[768,512]{1,0:T(8,128)(2,1)} %param.7) | copy-start | bytes 2359300
  0.6 24.7 %collective-permute-start.6 = (s32[768]{0:T(1024)}, s32[768]{0:T(1024)S(1)}, u32[]{:S(2)}, u32[]{:S(2)}) collective-permute-start(s32[768]{0:T(1024)} %param.8), channel_id=1, source_target_pairs={{0,64},{64,0},{1,65},{65,1},{2,66},{66,2},{3,67},{67,3},{4,68},{68... | collective-permute-start | bytes 9224 | tf_op jit(solution)/shard_map/bias/ppermute | solution.py:14
  6.5 56.8 %all-to-all-start = ((bf16[32,16,768]{2,1,0:T(8,128)(2,1)}), bf16[32,16,768]{2,1,0:T(8,128)(2,1)S(1)}, u32[]{:S(2)}, u32[]{:S(2)}) async-start(bf16[32,16,768]{2,1,0:T(8,128)(2,1)} %bitcast.1), calls=%async_computation | async-start | bytes 1572864 | tf_op jit(solution)/shard_map/weights/all_to_all | solution.py:157
  15.1 68.1 %collective-permute-start.5 = (bf16[768,256]{1,0:T(8,128)(2,1)}, bf16[768,256]{1,0:T(8,128)(2,1)S(1)}, u32[]{:S(2)}, u32[]{:S(2)}) collective-permute-start(bf16[768,256]{1,0:T(8,128)(2,1)} %get-tuple-element.24), channel_id=1, source_target_pairs={{0,64},{64,0},{1,65},{65,1},{2,66},{66,2},{3,67},{67,3},{4,68},{68... | collective-permute-start | bytes 1179656 | tf_op jit(solution)/shard_map/bias/ppermute | solution.py:14
  20.2 5.0 %copy-start.6 = (f32[8]{0:T(128)S(1)}, f32[8]{0:T(128)}, u32[]{:S(2)}) copy-start(f32[8]{0:T(128)} %param.9) | copy-start | bytes 100
  20.2 5.1 %copy-start.5 = (s32[768]{0:T(1024)S(1)}, s32[768]{0:T(1024)}, u32[]{:S(2)}) copy-start(s32[768]{0:T(1024)} %param.8) | copy-start | bytes 9220
  21.6 25.8 %collective-permute-start.1 = (bf16[192,1024]{0,1:T(8,128)(2,1)}, bf16[192,1024]{0,1:T(8,128)(2,1)}, u32[]{:S(2)}, u32[]{:S(2)}) collective-permute-start(bf16[192,1024]{0,1:T(8,128)(2,1)} %get-tuple-element.22), channel_id=1, source_target_pairs={{0,64},{64,0},{1,65},{65,1},{2,66},{66,2},{3,67},{67,3},{4,68},{68... | collective-permute-start | bytes 1179656 | tf_op jit(solution)/shard_map/tokens/ppermute | solution.py:14
  21.9 35.8 %collective-permute-start.2 = (bf16[192,1024]{0,1:T(8,128)(2,1)}, bf16[192,1024]{0,1:T(8,128)(2,1)}, u32[]{:S(2)}, u32[]{:S(2)}) collective-permute-start(bf16[192,1024]{0,1:T(8,128)(2,1)} %get-tuple-element.23), channel_id=1, source_target_pairs={{0,64},{64,0},{1,65},{65,1},{2,66},{66,2},{3,67},{67,3},{4,68},{68... | collective-permute-start | bytes 1179656 | tf_op jit(solution)/shard_map/tokens/ppermute | solution.py:14
  47.5 15.9 %collective-permute-start.3 = (bf16[192,1024]{0,1:T(8,128)(2,1)}, bf16[192,1024]{0,1:T(8,128)(2,1)}, u32[]{:S(2)}, u32[]{:S(2)}) collective-permute-start(bf16[192,1024]{0,1:T(8,128)(2,1)} %collective-permute-done.1), channel_id=1, source_target_pairs={{0,1},{1,0},{2,3},{3,2},{4,5},{5,4},{6,7},{7,6},{8,9},{9,8},{10,11... | collective-permute-start | bytes 1179656 | tf_op jit(solution)/shard_map/tokens/ppermute | solution.py:14
  57.6 13.2 %collective-permute-start.4 = (bf16[192,1024]{0,1:T(8,128)(2,1)}, bf16[192,1024]{0,1:T(8,128)(2,1)}, u32[]{:S(2)}, u32[]{:S(2)}) collective-permute-start(bf16[192,1024]{0,1:T(8,128)(2,1)} %collective-permute-done.2), channel_id=1, source_target_pairs={{0,1},{1,0},{2,3},{3,2},{4,5},{5,4},{6,7},{7,6},{8,9},{9,8},{10,11... | collective-permute-start | bytes 1179656 | tf_op jit(solution)/shard_map/tokens/ppermute | solution.py:14
  63.3 11.6 %copy-start.1 = (bf16[32,16,768]{2,1,0:T(8,128)(2,1)}, bf16[32,16,768]{2,1,0:T(8,128)(2,1)S(1)}, u32[]{:S(2)}) copy-start(bf16[32,16,768]{2,1,0:T(8,128)(2,1)S(1)} %all-to-all-done) | copy-start | bytes 2359300
  63.3 12.1 %collective-permute-start = (bf16[32,16,768]{2,1,0:T(8,128)(2,1)S(1)}, bf16[32,16,768]{2,1,0:T(8,128)(2,1)S(1)}, u32[]{:S(2)}, u32[]{:S(2)}) collective-permute-start(bf16[32,16,768]{2,1,0:T(8,128)(2,1)S(1)} %all-to-all-done), channel_id=1, source_target_pairs={{0,2},{2,0},{1,3},{3,1},{4,6},{6,4},{5,7},{7,5},{8,10},{10,8},{9,1... | collective-permute-start | bytes 2359304 | tf_op jit(solution)/shard_map/weights/ppermute | solution.py:14
  75.3 1.1 copy-start.2
  76.5 1.4 copy-start.3
  77.9 5.4 %slice-start = ((s8[9437184]{0:T(1024)(128)(4,1)}), s8[4194304]{0:T(1024)(128)(4,1)S(1)}, s32[]{:S(2)}) async-start(s8[9437184]{0:T(1024)(128)(4,1)} %bitcast.44), calls=%async_computation.2 | async-start | bytes 8388608
  77.9 5.4 %slice-start.1 = ((s8[9437184]{0:T(1024)(128)(4,1)}), s8[4194304]{0:T(1024)(128)(4,1)S(1)}, s32[]{:S(2)}) async-start(s8[9437184]{0:T(1024)(128)(4,1)} %bitcast.44), calls=%async_computation.3 | async-start | bytes 8388608
  79.3 4.0 %slice-start.2 = ((s8[9437184]{0:T(1024)(128)(4,1)}), s8[1048576]{0:T(1024)(128)(4,1)S(1)}, s32[]{:S(2)}) async-start(s8[9437184]{0:T(1024)(128)(4,1)} %bitcast.44), calls=%async_computation.4 | async-start | bytes 2097152
  79.3 69.9 %collective-permute-start.8 = (bf16[1024,768]{1,0:T(8,128)(2,1)S(1)}, bf16[1024,768]{1,0:T(8,128)(2,1)}, u32[]{:S(2)}, u32[]{:S(2)}) collective-permute-start(bf16[1024,768]{1,0:T(8,128)(2,1)S(1)} %bitcast.49), channel_id=1, source_target_pairs={{0,64},{64,0},{1,65},{65,1},{2,66},{66,2},{3,67},{67,3},{4,68},{68... | collective-permute-start | bytes 4718600 | tf_op jit(solution)/shard_map/d_tokens/ppermute | solution.py:14
  104.8 46.9 %collective-permute-start.9 = (bf16[768,384]{1,0:T(8,128)(2,1)S(1)}, bf16[768,384]{1,0:T(8,128)(2,1)}, u32[]{:S(2)}, u32[]{:S(2)}) collective-permute-start(bf16[768,384]{1,0:T(8,128)(2,1)S(1)} %get-tuple-element.11), channel_id=1, source_target_pairs={{0,64},{64,0},{1,65},{65,1},{2,66},{66,2},{3,67},{67,3},{4,68},{68... | collective-permute-start | bytes 1769480 | tf_op jit(solution)/shard_map/d_tokens/ppermute | solution.py:14
  127.6 21.6 %collective-permute-start.7 = (bf16[768,384]{1,0:T(8,128)(2,1)S(1)}, bf16[768,384]{1,0:T(8,128)(2,1)}, u32[]{:S(2)}, u32[]{:S(2)}) collective-permute-start(bf16[768,384]{1,0:T(8,128)(2,1)S(1)} %get-tuple-element.9), channel_id=1, source_target_pairs={{0,64},{64,0},{1,65},{65,1},{2,66},{66,2},{3,67},{67,3},{4,68},{68... | collective-permute-start | bytes 1769480 | tf_op jit(solution)/shard_map/d_tokens/ppermute | solution.py:14
  132.7 6.9 %collective-permute-start.12 = (f32[512,384]{0,1:T(8,128)S(1)}, f32[512,384]{0,1:T(8,128)S(1)}, u32[]{:S(2)}, u32[]{:S(2)}) collective-permute-start(f32[512,384]{0,1:T(8,128)S(1)} %slice.75), channel_id=1, source_target_pairs={{0,2},{2,0},{1,3},{3,1},{4,6},{6,4},{5,7},{7,5},{8,10},{10,8},{9,1... | collective-permute-start | bytes 2359304 | tf_op jit(solution)/shard_map/d_weight/ppermute | solution.py:14
  133.7 6.1 %collective-permute-start.13 = (f32[512,384]{0,1:T(8,128)S(1)}, f32[512,384]{0,1:T(8,128)S(1)}, u32[]{:S(2)}, u32[]{:S(2)}) collective-permute-start(f32[512,384]{0,1:T(8,128)S(1)} %slice.77), channel_id=1, source_target_pairs={{0,2},{2,0},{1,3},{3,1},{4,6},{6,4},{5,7},{7,5},{8,10},{10,8},{9,1... | collective-permute-start | bytes 2359304 | tf_op jit(solution)/shard_map/d_weight/ppermute | solution.py:14
  141.3 23.6 %all-to-all-start.1 = ((bf16[32,16,768]{2,1,0:T(8,128)(2,1)}), bf16[32,16,768]{2,1,0:T(8,128)(2,1)}, u32[]{:S(2)}, u32[]{:S(2)}) async-start(bf16[32,16,768]{2,1,0:T(8,128)(2,1)} %bitcast.16), calls=%async_computation.1 | async-start | bytes 1572864 | tf_op jit(solution)/shard_map/d_weight/all_to_all | solution.py:199
  149.2 2.5 %copy-start = (f32[768,1024]{1,0:T(8,128)S(1)}, f32[768,1024]{1,0:T(8,128)}, u32[]{:S(2)}) copy-start(f32[768,1024]{1,0:T(8,128)} %fusion.7) | copy-start | bytes 9437188
  156.3 21.2 %collective-permute-start.10 = (bf16[384,1024]{1,0:T(8,128)(2,1)}, bf16[384,1024]{1,0:T(8,128)(2,1)S(1)}, u32[]{:S(2)}, u32[]{:S(2)}) collective-permute-start(bf16[384,1024]{1,0:T(8,128)(2,1)} %get-tuple-element.20), channel_id=1, source_target_pairs={{0,1},{1,0},{2,3},{3,2},{4,5},{5,4},{6,7},{7,6},{8,9},{9,8},{10,11... | collective-permute-start | bytes 2359304 | tf_op jit(solution)/shard_map/d_tokens/ppermute | solution.py:14
  157.0 37.2 %collective-permute-start.11 = (bf16[384,1024]{1,0:T(8,128)(2,1)}, bf16[384,1024]{1,0:T(8,128)(2,1)S(1)}, u32[]{:S(2)}, u32[]{:S(2)}) collective-permute-start(bf16[384,1024]{1,0:T(8,128)(2,1)} %get-tuple-element.21), channel_id=1, source_target_pairs={{0,1},{1,0},{2,3},{3,2},{4,5},{5,4},{6,7},{7,6},{8,9},{9,8},{10,11... | collective-permute-start | bytes 2359304 | tf_op jit(solution)/shard_map/d_tokens/ppermute | solution.py:14

commit v2 on v1

v2 whole, which is shorter than its diff:
```python
import jax
import jax.numpy as jnp
from jax import lax
from jax.experimental import pallas as pl
from jax.experimental.pallas import tpu as pltpu
from jax.sharding import PartitionSpec as P

BF = jnp.bfloat16
F32 = jnp.float32
TILE = 256


def swap(value, axis):
    return lax.ppermute(value, axis, [(0, 1), (1, 0)])


def dot(a, b, dims=((1,), (0,))):
    return lax.dot_general(a, b, (dims, ((), ())), preferred_element_type=F32)


def attention_kernel(
    place_ref, slopes_ref, qo, qf, ko, kf, vo, vf, go, gf, logd_ref, near_ref, *rest,
):
    *far_refs, q_s, k_s, v_s, g_s, kt_s, dk_s, dv_s, s_s, dp_s = rest
    step = pl.program_id(0)
    rows = qo.shape[0]
    total = 2 * rows
    chunks = total // TILE

    @pl.when(step == 0)
    def _():
        for scratch, near, far in ((q_s, qo, qf), (k_s, ko, kf), (v_s, vo, vf), (g_s, go, gf)):
            scratch[:rows] = near[...]
            scratch[rows:] = far[...]
        kt_s[...] = k_s[...].astype(F32).T.astype(BF)
        dk_s[...] = jnp.zeros_like(dk_s)
        dv_s[...] = jnp.zeros_like(dv_s)

    here = pl.ds(pl.multiple_of(step * TILE, TILE), TILE)
    q = (q_s[here].astype(F32) * 0.125)
    g = g_s[here].astype(F32)
    q_t, g_t = q.T, g.T
    upper = lax.broadcasted_iota(jnp.int32, (128, TILE), 0) < 64
    left = lax.broadcasted_iota(jnp.int32, (TILE, 128), 1) < 64
    zero = jnp.float32(0)
    qts = [jnp.where(upper, q_t, zero).astype(BF), jnp.where(upper, zero, q_t).astype(BF)]
    gts = [jnp.where(upper, g_t, zero).astype(BF), jnp.where(upper, zero, g_t).astype(BF)]
    qs = [jnp.where(left, q, zero).astype(BF), jnp.where(left, zero, q).astype(BF)]
    gs = [jnp.where(left, g, zero).astype(BF), jnp.where(left, zero, g).astype(BF)]
    for h in range(2):
        slope = slopes_ref[h]
        top = None
        for c in range(chunks):
            part = slice(c * TILE, (c + 1) * TILE)
            score = dot(k_s[part], qts[h]) - slope * logd_ref[part]
            s_s[h, part] = score
            peak = jnp.max(score, axis=0, keepdims=True)
            top = peak if top is None else jnp.maximum(top, peak)
        norm = jnp.zeros((1, TILE), F32)
        delta = jnp.zeros((1, TILE), F32)
        for c in range(chunks):
            part = slice(c * TILE, (c + 1) * TILE)
            e = jnp.exp(s_s[h, part] - top)
            s_s[h, part] = e
            dp = dot(v_s[part], gts[h])
            dp_s[h, part] = dp
            norm += jnp.sum(e, axis=0, keepdims=True)
            delta += jnp.sum(e * dp, axis=0, keepdims=True)
        inverse = 1.0 / norm
        delta = delta * inverse
        dq_t = jnp.zeros((64, TILE), F32)
        for c in range(chunks):
            part = slice(c * TILE, (c + 1) * TILE)
            p = s_s[h, part] * inverse
            ds = (p * (dp_s[h, part] - delta)).astype(BF)
            dv_s[part] += dot(p.astype(BF), gs[h])
            dk_s[part] += dot(ds, qs[h])
            dq_t += dot(kt_s[h * 64 : (h + 1) * 64, part], ds)
        s_s[h, :64] = dq_t
    dq = jnp.concatenate([s_s[0, :64], s_s[1, :64]], 0).T * 0.125
    @pl.when(step < chunks // 2)
    def _():
        near_ref[here, :128] = dq.astype(BF)

    @pl.when(step >= chunks // 2)
    def _():
        q_s[here] = dq.astype(BF)

    @pl.when(step == chunks - 1)
    def _():
        near_ref[:, 128:256] = dk_s[:rows].astype(BF)
        near_ref[:, 256:384] = dv_s[:rows].astype(BF)
        third = rows // 3
        first = 0
        for far_ref in far_refs:
            for k in range(far_ref.shape[0] // third):
                at = (first + k) ^ place_ref[0] if first + k < 2 else first + k
                part = pl.ds(pl.multiple_of(rows + at * third, 64), third)
                mine = slice(k * third, (k + 1) * third)
                far_ref[mine, :128] = q_s[part]
                far_ref[mine, 128:256] = dk_s[part].astype(BF)
                far_ref[mine, 256:384] = dv_s[part].astype(BF)
            first += far_ref.shape[0] // third


def attention(place, slopes, near, far, g_near, g_far, logd, pair, pieces):
    rows = near.shape[0]
    total = 2 * rows
    sizes = [rows] + pieces

    def column(block):
        return pl.BlockSpec((rows, 128), lambda t: (0, block))

    specs = []
    for c in range(3):
        specs += [column(3 * pair + c)] * 2
    return pl.pallas_call(
        attention_kernel,
        grid=(total // TILE,),
        in_specs=[pl.BlockSpec(memory_space=pltpu.SMEM)] * 2
        + specs
        + [column(pair)] * 2
        + [pl.BlockSpec((total, TILE), lambda t: (0, t))],
        out_specs=[pl.BlockSpec((n, 384), lambda t: (0, 0)) for n in sizes],
        out_shape=[jax.ShapeDtypeStruct((n, 384), BF) for n in sizes],
        scratch_shapes=[pltpu.VMEM((total, 128), BF)] * 4
        + [pltpu.VMEM((128, total), BF)]
        + [pltpu.VMEM((total, 128), F32)] * 2
        + [pltpu.VMEM((2, total, TILE), F32)] * 2,
        compiler_params=pltpu.CompilerParams(vmem_limit_bytes=32 * 2**20),
        cost_estimate=pl.CostEstimate(
            flops=2 * 5 * 2 * total * total * 256, bytes_accessed=4 * total * total, transcendentals=2 * total * total
        ),
    )(place[None], slopes, near, far, near, far, near, far, g_near, g_far, logd)


def add_kernel(mine_ref, theirs_ref, *refs):
    refs[-1][...] = (mine_ref[...].astype(F32) + theirs_ref[...].astype(F32)).astype(BF)


def add_rows(out, mine, theirs, index, count):
    rows, width = mine.shape
    return pl.pallas_call(
        add_kernel,
        grid=(1,),
        in_specs=[pl.BlockSpec((rows, width), lambda i: (0, 0))] * 2
        + ([] if out is None else [pl.BlockSpec(memory_space=pl.ANY)]),
        out_specs=pl.BlockSpec((rows, width), lambda i: (index, 0)),
        out_shape=jax.ShapeDtypeStruct((rows * count, width), BF),
        input_output_aliases={} if out is None else {2: 0},
        cost_estimate=pl.CostEstimate(flops=1000, bytes_accessed=1000, transcendentals=0),
    )(mine, theirs, *([] if out is None else [out]))


def weight_kernel(place_ref, near_ref, far_ref, *refs):
    *grads, keep_ref, send_ref, term_s = refs
    core, x, head = place_ref[0], place_ref[1], place_ref[2]
    step = pl.program_id(0)
    third = far_ref.shape[0] // 3
    for p in range(len(grads) // 2):
        near = lax.dot_general(near_ref[...], grads[2 * p][...], (((0,), (0,)), ((), ())), preferred_element_type=F32)
        for k in range(3):
            at = k ^ head if k < 2 else k
            part = pl.ds(pl.multiple_of(at * third, 64), third)
            near += lax.dot_general(
                far_ref[k * third : (k + 1) * third],
                grads[2 * p + 1][part],
                (((0,), (0,)), ((), ())),
                preferred_element_type=F32,
            )
        term_s[:, p * 384 : (p + 1) * 384] = near
    groups = term_s.shape[0] // 128
    for i in range(groups):
        for j in range(4):
            to = pl.ds(pl.multiple_of((j * 8 + step * groups + i) * 16, 16), 16)
            at = 128 * i + 32 * (j ^ x)
            keep_ref[to] = term_s[pl.ds(pl.multiple_of(at + 16 * core, 16), 16)]
            send_ref[to] = term_s[pl.ds(pl.multiple_of(at + 16 * (1 - core), 16), 16)]


def weight_terms(place, near, far, grads):
    rows, width = near.shape
    columns = 192 * len(grads)
    tile = 256
    whole = pl.BlockSpec((rows, 384), lambda i: (0, 0))
    return pl.pallas_call(
        weight_kernel,
        grid=(width // tile,),
        in_specs=[pl.BlockSpec(memory_space=pltpu.SMEM)]
        + [pl.BlockSpec((rows, tile), lambda i: (0, i))] * 2
        + [whole] * len(grads),
        out_specs=[pl.BlockSpec((width // 2, columns), lambda i: (0, 0))] * 2,
        out_shape=[jax.ShapeDtypeStruct((width // 2, columns), F32)] * 2,
        scratch_shapes=[pltpu.VMEM((tile, columns), F32)],
        compiler_params=pltpu.CompilerParams(vmem_limit_bytes=32 * 2**20),
        cost_estimate=pl.CostEstimate(flops=1000, bytes_accessed=1000, transcendentals=0),
    )(place, near, far, *grads)


def pick(array, place, dim):
    first = lax.index_in_dim(array, 0, dim, keepdims=False)
    second = lax.index_in_dim(array, 1, dim, keepdims=False)
    return jnp.where(place == 0, first, second), jnp.where(place == 0, second, first)


def ordered(own, other, place):
    return jnp.where(place == 0, jnp.concatenate([own, other], 0), jnp.concatenate([other, own], 0))


def on_device(tokens, qkv_weight, grad_attn, positions, slopes):
    z_hi, z_lo, y_hi = lax.axis_index("zh"), lax.axis_index("zl"), lax.axis_index("yh")
    x, core, head = lax.axis_index("x"), lax.axis_index("c"), lax.axis_index("h")
    rows = tokens.shape[0]
    third = rows // 3

    def local(array):
        first, second = array[:third], array[third : 2 * third]
        return jnp.where(head == 0, array, jnp.concatenate([second, first, array[2 * third :]], 0))

    with jax.named_scope("tokens"):
        got = [swap(lax.dynamic_slice_in_dim(tokens, head * third, third, 0), "zh"), swap(tokens[2 * third :], "zh")]

    with jax.named_scope("weights"):
        w = qkv_weight.reshape(16, 3, 2, 2, 128).transpose(2, 0, 3, 1, 4).reshape(2, 16, 768)
        mine = lax.dynamic_index_in_dim(w, z_hi, 0, keepdims=False)
        theirs = lax.dynamic_index_in_dim(w, 1 - z_hi, 0, keepdims=False)
        digits = jnp.stack([(positions >> shift) & 255 for shift in (16, 8, 0)]).astype(BF)
        other = lax.ppermute(jnp.concatenate([theirs, digits], 0), ("zh", "zl"), [(i, i ^ 2) for i in range(4)])
        pieces = [
            mine,
            lax.ppermute(mine, ("zh", "zl"), [(i, i ^ 1) for i in range(4)]),
            other[:16],
            lax.ppermute(theirs, ("zh", "zl"), [(i, i ^ 3) for i in range(4)]),
        ]
        digits = other[16:].astype(jnp.int32)
        far_positions = local((digits[0] << 16) + (digits[1] << 8) + digits[2])
        pos = jnp.concatenate([positions, far_positions], 0)
        logd = jnp.log((1 + jnp.abs(pos[:, None] - pos[None, :])).astype(F32))
        pieces = [jnp.where(z_lo == 0, pieces[i], pieces[i ^ 1]) for i in range(4)]
        pieces = [jnp.where(z_hi == 0, pieces[i], pieces[i ^ 2]) for i in range(4)]
        w, grad_attn = lax.optimization_barrier((jnp.stack(pieces)[:, None], grad_attn))
        other = swap(w, "yh")
        w = jnp.where(y_hi == 0, jnp.concatenate([w, other], 1), jnp.concatenate([other, w], 1)).reshape(8, 16, 768)
        w, got[0], logd = lax.optimization_barrier((w, got[0], logd))
        relayed = swap(got[0], "h")
        pieces = [w] + [lax.ppermute(w, "x", [(i, i ^ j) for i in range(4)]) for j in range(1, 4)]
        pieces = [jnp.where((x & 1) == 0, pieces[i], pieces[i ^ 1]) for i in range(4)]
        pieces = [jnp.where((x & 2) == 0, pieces[i], pieces[i ^ 2]) for i in range(4)]
        w = jnp.stack(pieces, 1)
        other = swap(w, "c")
        w = jnp.where(core == 0, jnp.stack([w, other], 2), jnp.stack([other, w], 2)).reshape(1024, 768)
        far_tokens = jnp.concatenate([got[0], relayed, got[1]], 0)

    with jax.named_scope("bias"):
        g_near = lax.dynamic_slice_in_dim(grad_attn, z_hi * 256, 256, 1)
        g_far = swap(local(lax.dynamic_slice_in_dim(grad_attn, (1 - z_hi) * 256, 256, 1)), "zh")
        slopes = lax.dynamic_slice_in_dim(slopes, z_hi * 4, 4, 0)

    with jax.named_scope("projection"):
        near = dot(tokens, w).astype(BF)
        far = dot(far_tokens, w).astype(BF)
    with jax.named_scope("attention"):
        near0, far0 = attention(head, slopes[:2], near, far, g_near, g_far, logd, 0, [rows])
        g_near, near0 = lax.optimization_barrier((g_near, near0))
        near1, *far1 = attention(head, slopes[2:], near, far, g_near, g_far, logd, 1, [third, 2 * third])

    with jax.named_scope("d_tokens"):
        w_other = swap(w, "zh")
        back0 = swap(far0, "zh")
        back1 = [swap(part, "zh") for part in far1]
        base = dot(
            jnp.concatenate([near0, near1, back0], 1), jnp.concatenate([w, w_other[:, :384]], 1), ((1,), (1,))
        )
        mine = []
        for i in range(3):
            back = back1[0] if i == 0 else back1[1][(i - 1) * third : i * third]
            part = base[i * third : (i + 1) * third] + dot(back, w_other[:, 384:], ((1,), (1,)))
            mine.append(part.astype(BF))

    with jax.named_scope("d_weight"):
        far1 = jnp.concatenate(far1, 0)
        far1, back0 = lax.optimization_barrier((far1, back0))
        keep, send = weight_terms(jnp.stack([core, x, head]), tokens, far_tokens, [near0, far0, near1, far1])
        other = swap(send, "c")
        theirs = [swap(mine[0], "h")]
        other, theirs[0] = lax.optimization_barrier((other, theirs[0]))
        term = (keep + other).reshape(4, 8, 16, 768)
        total = term[0]
        for j in range(1, 4):
            piece = lax.ppermute(term[j].astype(BF), "x", [(i, i ^ j) for i in range(4)])
            total = total + piece.astype(F32)
        total = total.reshape(2, 2, 2, 16, 768)
        theirs.append(swap(mine[1], "h"))
        total, theirs[1], mine[2] = lax.optimization_barrier((total, theirs[1], mine[2]))
        theirs.append(swap(mine[2], "h"))
        mine_w, their_w = pick(total, y_hi, 2)
        total = mine_w + swap(their_w.astype(BF), "yh").astype(F32)
        halves = []
        for a in range(2):
            part = total if a == 0 else total[::-1]
            part = jnp.where(z_hi == 0, part[0], part[1])
            mine_w, their_w = pick(part, z_lo, 0)
            if a:
                mine_w = lax.ppermute(mine_w, ("zh", "zl"), [(i, i ^ 2) for i in range(4)])
            halves.append(mine_w + lax.ppermute(their_w, ("zh", "zl"), [(i, i ^ (2 * a + 1)) for i in range(4)]))
        total = jnp.where(z_hi == 0, jnp.stack(halves), jnp.stack(halves[::-1]))
        d_weight = total.reshape(2, 16, 2, 3, 128).transpose(1, 3, 0, 2, 4).reshape(16, 3, 512)

    with jax.named_scope("d_tokens"):
        d_tokens = None
        for i in range(3):
            d_tokens = add_rows(d_tokens, mine[i], theirs[i], i, 3)
    return d_tokens, d_weight


def solution(mesh):
    mesh = jax.sharding.Mesh(mesh.devices.reshape(2, 2, 2, 4, 2, 2), ("zh", "zl", "yh", "x", "c", "h"))
    ctx = ("zh", "zl", "yh", "x", "c")
    return jax.shard_map(
        on_device,
        mesh=mesh,
        in_specs=(P(ctx, None), P(ctx, None, "h"), P(ctx, "h"), P(ctx), P("h")),
        out_specs=(P(ctx, None), P(ctx, None, "h")),
        check_vma=False,
    )
```

time: 198 us -> 159 us (0.80)
  waiting for transfers between devices: 72.8 us -> 34.4 us
  Pallas kernels: 42.9 us -> 54.6 us
  matrix products: 17.3 us -> 6.4 us
  starting transfers between devices: 37 us -> 44.8 us
  other arithmetic: 13.3 us -> 6.87 us
    ppermute x14 -> x15, waiting for transfers between devices: 66.3 us -> 21.6 us  [swap(): return lax.ppermute(value, axis, [(0, 1), (1, 0)])]
    ppermute x0 -> x12, starting transfers between devices: none -> 19 us  [the longest x3 4.78 us: on_device(): lax.ppermute(term[j].astype(BF), 'x', [(i, i ^ j) for i in range(4)])]
    all_to_all x2 -> x0, starting transfers between devices: 15.7 us -> none  [the longest x1 7.91 us: on_device(): term = lax.all_to_all(term, ('zh', 'zl', 'yh', 'x'), 0, 0)]
    ppermute x0 -> x12, waiting for transfers between devices: none -> 12.8 us  [the longest x3 5.23 us: on_device(): lax.ppermute(term[j].astype(BF), 'x', [(i, i ^ j) for i in range(4)])]
    pallas_call x0 -> x4, Pallas kernels: none -> 11.7 us  [the longest x3 6.34 us: add_rows(): pl.pallas_call(add_kernel, grid=(1,), in_specs=[pl.BlockSpec((rows, width...]
    dot_general x10 -> x6, matrix products: 17.3 us -> 6.4 us  [dot(): return lax.dot_general(a, b, (dims, ((), ())), preferred_element_type=F32)]
    all_to_all x2 -> x0, waiting for transfers between devices: 6.53 us -> none  [the longest x1 6.53 us: on_device(): term = lax.all_to_all(term, ('zh', 'zl', 'yh', 'x'), 0, 0)]
    ppermute x14 -> x15, starting transfers between devices: 21.3 us -> 25.8 us  [swap(): return lax.ppermute(value, axis, [(0, 1), (1, 0)])]
  transfers between devices with their start and end apart: 16 -> 27, of which waited for: 6 -> 14; matrix products, arithmetic and copies ran while one was open for 19% -> 12% of each run, Pallas kernels for 22% -> 33%
where the time goes in v2:
time: 159 us
  Pallas kernels  54.6 us (34%)
  starting transfers between devices  44.8 us (28%)
  waiting for transfers between devices  34.4 us (22%)
  local copies, waits for them, and re-layouts  10.8 us (7%)
  other arithmetic  6.87 us (4%)
  matrix products  6.4 us (4%)
    pallas_call x2, Pallas kernels, attention(): pl.pallas_call(attention_kernel, grid=(total // TILE,), in_specs=[pl.Bloc...  42.9 us
    ppermute x15, starting transfers between devices, swap(): return lax.ppermute(value, axis, [(0, 1), (1, 0)])  25.8 us
    ppermute x15, waiting for transfers between devices, swap(): return lax.ppermute(value, axis, [(0, 1), (1, 0)])  21.6 us
    dot_general x6, matrix products, dot(): return lax.dot_general(a, b, (dims, ((), ())), preferred_element_type=F32)  6.4 us
    pallas_call x3, Pallas kernels, add_rows(): pl.pallas_call(add_kernel, grid=(1,), in_specs=[pl.BlockSpec((rows, width...  6.34 us
    unnamed x28, local copies, waits for them, and re-layouts  5.58 us
    pallas_call x1, Pallas kernels, weight_terms(): pl.pallas_call(weight_kernel, grid=(width // tile,), in_specs=[pl.BlockSp...  5.34 us
    ppermute x3, waiting for transfers between devices, on_device(): lax.ppermute(term[j].astype(BF), 'x', [(i, i ^ j) for i in range(4)])  5.23 us
  transfers between devices with their start and end apart: 27, of which 14 were waited for; matrix products, arithmetic and copies ran while one was open for 12% of the time, Pallas kernels for 33%

profile of v2, /device:TPU:0, one launch (start us, length us, event | category | flops | bytes accessed | tf_op | source)
XLA Modules:
  0.0 159.0 jit_solution(3985223770168138268)
XLA Ops:
  0.6 0.8 reshape.91
  1.6 4.2 %collective-permute-start.2 = (bf16[16,768]{1,0:T(8,128)(2,1)S(1)}, bf16[16,768]{1,0:T(8,128)(2,1)S(1)}, u32[]{:S(2)}, u32[]{:S(2)}) collective-permute-start(bf16[16,768]{1,0:T(8,128)(2,1)S(1)} %get-tuple-element.70), channel_id=1, source_target_pairs={{0,96},{32,64},{64,32},{96,0},{1,97},{33,65},{65,33},{97,1},{2,98}... | collective-permute-start | bytes 73736 | tf_op jit(solution)/shard_map/weights/ppermute | solution.py:233
  6.5 1.6 %collective-permute-start.1 = (bf16[19,768]{1,0:T(8,128)(2,1)S(1)}, bf16[19,768]{1,0:T(8,128)(2,1)S(1)}, u32[]{:S(2)}, u32[]{:S(2)}) collective-permute-start(bf16[19,768]{1,0:T(8,128)(2,1)S(1)} %pad_maximum_fusion.3), channel_id=1, source_target_pairs={{0,64},{32,96},{64,0},{96,32},{1,65},{33,97},{65,1},{97,33},{2,66}... | collective-permute-start | bytes 87560 | tf_op jit(solution)/shard_map/weights/ppermute | solution.py:228
  8.2 2.1 %fusion.35 = (bf16[256,1024]{1,0:T(8,128)(2,1)}, bf16[256,1024]{1,0:T(8,128)(2,1)S(1)}) fusion(bf16[768,1024]{1,0:T(8,128)(2,1)} %near_ref.1, s32[]{:T(128)S(6)} %select_n.223), kind=kLoop, calls=%fused_computation.89 | loop fusion | bytes 2097156 | tf_op jit(solution)/shard_map/tokens/slice | solution.py:221
  10.2 2.0 %collective-permute-start.4 = (bf16[256,1024]{1,0:T(8,128)(2,1)S(1)}, bf16[256,1024]{1,0:T(8,128)(2,1)}, u32[]{:S(2)}, u32[]{:S(2)}) collective-permute-start(bf16[256,1024]{1,0:T(8,128)(2,1)S(1)} %get-tuple-element.47), channel_id=1, source_target_pairs={{0,64},{64,0},{1,65},{65,1},{2,66},{66,2},{3,67},{67,3},{4,68},{68... | collective-permute-start | bytes 1572872 | tf_op jit(solution)/shard_map/tokens/ppermute | solution.py:14
  12.4 3.3 %collective-permute-start.3 = (bf16[4,1,16,768]{3,2,0,1:T(8,128)(2,1)S(1)}, bf16[4,1,16,768]{3,2,0,1:T(8,128)(2,1)S(1)}, u32[]{:S(2)}, u32[]{:S(2)}) collective-permute-start(bf16[4,1,16,768]{3,2,0,1:T(8,128)(2,1)S(1)} %bitcast.98), channel_id=1, source_target_pairs={{0,16},{16,0},{1,17},{17,1},{2,18},{18,2},{3,19},{19,3},{4,20},{20... | collective-permute-start | bytes 294920 | tf_op jit(solution)/shard_map/weights/ppermute | solution.py:14
  15.7 5.0 %convert_log_fusion.logd_ref = f32[1536,1536]{1,0:T(8,128)} fusion(s32[1536]{0:T(1024)S(1)} %pad_add_fusion), kind=kLoop, calls=%fused_computation | loop fusion | flops 9437184 | bytes 9443328 | tf_op jit(solution)/shard_map/weights/log | solution.py:238
  20.7 4.2 %collective-permute-done.4 = bf16[256,1024]{1,0:T(8,128)(2,1)} collective-permute-done((bf16[256,1024]{1,0:T(8,128)(2,1)S(1)}, bf16[256,1024]{1,0:T(8,128)(2,1)}, u32[]{:S(2)}, u32[]{:S(2)}) %collective-permute-start.4) | collective-permute-done | bytes 524320 | tf_op jit(solution)/shard_map/tokens/ppermute | solution.py:14
  25.0 2.8 %collective-permute-start.9 = (bf16[8,16,768]{2,1,0:T(8,128)(2,1)S(1)}, bf16[8,16,768]{2,1,0:T(8,128)(2,1)S(1)}, u32[]{:S(2)}, u32[]{:S(2)}) collective-permute-start(bf16[8,16,768]{2,1,0:T(8,128)(2,1)S(1)} %bitcast.100), channel_id=1, source_target_pairs={{0,12},{4,8},{8,4},{12,0},{1,13},{5,9},{9,5},{13,1},{2,14},{6,10},... | collective-permute-start | bytes 589832 | tf_op jit(solution)/shard_map/weights/ppermute | solution.py:246
  29.0 2.0 %collective-permute-start.6 = (bf16[256,1024]{1,0:T(8,128)(2,1)}, bf16[256,1024]{1,0:T(8,128)(2,1)}, u32[]{:S(2)}, u32[]{:S(2)}) collective-permute-start(bf16[256,1024]{1,0:T(8,128)(2,1)} %get-tuple-element.46), channel_id=1, source_target_pairs={{0,64},{64,0},{1,65},{65,1},{2,66},{66,2},{3,67},{67,3},{4,68},{68... | collective-permute-start | bytes 1572872 | tf_op jit(solution)/shard_map/tokens/ppermute | solution.py:14
  31.1 1.6 %collective-permute-start.5 = (bf16[256,1024]{1,0:T(8,128)(2,1)}, bf16[256,1024]{1,0:T(8,128)(2,1)}, u32[]{:S(2)}, u32[]{:S(2)}) collective-permute-start(bf16[256,1024]{1,0:T(8,128)(2,1)} %collective-permute-done.4), channel_id=1, source_target_pairs={{0,1},{1,0},{2,3},{3,2},{4,5},{5,4},{6,7},{7,6},{8,9},{9,8},{10,11... | collective-permute-start | bytes 1572872 | tf_op jit(solution)/shard_map/weights/ppermute | solution.py:14
  32.7 2.3 %collective-permute-done.9 = bf16[8,16,768]{2,1,0:T(8,128)(2,1)S(1)} collective-permute-done((bf16[8,16,768]{2,1,0:T(8,128)(2,1)S(1)}, bf16[8,16,768]{2,1,0:T(8,128)(2,1)S(1)}, u32[]{:S(2)}, u32[]{:S(2)}) %collective-permute-start.9) | collective-permute-done | bytes 196640 | tf_op jit(solution)/shard_map/weights/ppermute | solution.py:246
  35.0 1.2 collective-permute-done.8
  37.6 2.0 %collective-permute-start.11 = (bf16[768,256]{1,0:T(8,128)(2,1)S(1)}, bf16[768,256]{1,0:T(8,128)(2,1)S(1)}, u32[]{:S(2)}, u32[]{:S(2)}) collective-permute-start(bf16[768,256]{1,0:T(8,128)(2,1)S(1)} %get-tuple-element.51), channel_id=1, source_target_pairs={{0,64},{64,0},{1,65},{65,1},{2,66},{66,2},{3,67},{67,3},{4,68},{68... | collective-permute-start | bytes 1179656 | tf_op jit(solution)/shard_map/bias/ppermute | solution.py:14
  39.7 1.1 constant_dynamic-update-slice_fusion.2
  40.8 1.7 %collective-permute-done.5 = bf16[256,1024]{1,0:T(8,128)(2,1)} collective-permute-done((bf16[256,1024]{1,0:T(8,128)(2,1)}, bf16[256,1024]{1,0:T(8,128)(2,1)}, u32[]{:S(2)}, u32[]{:S(2)}) %collective-permute-start.5) | collective-permute-done | bytes 524320 | tf_op jit(solution)/shard_map/weights/ppermute | solution.py:14
  42.5 1.1 constant_dynamic-update-slice_fusion.1
  43.6 1.1 constant_dynamic-update-slice_fusion.far_ref
  44.8 1.2 copy-done
  46.1 1.4 fusion.9.qo.ko.vo
  47.5 1.8 %collective-permute-start.14 = (bf16[1024,768]{1,0:T(8,128)(2,1)S(1)}, bf16[1024,768]{1,0:T(8,128)(2,1)S(1)}, u32[]{:S(2)}, u32[]{:S(2)}) collective-permute-start(bf16[1024,768]{1,0:T(8,128)(2,1)S(1)} %bitcast.95), channel_id=1, source_target_pairs={{0,64},{64,0},{1,65},{65,1},{2,66},{66,2},{3,67},{67,3},{4,68},{68... | collective-permute-start | bytes 4718600 | tf_op jit(solution)/shard_map/d_tokens/ppermute | solution.py:14
  49.3 1.4 convolution_convert_fusion.1.qf.kf.vf
  51.2 21.5 %attention.2 = (bf16[768,384]{1,0:T(8,128)(2,1)S(1)}, bf16[768,384]{1,0:T(8,128)(2,1)S(1)}) custom-call(s32[1]{0:T(128)} %bitcast.2.place_ref, f32[2]{0:T(128)S(1)} %get-tuple-element.79.slopes_ref, bf16[768,768]{1,0:T(8,128)(2,1)S(1)} %fusion.9.qo.ko.vo, bf16[768,768]{1,0:T(8,128)(2,1)S(1)} %convolution_convert_fusion.1.qf.kf.vf, ...), custom_call_target="tpu_custom_call" | custom-call | flops 12079595520 | bytes 9437184 | tf_op jit(solution)/shard_map/attention/pallas_call | solution.py:117
  72.7 2.1 %collective-permute-start.12 = (bf16[768,384]{1,0:T(8,128)(2,1)S(1)}, bf16[768,384]{1,0:T(8,128)(2,1)S(1)}, u32[]{:S(2)}, u32[]{:S(2)}) collective-permute-start(bf16[768,384]{1,0:T(8,128)(2,1)S(1)} %get-tuple-element.29.refs_1_), channel_id=1, source_target_pairs={{0,64},{64,0},{1,65},{65,1},{2,66},{66,2},{3,67},{67,3},{4,68},{68... | collective-permute-start | bytes 1769480 | tf_op jit(solution)/shard_map/d_tokens/ppermute | solution.py:14
  74.8 21.4 %attention.3 = (bf16[768,384]{1,0:T(8,128)(2,1)S(1)}, bf16[256,384]{1,0:T(8,128)(2,1)S(1)}, bf16[512,384]{1,0:T(8,128)(2,1)S(1)}) custom-call(s32[1]{0:T(128)} %bitcast.2.place_ref, f32[2]{0:T(128)S(1)} %get-tuple-element.78.slopes_ref, bf16[768,768]{1,0:T(8,128)(2,1)S(1)} %fusion.9.qo.ko.vo, bf16[768,768]{1,0:T(8,128)(2,1)S(1)} %convolution_convert_fusion.1.qf.kf.vf, ...), custom_call_target="tpu_custom_call" | custom-call | flops 12079595520 | bytes 9437184 | tf_op jit(solution)/shard_map/attention/pallas_call | solution.py:117
  96.9 5.3 %d_weight.1 = (f32[512,768]{1,0:T(8,128)S(1)}, f32[512,768]{1,0:T(8,128)S(1)}) custom-call(s32[3]{0:T(128)S(1)} %pad_add_fusion.1.place_ref, bf16[768,1024]{1,0:T(8,128)(2,1)S(1)} %copy-done, bf16[768,1024]{1,0:T(8,128)(2,1)S(1)} %constant_dynamic-update-slice_fusion.far_ref, bf16[768,384]{1,0:T(8,128)(2,1)S(1)} %get-tuple-element.28.refs_0_, ...), custom_call_target="tpu_custom_call" | custom-call | flops 1000 | bytes 1000 | tf_op jit(solution)/shard_map/d_weight/pallas_call | solution.py:186
  102.3 2.1 %collective-permute-start.15 = (bf16[256,384]{1,0:T(8,128)(2,1)S(1)}, bf16[256,384]{1,0:T(8,128)(2,1)S(1)}, u32[]{:S(2)}, u32[]{:S(2)}) collective-permute-start(bf16[256,384]{1,0:T(8,128)(2,1)S(1)} %get-tuple-element.32), channel_id=1, source_target_pairs={{0,64},{64,0},{1,65},{65,1},{2,66},{66,2},{3,67},{67,3},{4,68},{68... | collective-permute-start | bytes 589832 | tf_op jit(solution)/shard_map/d_tokens/ppermute | solution.py:14
  104.4 1.6 collective-permute-start.20
  106.0 2.2 %fusion = f32[768,1024]{1,0:T(8,128)S(1)} fusion(bf16[1024,384]{1,0:T(8,128)(2,1)S(1)} %slice.169, bf16[1024,768]{1,0:T(8,128)(2,1)S(1)} %bitcast.97, bf16[768,384]{1,0:T(8,128)(2,1)S(1)} %collective-permute-done.12, bf16[768,384]{1,0:T(8,128)(2,1)S(1)} %get-tuple-element.31.refs_2_, bf16[768,384]{1,0:T(8,128)(2,1)S(1)} %get-tuple-element.28.refs_0_), kind=kOutput, calls=%fused_computation.1 | convolution fusion | flops 1821966336 | bytes 7274496 | tf_op jit(solution)/shard_map/d_tokens/dot_general | solution.py:18
  108.2 3.4 %collective-permute-done.15 = bf16[256,384]{1,0:T(8,128)(2,1)S(1)} collective-permute-done((bf16[256,384]{1,0:T(8,128)(2,1)S(1)}, bf16[256,384]{1,0:T(8,128)(2,1)S(1)}, u32[]{:S(2)}, u32[]{:S(2)}) %collective-permute-start.15) | collective-permute-done | bytes 196640 | tf_op jit(solution)/shard_map/d_tokens/ppermute | solution.py:14
  112.1 1.7 %collective-permute-start.16 = (bf16[256,1024]{1,0:T(8,128)(2,1)S(1)}, bf16[256,1024]{1,0:T(8,128)(2,1)S(1)}, u32[]{:S(2)}, u32[]{:S(2)}) collective-permute-start(bf16[256,1024]{1,0:T(8,128)(2,1)S(1)} %fusion.12.mine_ref), channel_id=1, source_target_pairs={{0,1},{1,0},{2,3},{3,2},{4,5},{5,4},{6,7},{7,6},{8,9},{9,8},{10,11... | collective-permute-start | bytes 1572872 | tf_op jit(solution)/shard_map/d_weight/ppermute | solution.py:14
  113.7 5.8 %collective-permute-done.20 = bf16[512,384]{1,0:T(8,128)(2,1)S(1)} collective-permute-done((bf16[512,384]{1,0:T(8,128)(2,1)S(1)}, bf16[512,384]{1,0:T(8,128)(2,1)S(1)}, u32[]{:S(2)}, u32[]{:S(2)}) %collective-permute-start.20) | collective-permute-done | bytes 393248 | tf_op jit(solution)/shard_map/d_tokens/ppermute | solution.py:14
  120.0 1.7 %collective-permute-start.21 = (bf16[256,1024]{1,0:T(8,128)(2,1)S(1)}, bf16[256,1024]{1,0:T(8,128)(2,1)S(1)}, u32[]{:S(2)}, u32[]{:S(2)}) collective-permute-start(bf16[256,1024]{1,0:T(8,128)(2,1)S(1)} %fusion.11.mine_ref), channel_id=1, source_target_pairs={{0,1},{1,0},{2,3},{3,2},{4,5},{5,4},{6,7},{7,6},{8,9},{9,8},{10,11... | collective-permute-start | bytes 1572872 | tf_op jit(solution)/shard_map/d_weight/ppermute | solution.py:14
  121.7 5.3 %collective-permute-done.16.theirs_ref = bf16[256,1024]{1,0:T(8,128)(2,1)S(1)} collective-permute-done((bf16[256,1024]{1,0:T(8,128)(2,1)S(1)}, bf16[256,1024]{1,0:T(8,128)(2,1)S(1)}, u32[]{:S(2)}, u32[]{:S(2)}) %collective-permute-start.16) | collective-permute-done | bytes 524320 | tf_op jit(solution)/shard_map/d_weight/ppermute | solution.py:14
  127.9 2.8 %collective-permute-start.19 = (bf16[8,16,768]{2,1,0:T(8,128)(2,1)S(1)}, bf16[8,16,768]{2,1,0:T(8,128)(2,1)S(1)}, u32[]{:S(2)}, u32[]{:S(2)}) collective-permute-start(bf16[8,16,768]{2,1,0:T(8,128)(2,1)S(1)} %bitcast.109), channel_id=1, source_target_pairs={{0,12},{4,8},{8,4},{12,0},{1,13},{5,9},{9,5},{13,1},{2,14},{6,10},... | collective-permute-start | bytes 589832 | tf_op jit(solution)/shard_map/d_weight/ppermute | solution.py:290
  130.9 1.7 %collective-permute-start.18 = (bf16[8,16,768]{2,1,0:T(8,128)(2,1)S(1)}, bf16[8,16,768]{2,1,0:T(8,128)(2,1)S(1)}, u32[]{:S(2)}, u32[]{:S(2)}) collective-permute-start(bf16[8,16,768]{2,1,0:T(8,128)(2,1)S(1)} %bitcast.107), channel_id=1, source_target_pairs={{0,8},{4,12},{8,0},{12,4},{1,9},{5,13},{9,1},{13,5},{2,10},{6,14},... | collective-permute-start | bytes 589832 | tf_op jit(solution)/shard_map/d_weight/ppermute | solution.py:290
  133.2 2.5 %collective-permute-done.19 = bf16[8,16,768]{2,1,0:T(8,128)(2,1)S(1)} collective-permute-done((bf16[8,16,768]{2,1,0:T(8,128)(2,1)S(1)}, bf16[8,16,768]{2,1,0:T(8,128)(2,1)S(1)}, u32[]{:S(2)}, u32[]{:S(2)}) %collective-permute-start.19) | collective-permute-done | bytes 196640 | tf_op jit(solution)/shard_map/d_weight/ppermute | solution.py:290
  136.4 2.0 %collective-permute-done.18 = bf16[8,16,768]{2,1,0:T(8,128)(2,1)S(1)} collective-permute-done((bf16[8,16,768]{2,1,0:T(8,128)(2,1)S(1)}, bf16[8,16,768]{2,1,0:T(8,128)(2,1)S(1)}, u32[]{:S(2)}, u32[]{:S(2)}) %collective-permute-start.18) | collective-permute-done | bytes 196640 | tf_op jit(solution)/shard_map/d_weight/ppermute | solution.py:290
  138.5 3.3 %collective-permute-start.23 = (bf16[2,2,16,768]{3,2,1,0:T(8,128)(2,1)S(1)}, bf16[2,2,16,768]{3,2,1,0:T(8,128)(2,1)S(1)}, u32[]{:S(2)}, u32[]{:S(2)}) collective-permute-start(bf16[2,2,16,768]{3,2,1,0:T(8,128)(2,1)S(1)} %fusion.29), channel_id=1, source_target_pairs={{0,16},{16,0},{1,17},{17,1},{2,18},{18,2},{3,19},{19,3},{4,20},{20... | collective-permute-start | bytes 294920 | tf_op jit(solution)/shard_map/d_weight/ppermute | solution.py:14
  141.8 2.1 %d_tokens.3.refs_0_ = bf16[768,1024]{1,0:T(8,128)(2,1)} custom-call(bf16[256,1024]{1,0:T(8,128)(2,1)} %copy-done.1, bf16[256,1024]{1,0:T(8,128)(2,1)} %copy-done.5), custom_call_target="tpu_custom_call" | custom-call | flops 1000 | bytes 1000 | tf_op jit(solution)/shard_map/d_tokens/pallas_call | solution.py:143
  144.6 2.1 %d_tokens.4.refs_0_ = bf16[768,1024]{1,0:T(8,128)(2,1)} custom-call(bf16[256,1024]{1,0:T(8,128)(2,1)} %copy-done.3, bf16[256,1024]{1,0:T(8,128)(2,1)} %copy-done.6, bf16[768,1024]{1,0:T(8,128)(2,1)} %d_tokens.3.refs_0_), custom_call_target="tpu_custom_call", output_to_operand_aliasing={{}: (2, {})} | custom-call | flops 1000 | bytes 1000 | tf_op jit(solution)/shard_map/d_tokens/pallas_call | solution.py:143
  146.8 1.0 collective-permute-start.24
  147.8 1.8 %collective-permute-start.26 = (f32[16,768]{1,0:T(8,128)S(1)}, f32[16,768]{1,0:T(8,128)S(1)}, u32[]{:S(2)}, u32[]{:S(2)}) collective-permute-start(f32[16,768]{1,0:T(8,128)S(1)} %get-tuple-element.68), channel_id=1, source_target_pairs={{0,96},{32,64},{64,32},{96,0},{1,97},{33,65},{65,33},{97,1},{2,98}... | collective-permute-start | bytes 147464 | tf_op jit(solution)/shard_map/d_weight/ppermute | solution.py:305
  149.6 1.5 collective-permute-start.25
  151.2 2.0 %collective-permute-done.26 = f32[16,768]{1,0:T(8,128)S(1)} collective-permute-done((f32[16,768]{1,0:T(8,128)S(1)}, f32[16,768]{1,0:T(8,128)S(1)}, u32[]{:S(2)}, u32[]{:S(2)}) %collective-permute-start.26) | collective-permute-done | bytes 49184 | tf_op jit(solution)/shard_map/d_weight/ppermute | solution.py:305
  153.2 2.0 %collective-permute-done.25 = f32[16,768]{1,0:T(8,128)S(1)} collective-permute-done((f32[16,768]{1,0:T(8,128)S(1)}, f32[16,768]{1,0:T(8,128)S(1)}, u32[]{:S(2)}, u32[]{:S(2)}) %collective-permute-start.25) | collective-permute-done | bytes 49184 | tf_op jit(solution)/shard_map/d_weight/ppermute | solution.py:304
  156.0 0.8 copy-done.7
  156.8 2.1 %d_tokens.5 = bf16[768,1024]{1,0:T(8,128)(2,1)} custom-call(bf16[256,1024]{1,0:T(8,128)(2,1)} %copy-done.2, bf16[256,1024]{1,0:T(8,128)(2,1)} %copy-done.7, bf16[768,1024]{1,0:T(8,128)(2,1)} %d_tokens.4.refs_0_), custom_call_target="tpu_custom_call", output_to_operand_aliasing={{}: (2, {})} | custom-call | flops 1000 | bytes 1000 | tf_op jit(solution)/shard_map/d_tokens/pallas_call | solution.py:143
  (93 shorter events, 10.2 us)
Async XLA Ops:
  0.6 11.7 %copy-start.8 = (s32[768]{0:T(1024)S(1)}, s32[768]{0:T(1024)}, u32[]{:S(2)}) copy-start(s32[768]{0:T(1024)} %param.8) | copy-start | bytes 9220
  1.6 10.7 %collective-permute-start.2 = (bf16[16,768]{1,0:T(8,128)(2,1)S(1)}, bf16[16,768]{1,0:T(8,128)(2,1)S(1)}, u32[]{:S(2)}, u32[]{:S(2)}) collective-permute-start(bf16[16,768]{1,0:T(8,128)(2,1)S(1)} %get-tuple-element.70), channel_id=1, source_target_pairs={{0,96},{32,64},{64,32},{96,0},{1,97},{33,65},{65,33},{97,1},{2,98}... | collective-permute-start | bytes 73736 | tf_op jit(solution)/shard_map/weights/ppermute | solution.py:233
  5.8 6.5 %collective-permute-start = (bf16[16,768]{1,0:T(8,128)(2,1)S(1)}, bf16[16,768]{1,0:T(8,128)(2,1)S(1)}, u32[]{:S(2)}, u32[]{:S(2)}) collective-permute-start(bf16[16,768]{1,0:T(8,128)(2,1)S(1)} %get-tuple-element.71), channel_id=1, source_target_pairs={{0,32},{32,0},{64,96},{96,64},{1,33},{33,1},{65,97},{97,65},{2,34}... | collective-permute-start | bytes 73736 | tf_op jit(solution)/shard_map/weights/ppermute | solution.py:231
  6.5 5.7 %collective-permute-start.1 = (bf16[19,768]{1,0:T(8,128)(2,1)S(1)}, bf16[19,768]{1,0:T(8,128)(2,1)S(1)}, u32[]{:S(2)}, u32[]{:S(2)}) collective-permute-start(bf16[19,768]{1,0:T(8,128)(2,1)S(1)} %pad_maximum_fusion.3), channel_id=1, source_target_pairs={{0,64},{32,96},{64,0},{96,32},{1,65},{33,97},{65,1},{97,33},{2,66}... | collective-permute-start | bytes 87560 | tf_op jit(solution)/shard_map/weights/ppermute | solution.py:228
  10.2 14.7 %collective-permute-start.4 = (bf16[256,1024]{1,0:T(8,128)(2,1)S(1)}, bf16[256,1024]{1,0:T(8,128)(2,1)}, u32[]{:S(2)}, u32[]{:S(2)}) collective-permute-start(bf16[256,1024]{1,0:T(8,128)(2,1)S(1)} %get-tuple-element.47), channel_id=1, source_target_pairs={{0,64},{64,0},{1,65},{65,1},{2,66},{66,2},{3,67},{67,3},{4,68},{68... | collective-permute-start | bytes 1572872 | tf_op jit(solution)/shard_map/tokens/ppermute | solution.py:14
  12.4 18.6 %copy-start.9 = (f32[8]{0:T(128)S(1)}, f32[8]{0:T(128)}, u32[]{:S(2)}) copy-start(f32[8]{0:T(128)} %param.9) | copy-start | bytes 100
  12.4 8.3 %collective-permute-start.3 = (bf16[4,1,16,768]{3,2,0,1:T(8,128)(2,1)S(1)}, bf16[4,1,16,768]{3,2,0,1:T(8,128)(2,1)S(1)}, u32[]{:S(2)}, u32[]{:S(2)}) collective-permute-start(bf16[4,1,16,768]{3,2,0,1:T(8,128)(2,1)S(1)} %bitcast.98), channel_id=1, source_target_pairs={{0,16},{16,0},{1,17},{17,1},{2,18},{18,2},{3,19},{19,3},{4,20},{20... | collective-permute-start | bytes 294920 | tf_op jit(solution)/shard_map/weights/ppermute | solution.py:14
  25.0 10.1 %collective-permute-start.9 = (bf16[8,16,768]{2,1,0:T(8,128)(2,1)S(1)}, bf16[8,16,768]{2,1,0:T(8,128)(2,1)S(1)}, u32[]{:S(2)}, u32[]{:S(2)}) collective-permute-start(bf16[8,16,768]{2,1,0:T(8,128)(2,1)S(1)} %bitcast.100), channel_id=1, source_target_pairs={{0,12},{4,8},{8,4},{12,0},{1,13},{5,9},{9,5},{13,1},{2,14},{6,10},... | collective-permute-start | bytes 589832 | tf_op jit(solution)/shard_map/weights/ppermute | solution.py:246
  27.7 8.5 %collective-permute-start.8 = (bf16[8,16,768]{2,1,0:T(8,128)(2,1)S(1)}, bf16[8,16,768]{2,1,0:T(8,128)(2,1)S(1)}, u32[]{:S(2)}, u32[]{:S(2)}) collective-permute-start(bf16[8,16,768]{2,1,0:T(8,128)(2,1)S(1)} %bitcast.101), channel_id=1, source_target_pairs={{0,8},{4,12},{8,0},{12,4},{1,9},{5,13},{9,1},{13,5},{2,10},{6,14},... | collective-permute-start | bytes 589832 | tf_op jit(solution)/shard_map/weights/ppermute | solution.py:246
  28.5 7.7 %collective-permute-start.7 = (bf16[8,16,768]{2,1,0:T(8,128)(2,1)S(1)}, bf16[8,16,768]{2,1,0:T(8,128)(2,1)S(1)}, u32[]{:S(2)}, u32[]{:S(2)}) collective-permute-start(bf16[8,16,768]{2,1,0:T(8,128)(2,1)S(1)} %bitcast.102), channel_id=1, source_target_pairs={{0,4},{4,0},{8,12},{12,8},{1,5},{5,1},{9,13},{13,9},{2,6},{6,2},{1... | collective-permute-start | bytes 589832 | tf_op jit(solution)/shard_map/weights/ppermute | solution.py:246
  29.0 14.5 %collective-permute-start.6 = (bf16[256,1024]{1,0:T(8,128)(2,1)}, bf16[256,1024]{1,0:T(8,128)(2,1)}, u32[]{:S(2)}, u32[]{:S(2)}) collective-permute-start(bf16[256,1024]{1,0:T(8,128)(2,1)} %get-tuple-element.46), channel_id=1, source_target_pairs={{0,64},{64,0},{1,65},{65,1},{2,66},{66,2},{3,67},{67,3},{4,68},{68... | collective-permute-start | bytes 1572872 | tf_op jit(solution)/shard_map/tokens/ppermute | solution.py:14
  31.1 11.4 %collective-permute-start.5 = (bf16[256,1024]{1,0:T(8,128)(2,1)}, bf16[256,1024]{1,0:T(8,128)(2,1)}, u32[]{:S(2)}, u32[]{:S(2)}) collective-permute-start(bf16[256,1024]{1,0:T(8,128)(2,1)} %collective-permute-done.4), channel_id=1, source_target_pairs={{0,1},{1,0},{2,3},{3,2},{4,5},{5,4},{6,7},{7,6},{8,9},{9,8},{10,11... | collective-permute-start | bytes 1572872 | tf_op jit(solution)/shard_map/weights/ppermute | solution.py:14
  36.3 1.1 copy-start.4
  36.5 8.2 %collective-permute-start.10 = (bf16[8,4,16,768]{3,2,1,0:T(8,128)(2,1)S(1)}, bf16[8,4,16,768]{3,2,1,0:T(8,128)(2,1)S(1)}, u32[]{:S(2)}, u32[]{:S(2)}) collective-permute-start(bf16[8,4,16,768]{3,2,1,0:T(8,128)(2,1)S(1)} %get-tuple-element.57), channel_id=1, source_target_pairs={{0,2},{2,0},{1,3},{3,1},{4,6},{6,4},{5,7},{7,5},{8,10},{10,8},{9,1... | collective-permute-start | bytes 2359304 | tf_op jit(solution)/shard_map/weights/ppermute | solution.py:14
  37.6 13.6 %collective-permute-start.11 = (bf16[768,256]{1,0:T(8,128)(2,1)S(1)}, bf16[768,256]{1,0:T(8,128)(2,1)S(1)}, u32[]{:S(2)}, u32[]{:S(2)}) collective-permute-start(bf16[768,256]{1,0:T(8,128)(2,1)S(1)} %get-tuple-element.51), channel_id=1, source_target_pairs={{0,64},{64,0},{1,65},{65,1},{2,66},{66,2},{3,67},{67,3},{4,68},{68... | collective-permute-start | bytes 1179656 | tf_op jit(solution)/shard_map/bias/ppermute | solution.py:14
  44.7 1.4 copy-start
  46.1 5.1 %slice-start = ((s8[9437184]{0:T(1024)(128)(4,1)}), s8[4194304]{0:T(1024)(128)(4,1)S(1)}, s32[]{:S(2)}) async-start(s8[9437184]{0:T(1024)(128)(4,1)} %bitcast.89), calls=%async_computation | async-start | bytes 8388608
  46.1 5.1 %slice-start.1 = ((s8[9437184]{0:T(1024)(128)(4,1)}), s8[4194304]{0:T(1024)(128)(4,1)S(1)}, s32[]{:S(2)}) async-start(s8[9437184]{0:T(1024)(128)(4,1)} %bitcast.89), calls=%async_computation.1 | async-start | bytes 8388608
  47.5 3.7 %slice-start.2 = ((s8[9437184]{0:T(1024)(128)(4,1)}), s8[1048576]{0:T(1024)(128)(4,1)S(1)}, s32[]{:S(2)}) async-start(s8[9437184]{0:T(1024)(128)(4,1)} %bitcast.89), calls=%async_computation.2 | async-start | bytes 2097152
  47.5 58.4 %collective-permute-start.14 = (bf16[1024,768]{1,0:T(8,128)(2,1)S(1)}, bf16[1024,768]{1,0:T(8,128)(2,1)S(1)}, u32[]{:S(2)}, u32[]{:S(2)}) collective-permute-start(bf16[1024,768]{1,0:T(8,128)(2,1)S(1)} %bitcast.95), channel_id=1, source_target_pairs={{0,64},{64,0},{1,65},{65,1},{2,66},{66,2},{3,67},{67,3},{4,68},{68... | collective-permute-start | bytes 4718600 | tf_op jit(solution)/shard_map/d_tokens/ppermute | solution.py:14
  72.7 24.1 %collective-permute-start.12 = (bf16[768,384]{1,0:T(8,128)(2,1)S(1)}, bf16[768,384]{1,0:T(8,128)(2,1)S(1)}, u32[]{:S(2)}, u32[]{:S(2)}) collective-permute-start(bf16[768,384]{1,0:T(8,128)(2,1)S(1)} %get-tuple-element.29.refs_1_), channel_id=1, source_target_pairs={{0,64},{64,0},{1,65},{65,1},{2,66},{66,2},{3,67},{67,3},{4,68},{68... | collective-permute-start | bytes 1769480 | tf_op jit(solution)/shard_map/d_tokens/ppermute | solution.py:14
  102.2 24.8 %collective-permute-start.13 = (f32[512,768]{1,0:T(8,128)S(1)}, f32[512,768]{1,0:T(8,128)S(1)}, u32[]{:S(2)}, u32[]{:S(2)}) collective-permute-start(f32[512,768]{1,0:T(8,128)S(1)} %get-tuple-element.36), channel_id=1, source_target_pairs={{0,2},{2,0},{1,3},{3,1},{4,6},{6,4},{5,7},{7,5},{8,10},{10,8},{9,1... | collective-permute-start | bytes 4718600 | tf_op jit(solution)/shard_map/d_weight/ppermute | solution.py:14
  102.3 9.3 %collective-permute-start.15 = (bf16[256,384]{1,0:T(8,128)(2,1)S(1)}, bf16[256,384]{1,0:T(8,128)(2,1)S(1)}, u32[]{:S(2)}, u32[]{:S(2)}) collective-permute-start(bf16[256,384]{1,0:T(8,128)(2,1)S(1)} %get-tuple-element.32), channel_id=1, source_target_pairs={{0,64},{64,0},{1,65},{65,1},{2,66},{66,2},{3,67},{67,3},{4,68},{68... | collective-permute-start | bytes 589832 | tf_op jit(solution)/shard_map/d_tokens/ppermute | solution.py:14
  104.4 15.2 %collective-permute-start.20 = (bf16[512,384]{1,0:T(8,128)(2,1)S(1)}, bf16[512,384]{1,0:T(8,128)(2,1)S(1)}, u32[]{:S(2)}, u32[]{:S(2)}) collective-permute-start(bf16[512,384]{1,0:T(8,128)(2,1)S(1)} %get-tuple-element.33), channel_id=1, source_target_pairs={{0,64},{64,0},{1,65},{65,1},{2,66},{66,2},{3,67},{67,3},{4,68},{68... | collective-permute-start | bytes 1179656 | tf_op jit(solution)/shard_map/d_tokens/ppermute | solution.py:14
  112.1 15.2 %copy-start.1 = (bf16[256,1024]{1,0:T(8,128)(2,1)}, bf16[256,1024]{1,0:T(8,128)(2,1)S(1)}, u32[]{:S(2)}) copy-start(bf16[256,1024]{1,0:T(8,128)(2,1)S(1)} %fusion.12.mine_ref) | copy-start | bytes 1572868
  112.1 14.9 %collective-permute-start.16 = (bf16[256,1024]{1,0:T(8,128)(2,1)S(1)}, bf16[256,1024]{1,0:T(8,128)(2,1)S(1)}, u32[]{:S(2)}, u32[]{:S(2)}) collective-permute-start(bf16[256,1024]{1,0:T(8,128)(2,1)S(1)} %fusion.12.mine_ref), channel_id=1, source_target_pairs={{0,1},{1,0},{2,3},{3,2},{4,5},{5,4},{6,7},{7,6},{8,9},{9,8},{10,11... | collective-permute-start | bytes 1572872 | tf_op jit(solution)/shard_map/d_weight/ppermute | solution.py:14
  120.0 7.2 %copy-start.3 = (bf16[256,1024]{1,0:T(8,128)(2,1)}, bf16[256,1024]{1,0:T(8,128)(2,1)S(1)}, u32[]{:S(2)}) copy-start(bf16[256,1024]{1,0:T(8,128)(2,1)S(1)} %fusion.11.mine_ref) | copy-start | bytes 1572868
  120.0 18.4 %collective-permute-start.21 = (bf16[256,1024]{1,0:T(8,128)(2,1)S(1)}, bf16[256,1024]{1,0:T(8,128)(2,1)S(1)}, u32[]{:S(2)}, u32[]{:S(2)}) collective-permute-start(bf16[256,1024]{1,0:T(8,128)(2,1)S(1)} %fusion.11.mine_ref), channel_id=1, source_target_pairs={{0,1},{1,0},{2,3},{3,2},{4,5},{5,4},{6,7},{7,6},{8,9},{9,8},{10,11... | collective-permute-start | bytes 1572872 | tf_op jit(solution)/shard_map/d_weight/ppermute | solution.py:14
  127.0 0.8 copy-start.5
  127.9 7.8 %collective-permute-start.19 = (bf16[8,16,768]{2,1,0:T(8,128)(2,1)S(1)}, bf16[8,16,768]{2,1,0:T(8,128)(2,1)S(1)}, u32[]{:S(2)}, u32[]{:S(2)}) collective-permute-start(bf16[8,16,768]{2,1,0:T(8,128)(2,1)S(1)} %bitcast.109), channel_id=1, source_target_pairs={{0,12},{4,8},{8,4},{12,0},{1,13},{5,9},{9,5},{13,1},{2,14},{6,10},... | collective-permute-start | bytes 589832 | tf_op jit(solution)/shard_map/d_weight/ppermute | solution.py:290
  130.7 5.7 %collective-permute-start.17 = (bf16[8,16,768]{2,1,0:T(8,128)(2,1)S(1)}, bf16[8,16,768]{2,1,0:T(8,128)(2,1)S(1)}, u32[]{:S(2)}, u32[]{:S(2)}) collective-permute-start(bf16[8,16,768]{2,1,0:T(8,128)(2,1)S(1)} %bitcast.108), channel_id=1, source_target_pairs={{0,4},{4,0},{8,12},{12,8},{1,5},{5,1},{9,13},{13,9},{2,6},{6,2},{1... | collective-permute-start | bytes 589832 | tf_op jit(solution)/shard_map/d_weight/ppermute | solution.py:290
  130.9 7.5 %collective-permute-start.18 = (bf16[8,16,768]{2,1,0:T(8,128)(2,1)S(1)}, bf16[8,16,768]{2,1,0:T(8,128)(2,1)S(1)}, u32[]{:S(2)}, u32[]{:S(2)}) collective-permute-start(bf16[8,16,768]{2,1,0:T(8,128)(2,1)S(1)} %bitcast.107), channel_id=1, source_target_pairs={{0,8},{4,12},{8,0},{12,4},{1,9},{5,13},{9,1},{13,5},{2,10},{6,14},... | collective-permute-start | bytes 589832 | tf_op jit(solution)/shard_map/d_weight/ppermute | solution.py:290
  133.1 10.8 %copy-start.2 = (bf16[256,1024]{1,0:T(8,128)(2,1)}, bf16[256,1024]{1,0:T(8,128)(2,1)S(1)}, u32[]{:S(2)}) copy-start(bf16[256,1024]{1,0:T(8,128)(2,1)S(1)} %fusion.10.mine_ref) | copy-start | bytes 1572868
  138.5 6.1 %copy-start.6 = (bf16[256,1024]{1,0:T(8,128)(2,1)}, bf16[256,1024]{1,0:T(8,128)(2,1)S(1)}, u32[]{:S(2)}) copy-start(bf16[256,1024]{1,0:T(8,128)(2,1)S(1)} %collective-permute-done.21.theirs_ref) | copy-start | bytes 1572868
  138.5 8.2 %collective-permute-start.23 = (bf16[2,2,16,768]{3,2,1,0:T(8,128)(2,1)S(1)}, bf16[2,2,16,768]{3,2,1,0:T(8,128)(2,1)S(1)}, u32[]{:S(2)}, u32[]{:S(2)}) collective-permute-start(bf16[2,2,16,768]{3,2,1,0:T(8,128)(2,1)S(1)} %fusion.29), channel_id=1, source_target_pairs={{0,16},{16,0},{1,17},{17,1},{2,18},{18,2},{3,19},{19,3},{4,20},{20... | collective-permute-start | bytes 294920 | tf_op jit(solution)/shard_map/d_weight/ppermute | solution.py:14
  143.9 12.1 %collective-permute-start.22 = (bf16[256,1024]{1,0:T(8,128)(2,1)S(1)}, bf16[256,1024]{1,0:T(8,128)(2,1)S(1)}, u32[]{:S(2)}, u32[]{:S(2)}) collective-permute-start(bf16[256,1024]{1,0:T(8,128)(2,1)S(1)} %fusion.10.mine_ref), channel_id=1, source_target_pairs={{0,1},{1,0},{2,3},{3,2},{4,5},{5,4},{6,7},{7,6},{8,9},{9,8},{10,11... | collective-permute-start | bytes 1572872 | tf_op jit(solution)/shard_map/d_weight/ppermute | solution.py:14
  146.8 4.3 %collective-permute-start.24 = (f32[16,768]{1,0:T(8,128)S(1)}, f32[16,768]{1,0:T(8,128)S(1)}, u32[]{:S(2)}, u32[]{:S(2)}) collective-permute-start(f32[16,768]{1,0:T(8,128)S(1)} %select_bitcast_fusion.6), channel_id=1, source_target_pairs={{0,32},{32,0},{64,96},{96,64},{1,33},{33,1},{65,97},{97,65},{2,34}... | collective-permute-start | bytes 147464 | tf_op jit(solution)/shard_map/d_weight/ppermute | solution.py:305
  147.8 5.4 %collective-permute-start.26 = (f32[16,768]{1,0:T(8,128)S(1)}, f32[16,768]{1,0:T(8,128)S(1)}, u32[]{:S(2)}, u32[]{:S(2)}) collective-permute-start(f32[16,768]{1,0:T(8,128)S(1)} %get-tuple-element.68), channel_id=1, source_target_pairs={{0,96},{32,64},{64,32},{96,0},{1,97},{33,65},{65,33},{97,1},{2,98}... | collective-permute-start | bytes 147464 | tf_op jit(solution)/shard_map/d_weight/ppermute | solution.py:305
  149.6 5.6 %collective-permute-start.25 = (f32[16,768]{1,0:T(8,128)S(1)}, f32[16,768]{1,0:T(8,128)S(1)}, u32[]{:S(2)}, u32[]{:S(2)}) collective-permute-start(f32[16,768]{1,0:T(8,128)S(1)} %get-tuple-element.69), channel_id=1, source_target_pairs={{0,64},{32,96},{64,0},{96,32},{1,65},{33,97},{65,1},{97,33},{2,66}... | collective-permute-start | bytes 147464 | tf_op jit(solution)/shard_map/d_weight/ppermute | solution.py:304
  156.0 0.8 copy-start.7

commit v3 on v2

--- a/solution.py
+++ b/solution.py
@@ -7,7 +7,8 @@
 
 BF = jnp.bfloat16
 F32 = jnp.float32
-TILE = 256
+TILE = 512
+CHUNK = 128
 
 
 def swap(value, axis):
@@ -21,11 +22,11 @@
 def attention_kernel(
     place_ref, slopes_ref, qo, qf, ko, kf, vo, vf, go, gf, logd_ref, near_ref, *rest,
 ):
-    *far_refs, q_s, k_s, v_s, g_s, kt_s, dk_s, dv_s, s_s, dp_s = rest
+    *far_refs, q_s, k_s, v_s, g_s, kt_s, dq_s, dk_s, dv_s, s_s, dp_s = rest
     step = pl.program_id(0)
     rows = qo.shape[0]
     total = 2 * rows
-    chunks = total // TILE
+    steps = total // TILE
 
     @pl.when(step == 0)
     def _():
@@ -37,7 +38,7 @@
         dv_s[...] = jnp.zeros_like(dv_s)
 
     here = pl.ds(pl.multiple_of(step * TILE, TILE), TILE)
-    q = (q_s[here].astype(F32) * 0.125)
+    q = q_s[here].astype(F32) * 0.125
     g = g_s[here].astype(F32)
     q_t, g_t = q.T, g.T
     upper = lax.broadcasted_iota(jnp.int32, (128, TILE), 0) < 64
@@ -47,47 +48,55 @@
     gts = [jnp.where(upper, g_t, zero).astype(BF), jnp.where(upper, zero, g_t).astype(BF)]
     qs = [jnp.where(left, q, zero).astype(BF), jnp.where(left, zero, q).astype(BF)]
     gs = [jnp.where(left, g, zero).astype(BF), jnp.where(left, zero, g).astype(BF)]
-    for h in range(2):
-        slope = slopes_ref[h]
-        top = None
-        for c in range(chunks):
-            part = slice(c * TILE, (c + 1) * TILE)
-            score = dot(k_s[part], qts[h]) - slope * logd_ref[part]
-            s_s[h, part] = score
-            peak = jnp.max(score, axis=0, keepdims=True)
-            top = peak if top is None else jnp.maximum(top, peak)
-        norm = jnp.zeros((1, TILE), F32)
-        delta = jnp.zeros((1, TILE), F32)
-        for c in range(chunks):
-            part = slice(c * TILE, (c + 1) * TILE)
-            e = jnp.exp(s_s[h, part] - top)
-            s_s[h, part] = e
-            dp = dot(v_s[part], gts[h])
-            dp_s[h, part] = dp
-            norm += jnp.sum(e, axis=0, keepdims=True)
-            delta += jnp.sum(e * dp, axis=0, keepdims=True)
-        inverse = 1.0 / norm
-        delta = delta * inverse
-        dq_t = jnp.zeros((64, TILE), F32)
-        for c in range(chunks):
-            part = slice(c * TILE, (c + 1) * TILE)
-            p = s_s[h, part] * inverse
-            ds = (p * (dp_s[h, part] - delta)).astype(BF)
-            dv_s[part] += dot(p.astype(BF), gs[h])
-            dk_s[part] += dot(ds, qs[h])
-            dq_t += dot(kt_s[h * 64 : (h + 1) * 64, part], ds)
-        s_s[h, :64] = dq_t
-    dq = jnp.concatenate([s_s[0, :64], s_s[1, :64]], 0).T * 0.125
-    @pl.when(step < chunks // 2)
+    top = [jnp.full((1, TILE), -jnp.inf, F32)] * 2
+    norm = [jnp.zeros((1, TILE), F32)] * 2
+    delta = [jnp.zeros((1, TILE), F32)] * 2
+    inverse = [None] * 2
+    dq_t = [jnp.zeros((64, TILE), F32)] * 2
+    parts = [slice(c * CHUNK, (c + 1) * CHUNK) for c in range(total // CHUNK)]
+
+    def scores(h, part):
+        score = dot(k_s[part], qts[h]) - slopes_ref[h] * logd_ref[part]
+        s_s[h, part] = score
+        top[h] = jnp.maximum(top[h], jnp.max(score, axis=0, keepdims=True))
+
+    def sums(h, part):
+        e = jnp.exp(s_s[h, part] - top[h])
+        s_s[h, part] = e
+        dp = dot(v_s[part], gts[h])
+        dp_s[h, part] = dp
+        norm[h] += jnp.sum(e, axis=0, keepdims=True)
+        delta[h] += jnp.sum(e * dp, axis=0, keepdims=True)
+
+    def normalise(h):
+        inverse[h] = 1.0 / norm[h]
+        delta[h] = delta[h] * inverse[h]
+
+    def products(h, part):
+        p = s_s[h, part] * inverse[h]
+        ds = (p * (dp_s[h, part] - delta[h])).astype(BF)
+        dv_s[part] += dot(p.astype(BF), gs[h])
+        dk_s[part] += dot(ds, qs[h])
+        dq_t[h] += dot(kt_s[h * 64 : (h + 1) * 64, part], ds)
+
+    for part in parts:
+        scores(0, part)
+    for part in parts:
+        sums(0, part)
+        scores(1, part)
+    normalise(0)
+    for part in parts:
+        products(0, part)
+        sums(1, part)
+    normalise(1)
+    for part in parts:
+        products(1, part)
+    dq = jnp.concatenate(dq_t, 0).T * 0.125
+    dq_s[here] = dq.astype(BF)
+
+    @pl.when(step == steps - 1)
     def _():
-        near_ref[here, :128] = dq.astype(BF)
-
-    @pl.when(step >= chunks // 2)
-    def _():
-        q_s[here] = dq.astype(BF)
-
-    @pl.when(step == chunks - 1)
-    def _():
+        near_ref[:, :128] = dq_s[:rows]
         near_ref[:, 128:256] = dk_s[:rows].astype(BF)
         near_ref[:, 256:384] = dv_s[:rows].astype(BF)
         third = rows // 3
@@ -97,7 +106,7 @@
                 at = (first + k) ^ place_ref[0] if first + k < 2 else first + k
                 part = pl.ds(pl.multiple_of(rows + at * third, 64), third)
                 mine = slice(k * third, (k + 1) * third)
-                far_ref[mine, :128] = q_s[part]
+                far_ref[mine, :128] = dq_s[part]
                 far_ref[mine, 128:256] = dk_s[part].astype(BF)
                 far_ref[mine, 256:384] = dv_s[part].astype(BF)
             first += far_ref.shape[0] // third
@@ -124,10 +133,10 @@
         out_specs=[pl.BlockSpec((n, 384), lambda t: (0, 0)) for n in sizes],
         out_shape=[jax.ShapeDtypeStruct((n, 384), BF) for n in sizes],
         scratch_shapes=[pltpu.VMEM((total, 128), BF)] * 4
-        + [pltpu.VMEM((128, total), BF)]
+        + [pltpu.VMEM((128, total), BF), pltpu.VMEM((total, 128), BF)]
         + [pltpu.VMEM((total, 128), F32)] * 2
         + [pltpu.VMEM((2, total, TILE), F32)] * 2,
-        compiler_params=pltpu.CompilerParams(vmem_limit_bytes=32 * 2**20),
+        compiler_params=pltpu.CompilerParams(vmem_limit_bytes=44 * 2**20),
         cost_estimate=pl.CostEstimate(
             flops=2 * 5 * 2 * total * total * 256, bytes_accessed=4 * total * total, transcendentals=2 * total * total
         ),
@@ -203,6 +212,11 @@
     return jnp.where(place == 0, first, second), jnp.where(place == 0, second, first)
 
 
+def by_core(own, other, core):
+    both = jnp.where(core == 0, jnp.stack([own, other], 2), jnp.stack([other, own], 2))
+    return both.reshape(1024, own.shape[-1])
+
+
 def ordered(own, other, place):
     return jnp.where(place == 0, jnp.concatenate([own, other], 0), jnp.concatenate([other, own], 0))
 
@@ -241,14 +255,14 @@
         w, grad_attn = lax.optimization_barrier((jnp.stack(pieces)[:, None], grad_attn))
         other = swap(w, "yh")
         w = jnp.where(y_hi == 0, jnp.concatenate([w, other], 1), jnp.concatenate([other, w], 1)).reshape(8, 16, 768)
-        w, got[0], logd = lax.optimization_barrier((w, got[0], logd))
+        w, logd = lax.optimization_barrier((w, logd))
+        pieces = [w] + [lax.ppermute(w, "x", [(i, i ^ j) for i in range(4)]) for j in range(1, 4)]
+        pieces[1], got[0] = lax.optimization_barrier((pieces[1], got[0]))
         relayed = swap(got[0], "h")
-        pieces = [w] + [lax.ppermute(w, "x", [(i, i ^ j) for i in range(4)]) for j in range(1, 4)]
         pieces = [jnp.where((x & 1) == 0, pieces[i], pieces[i ^ 1]) for i in range(4)]
         pieces = [jnp.where((x & 2) == 0, pieces[i], pieces[i ^ 2]) for i in range(4)]
-        w = jnp.stack(pieces, 1)
-        other = swap(w, "c")
-        w = jnp.where(core == 0, jnp.stack([w, other], 2), jnp.stack([other, w], 2)).reshape(1024, 768)
+        w_core = jnp.stack(pieces, 1)
+        w = by_core(w_core, swap(w_core, "c"), core)
         far_tokens = jnp.concatenate([got[0], relayed, got[1]], 0)
 
     with jax.named_scope("bias"):
@@ -261,11 +275,13 @@
         far = dot(far_tokens, w).astype(BF)
     with jax.named_scope("attention"):
         near0, far0 = attention(head, slopes[:2], near, far, g_near, g_far, logd, 0, [rows])
-        g_near, near0 = lax.optimization_barrier((g_near, near0))
+        w_core, near = lax.optimization_barrier((w_core, near))
+        w_other = swap(w_core, "zh")
+        g_near, near0, w_other = lax.optimization_barrier((g_near, near0, w_other))
         near1, *far1 = attention(head, slopes[2:], near, far, g_near, g_far, logd, 1, [third, 2 * third])
 
     with jax.named_scope("d_tokens"):
-        w_other = swap(w, "zh")
+        w_other = by_core(w_other, swap(w_other, "c"), core)
         back0 = swap(far0, "zh")
         back1 = [swap(part, "zh") for part in far1]
         base = dot(
@@ -279,7 +295,7 @@
 
     with jax.named_scope("d_weight"):
         far1 = jnp.concatenate(far1, 0)
-        far1, back0 = lax.optimization_barrier((far1, back0))
+        far1, back0, mine[0] = lax.optimization_barrier((far1, back0, mine[0]))
         keep, send = weight_terms(jnp.stack([core, x, head]), tokens, far_tokens, [near0, far0, near1, far1])
         other = swap(send, "c")
         theirs = [swap(mine[0], "h")]

time: 159 us -> 151 us (0.950)
  Pallas kernels: 54.6 us -> 48.9 us
  starting transfers between devices: 44.8 us -> 40.4 us
    pallas_call x2, Pallas kernels: 42.9 us -> 37.2 us  [attention(): pl.pallas_call(attention_kernel, grid=(total // TILE,), in_specs=[pl.Bloc...]
    ppermute x15 -> x16, starting transfers between devices: 25.8 us -> 21.2 us  [swap(): return lax.ppermute(value, axis, [(0, 1), (1, 0)])]
    ppermute x15 -> x16, waiting for transfers between devices: 21.6 us -> 19.3 us  [swap(): return lax.ppermute(value, axis, [(0, 1), (1, 0)])]
    ppermute x3, waiting for transfers between devices: 3.55 us -> 5.84 us  [on_device(): lax.ppermute(w, 'x', [(i, i ^ j) for i in range(4)])]
    ppermute x1, waiting for transfers between devices: 1.98 us -> 0.01 us  [on_device(): mine_w = lax.ppermute(mine_w, ('zh', 'zl'), [(i, i ^ 2) for i in range(4)])]
    ppermute x3, waiting for transfers between devices: 5.23 us -> 6.96 us  [on_device(): lax.ppermute(term[j].astype(BF), 'x', [(i, i ^ j) for i in range(4)])]
    unnamed x28 -> x22, local copies, waits for them, and re-layouts: 5.58 us -> 5.55 us
  transfers between devices with their start and end apart: 27 -> 28, of which waited for: 14 -> 12; matrix products, arithmetic and copies ran while one was open for 12% -> 13% of each run, Pallas kernels for 33% -> 28%
where the time goes in v3:
time: 151 us
  Pallas kernels  48.9 us (32%)
  starting transfers between devices  40.4 us (27%)
  waiting for transfers between devices  35.6 us (24%)
  local copies, waits for them, and re-layouts  11 us (7%)
  other arithmetic  7.14 us (5%)
  matrix products  6.44 us (4%)
    pallas_call x2, Pallas kernels, attention(): pl.pallas_call(attention_kernel, grid=(total // TILE,), in_specs=[pl.Bloc...  37.2 us
    ppermute x16, starting transfers between devices, swap(): return lax.ppermute(value, axis, [(0, 1), (1, 0)])  21.2 us
    ppermute x16, waiting for transfers between devices, swap(): return lax.ppermute(value, axis, [(0, 1), (1, 0)])  19.3 us
    ppermute x3, waiting for transfers between devices, on_device(): lax.ppermute(term[j].astype(BF), 'x', [(i, i ^ j) for i in range(4)])  6.96 us
    dot_general x6, matrix products, dot(): return lax.dot_general(a, b, (dims, ((), ())), preferred_element_type=F32)  6.44 us
    pallas_call x3, Pallas kernels, add_rows(): pl.pallas_call(add_kernel, grid=(1,), in_specs=[pl.BlockSpec((rows, width...  6.34 us
    ppermute x3, waiting for transfers between devices, on_device(): lax.ppermute(w, 'x', [(i, i ^ j) for i in range(4)])  5.84 us
    unnamed x22, local copies, waits for them, and re-layouts  5.55 us
  transfers between devices with their start and end apart: 28, of which 12 were waited for; matrix products, arithmetic and copies ran while one was open for 13% of the time, Pallas kernels for 28%

profile of v3, /device:TPU:0, one launch (start us, length us, event | category | flops | bytes accessed | tf_op | source)
XLA Modules:
  0.0 150.6 jit_solution(6489132373764625676)
XLA Ops:
  0.6 0.8 reshape.96
  1.6 4.2 %collective-permute-start.2 = (bf16[16,768]{1,0:T(8,128)(2,1)S(1)}, bf16[16,768]{1,0:T(8,128)(2,1)S(1)}, u32[]{:S(2)}, u32[]{:S(2)}) collective-permute-start(bf16[16,768]{1,0:T(8,128)(2,1)S(1)} %get-tuple-element.80), channel_id=1, source_target_pairs={{0,96},{32,64},{64,32},{96,0},{1,97},{33,65},{65,33},{97,1},{2,98}... | collective-permute-start | bytes 73736 | tf_op jit(solution)/shard_map/weights/ppermute | solution.py:247
  6.5 1.6 %collective-permute-start.1 = (bf16[19,768]{1,0:T(8,128)(2,1)S(1)}, bf16[19,768]{1,0:T(8,128)(2,1)S(1)}, u32[]{:S(2)}, u32[]{:S(2)}) collective-permute-start(bf16[19,768]{1,0:T(8,128)(2,1)S(1)} %pad_maximum_fusion.3), channel_id=1, source_target_pairs={{0,64},{32,96},{64,0},{96,32},{1,65},{33,97},{65,1},{97,33},{2,66}... | collective-permute-start | bytes 87560 | tf_op jit(solution)/shard_map/weights/ppermute | solution.py:242
  8.2 2.1 %fusion.35 = (bf16[256,1024]{1,0:T(8,128)(2,1)}, bf16[256,1024]{1,0:T(8,128)(2,1)S(1)}) fusion(bf16[768,1024]{1,0:T(8,128)(2,1)} %near_ref.1, s32[]{:T(128)S(6)} %select_n.233), kind=kLoop, calls=%fused_computation.90 | loop fusion | bytes 2097156 | tf_op jit(solution)/shard_map/tokens/slice | solution.py:235
  10.2 2.0 %collective-permute-start.5 = (bf16[256,1024]{1,0:T(8,128)(2,1)S(1)}, bf16[256,1024]{1,0:T(8,128)(2,1)}, u32[]{:S(2)}, u32[]{:S(2)}) collective-permute-start(bf16[256,1024]{1,0:T(8,128)(2,1)S(1)} %get-tuple-element.57), channel_id=1, source_target_pairs={{0,64},{64,0},{1,65},{65,1},{2,66},{66,2},{3,67},{67,3},{4,68},{68... | collective-permute-start | bytes 1572872 | tf_op jit(solution)/shard_map/tokens/ppermute | solution.py:15
  12.4 3.3 %collective-permute-start.3 = (bf16[4,1,16,768]{3,2,0,1:T(8,128)(2,1)S(1)}, bf16[4,1,16,768]{3,2,0,1:T(8,128)(2,1)S(1)}, u32[]{:S(2)}, u32[]{:S(2)}) collective-permute-start(bf16[4,1,16,768]{3,2,0,1:T(8,128)(2,1)S(1)} %bitcast.102), channel_id=1, source_target_pairs={{0,16},{16,0},{1,17},{17,1},{2,18},{18,2},{3,19},{19,3},{4,20},{20... | collective-permute-start | bytes 294920 | tf_op jit(solution)/shard_map/weights/ppermute | solution.py:15
  15.7 5.0 %convert_log_fusion.logd_ref = f32[1536,1536]{1,0:T(8,128)} fusion(s32[1536]{0:T(1024)S(1)} %pad_add_fusion), kind=kLoop, calls=%fused_computation | loop fusion | flops 9437184 | bytes 9443328 | tf_op jit(solution)/shard_map/weights/log | solution.py:252
  20.7 1.6 %collective-permute-start.4 = (bf16[8,16,768]{2,1,0:T(8,128)(2,1)S(1)}, bf16[8,16,768]{2,1,0:T(8,128)(2,1)S(1)}, u32[]{:S(2)}, u32[]{:S(2)}) collective-permute-start(bf16[8,16,768]{2,1,0:T(8,128)(2,1)S(1)} %bitcast.104), channel_id=1, source_target_pairs={{0,4},{4,0},{8,12},{12,8},{1,5},{5,1},{9,13},{13,9},{2,6},{6,2},{1... | collective-permute-start | bytes 589832 | tf_op jit(solution)/shard_map/weights/ppermute | solution.py:259
  22.3 2.1 %collective-permute-start.9 = (bf16[8,16,768]{2,1,0:T(8,128)(2,1)S(1)}, bf16[8,16,768]{2,1,0:T(8,128)(2,1)S(1)}, u32[]{:S(2)}, u32[]{:S(2)}) collective-permute-start(bf16[8,16,768]{2,1,0:T(8,128)(2,1)S(1)} %bitcast.105), channel_id=1, source_target_pairs={{0,12},{4,8},{8,4},{12,0},{1,13},{5,9},{9,5},{13,1},{2,14},{6,10},... | collective-permute-start | bytes 589832 | tf_op jit(solution)/shard_map/weights/ppermute | solution.py:259
  25.0 1.6 %collective-permute-start.7 = (bf16[256,1024]{1,0:T(8,128)(2,1)}, bf16[256,1024]{1,0:T(8,128)(2,1)}, u32[]{:S(2)}, u32[]{:S(2)}) collective-permute-start(bf16[256,1024]{1,0:T(8,128)(2,1)} %get-tuple-element.56), channel_id=1, source_target_pairs={{0,64},{64,0},{1,65},{65,1},{2,66},{66,2},{3,67},{67,3},{4,68},{68... | collective-permute-start | bytes 1572872 | tf_op jit(solution)/shard_map/tokens/ppermute | solution.py:15
  26.7 1.2 collective-permute-done.4
  28.6 4.6 %collective-permute-done.9 = bf16[8,16,768]{2,1,0:T(8,128)(2,1)S(1)} collective-permute-done((bf16[8,16,768]{2,1,0:T(8,128)(2,1)S(1)}, bf16[8,16,768]{2,1,0:T(8,128)(2,1)S(1)}, u32[]{:S(2)}, u32[]{:S(2)}) %collective-permute-start.9) | collective-permute-done | bytes 196640 | tf_op jit(solution)/shard_map/weights/ppermute | solution.py:259
  34.6 1.7 %collective-permute-start.11 = (bf16[768,256]{1,0:T(8,128)(2,1)S(1)}, bf16[768,256]{1,0:T(8,128)(2,1)S(1)}, u32[]{:S(2)}, u32[]{:S(2)}) collective-permute-start(bf16[768,256]{1,0:T(8,128)(2,1)S(1)} %get-tuple-element.61), channel_id=1, source_target_pairs={{0,64},{64,0},{1,65},{65,1},{2,66},{66,2},{3,67},{67,3},{4,68},{68... | collective-permute-start | bytes 1179656 | tf_op jit(solution)/shard_map/bias/ppermute | solution.py:15
  36.2 1.1 constant_dynamic-update-slice_fusion.2
  37.3 1.4 collective-permute-done.6
  38.7 1.1 constant_dynamic-update-slice_fusion.1
  39.8 1.1 constant_dynamic-update-slice_fusion.far_ref
  41.1 1.2 copy-done
  42.3 1.4 fusion.9.qo.ko.vo
  43.7 2.2 %collective-permute-start.12 = (bf16[8,4,16,768]{3,2,1,0:T(8,128)(2,1)S(1)}, bf16[8,4,16,768]{3,2,1,0:T(8,128)(2,1)S(1)}, u32[]{:S(2)}, u32[]{:S(2)}) collective-permute-start(bf16[8,4,16,768]{3,2,1,0:T(8,128)(2,1)S(1)} %get-tuple-element.34), channel_id=1, source_target_pairs={{0,64},{64,0},{1,65},{65,1},{2,66},{66,2},{3,67},{67,3},{4,68},{68... | collective-permute-start | bytes 2359304 | tf_op jit(solution)/shard_map/attention/ppermute | solution.py:15
  46.0 1.4 convolution_convert_fusion.1.qf.kf.vf
  47.4 0.8 collective-permute-done.11.gf
  48.2 18.6 %attention.2 = (bf16[768,384]{1,0:T(8,128)(2,1)S(1)}, bf16[768,384]{1,0:T(8,128)(2,1)S(1)}) custom-call(s32[1]{0:T(128)} %bitcast.2.place_ref, f32[2]{0:T(128)S(1)} %get-tuple-element.89.slopes_ref, bf16[768,768]{1,0:T(8,128)(2,1)S(1)} %fusion.9.qo.ko.vo, bf16[768,768]{1,0:T(8,128)(2,1)S(1)} %convolution_convert_fusion.1.qf.kf.vf, ...), custom_call_target="tpu_custom_call" | custom-call | flops 12079595520 | bytes 9437184 | tf_op jit(solution)/shard_map/attention/pallas_call | solution.py:126
  66.8 1.2 collective-permute-start.13
  68.0 18.6 %attention.3 = (bf16[768,384]{1,0:T(8,128)(2,1)S(1)}, bf16[256,384]{1,0:T(8,128)(2,1)S(1)}, bf16[512,384]{1,0:T(8,128)(2,1)S(1)}) custom-call(s32[1]{0:T(128)} %bitcast.2.place_ref, f32[2]{0:T(128)S(1)} %get-tuple-element.88.slopes_ref, bf16[768,768]{1,0:T(8,128)(2,1)S(1)} %fusion.9.qo.ko.vo, bf16[768,768]{1,0:T(8,128)(2,1)S(1)} %convolution_convert_fusion.1.qf.kf.vf, ...), custom_call_target="tpu_custom_call" | custom-call | flops 12079595520 | bytes 9437184 | tf_op jit(solution)/shard_map/attention/pallas_call | solution.py:126
  86.6 2.5 %collective-permute-start.15 = (bf16[256,384]{1,0:T(8,128)(2,1)S(1)}, bf16[256,384]{1,0:T(8,128)(2,1)S(1)}, u32[]{:S(2)}, u32[]{:S(2)}) collective-permute-start(bf16[256,384]{1,0:T(8,128)(2,1)S(1)} %get-tuple-element.40), channel_id=1, source_target_pairs={{0,64},{64,0},{1,65},{65,1},{2,66},{66,2},{3,67},{67,3},{4,68},{68... | collective-permute-start | bytes 589832 | tf_op jit(solution)/shard_map/d_tokens/ppermute | solution.py:15
  89.7 2.2 %fusion = f32[768,1024]{1,0:T(8,128)S(1)} fusion(bf16[1024,384]{1,0:T(8,128)(2,1)S(1)} %slice.169, bf16[1024,768]{1,0:T(8,128)(2,1)S(1)} %bitcast.101, bf16[768,384]{1,0:T(8,128)(2,1)S(1)} %collective-permute-done.13, bf16[768,384]{1,0:T(8,128)(2,1)S(1)} %get-tuple-element.39.refs_2_, bf16[768,384]{1,0:T(8,128)(2,1)S(1)} %get-tuple-element.35.refs_0_), kind=kOutput, calls=%fused_computation.1 | convolution fusion | flops 1821966336 | bytes 7274496 | tf_op jit(solution)/shard_map/d_tokens/dot_general | solution.py:19
  92.0 3.5 %collective-permute-done.15 = bf16[256,384]{1,0:T(8,128)(2,1)S(1)} collective-permute-done((bf16[256,384]{1,0:T(8,128)(2,1)S(1)}, bf16[256,384]{1,0:T(8,128)(2,1)S(1)}, u32[]{:S(2)}, u32[]{:S(2)}) %collective-permute-start.15) | collective-permute-done | bytes 196640 | tf_op jit(solution)/shard_map/d_tokens/ppermute | solution.py:15
  96.0 5.4 %d_weight.1 = (f32[512,768]{1,0:T(8,128)S(1)}, f32[512,768]{1,0:T(8,128)S(1)}) custom-call(s32[3]{0:T(128)S(1)} %pad_add_fusion.1.place_ref, bf16[768,1024]{1,0:T(8,128)(2,1)S(1)} %copy-done, bf16[768,1024]{1,0:T(8,128)(2,1)S(1)} %constant_dynamic-update-slice_fusion.far_ref, bf16[768,384]{1,0:T(8,128)(2,1)S(1)} %get-tuple-element.35.refs_0_, ...), custom_call_target="tpu_custom_call" | custom-call | flops 1000 | bytes 1000 | tf_op jit(solution)/shard_map/d_weight/pallas_call | solution.py:195
  101.5 2.5 %collective-permute-start.21 = (bf16[512,384]{1,0:T(8,128)(2,1)S(1)}, bf16[512,384]{1,0:T(8,128)(2,1)S(1)}, u32[]{:S(2)}, u32[]{:S(2)}) collective-permute-start(bf16[512,384]{1,0:T(8,128)(2,1)S(1)} %get-tuple-element.41), channel_id=1, source_target_pairs={{0,64},{64,0},{1,65},{65,1},{2,66},{66,2},{3,67},{67,3},{4,68},{68... | collective-permute-start | bytes 1179656 | tf_op jit(solution)/shard_map/d_tokens/ppermute | solution.py:15
  104.6 9.9 %collective-permute-done.21 = bf16[512,384]{1,0:T(8,128)(2,1)S(1)} collective-permute-done((bf16[512,384]{1,0:T(8,128)(2,1)S(1)}, bf16[512,384]{1,0:T(8,128)(2,1)S(1)}, u32[]{:S(2)}, u32[]{:S(2)}) %collective-permute-start.21) | collective-permute-done | bytes 393248 | tf_op jit(solution)/shard_map/d_tokens/ppermute | solution.py:15
  115.7 2.7 %collective-permute-done.17.theirs_ref = bf16[256,1024]{1,0:T(8,128)(2,1)S(1)} collective-permute-done((bf16[256,1024]{1,0:T(8,128)(2,1)S(1)}, bf16[256,1024]{1,0:T(8,128)(2,1)S(1)}, u32[]{:S(2)}, u32[]{:S(2)}) %collective-permute-start.17) | collective-permute-done | bytes 524320 | tf_op jit(solution)/shard_map/d_weight/ppermute | solution.py:15
  119.3 1.8 %collective-permute-start.20 = (bf16[8,16,768]{2,1,0:T(8,128)(2,1)S(1)}, bf16[8,16,768]{2,1,0:T(8,128)(2,1)S(1)}, u32[]{:S(2)}, u32[]{:S(2)}) collective-permute-start(bf16[8,16,768]{2,1,0:T(8,128)(2,1)S(1)} %bitcast.115), channel_id=1, source_target_pairs={{0,12},{4,8},{8,4},{12,0},{1,13},{5,9},{9,5},{13,1},{2,14},{6,10},... | collective-permute-start | bytes 589832 | tf_op jit(solution)/shard_map/d_weight/ppermute | solution.py:306
  121.1 1.0 collective-permute-start.18
  122.1 2.0 %collective-permute-start.19 = (bf16[8,16,768]{2,1,0:T(8,128)(2,1)S(1)}, bf16[8,16,768]{2,1,0:T(8,128)(2,1)S(1)}, u32[]{:S(2)}, u32[]{:S(2)}) collective-permute-start(bf16[8,16,768]{2,1,0:T(8,128)(2,1)S(1)} %bitcast.113), channel_id=1, source_target_pairs={{0,8},{4,12},{8,0},{12,4},{1,9},{5,13},{9,1},{13,5},{2,10},{6,14},... | collective-permute-start | bytes 589832 | tf_op jit(solution)/shard_map/d_weight/ppermute | solution.py:306
  124.6 3.1 %collective-permute-done.20 = bf16[8,16,768]{2,1,0:T(8,128)(2,1)S(1)} collective-permute-done((bf16[8,16,768]{2,1,0:T(8,128)(2,1)S(1)}, bf16[8,16,768]{2,1,0:T(8,128)(2,1)S(1)}, u32[]{:S(2)}, u32[]{:S(2)}) %collective-permute-start.20) | collective-permute-done | bytes 196640 | tf_op jit(solution)/shard_map/d_weight/ppermute | solution.py:306
  127.7 1.1 collective-permute-done.18
  128.8 2.7 %collective-permute-done.19 = bf16[8,16,768]{2,1,0:T(8,128)(2,1)S(1)} collective-permute-done((bf16[8,16,768]{2,1,0:T(8,128)(2,1)S(1)}, bf16[8,16,768]{2,1,0:T(8,128)(2,1)S(1)}, u32[]{:S(2)}, u32[]{:S(2)}) %collective-permute-start.19) | collective-permute-done | bytes 196640 | tf_op jit(solution)/shard_map/d_weight/ppermute | solution.py:306
  131.7 1.2 collective-permute-start.24
  133.0 2.1 %d_tokens.3.refs_0_ = bf16[768,1024]{1,0:T(8,128)(2,1)} custom-call(bf16[256,1024]{1,0:T(8,128)(2,1)} %copy-done.1, bf16[256,1024]{1,0:T(8,128)(2,1)} %copy-done.5), custom_call_target="tpu_custom_call" | custom-call | flops 1000 | bytes 1000 | tf_op jit(solution)/shard_map/d_tokens/pallas_call | solution.py:152
  135.1 0.8 collective-permute-start.23
  135.9 2.1 %d_tokens.4.refs_0_ = bf16[768,1024]{1,0:T(8,128)(2,1)} custom-call(bf16[256,1024]{1,0:T(8,128)(2,1)} %copy-done.3, bf16[256,1024]{1,0:T(8,128)(2,1)} %copy-done.6, bf16[768,1024]{1,0:T(8,128)(2,1)} %d_tokens.3.refs_0_), custom_call_target="tpu_custom_call", output_to_operand_aliasing={{}: (2, {})} | custom-call | flops 1000 | bytes 1000 | tf_op jit(solution)/shard_map/d_tokens/pallas_call | solution.py:152
  138.0 0.9 collective-permute-done.24
  139.0 1.9 %collective-permute-start.25 = (f32[16,768]{1,0:T(8,128)S(1)}, f32[16,768]{1,0:T(8,128)S(1)}, u32[]{:S(2)}, u32[]{:S(2)}) collective-permute-start(f32[16,768]{1,0:T(8,128)S(1)} %select_bitcast_fusion.6), channel_id=1, source_target_pairs={{0,32},{32,0},{64,96},{96,64},{1,33},{33,1},{65,97},{97,65},{2,34}... | collective-permute-start | bytes 147464 | tf_op jit(solution)/shard_map/d_weight/ppermute | solution.py:321
  141.0 2.2 %collective-permute-start.26 = (f32[16,768]{1,0:T(8,128)S(1)}, f32[16,768]{1,0:T(8,128)S(1)}, u32[]{:S(2)}, u32[]{:S(2)}) collective-permute-start(f32[16,768]{1,0:T(8,128)S(1)} %get-tuple-element.79), channel_id=1, source_target_pairs={{0,64},{32,96},{64,0},{96,32},{1,65},{33,97},{65,1},{97,33},{2,66}... | collective-permute-start | bytes 147464 | tf_op jit(solution)/shard_map/d_weight/ppermute | solution.py:320
  143.3 3.5 %collective-permute-done.27 = f32[16,768]{1,0:T(8,128)S(1)} collective-permute-done((f32[16,768]{1,0:T(8,128)S(1)}, f32[16,768]{1,0:T(8,128)S(1)}, u32[]{:S(2)}, u32[]{:S(2)}) %collective-permute-start.27) | collective-permute-done | bytes 49184 | tf_op jit(solution)/shard_map/d_weight/ppermute | solution.py:321
  147.7 0.8 copy-done.7
  148.5 2.1 %d_tokens.5 = bf16[768,1024]{1,0:T(8,128)(2,1)} custom-call(bf16[256,1024]{1,0:T(8,128)(2,1)} %copy-done.2, bf16[256,1024]{1,0:T(8,128)(2,1)} %copy-done.7, bf16[768,1024]{1,0:T(8,128)(2,1)} %d_tokens.4.refs_0_), custom_call_target="tpu_custom_call", output_to_operand_aliasing={{}: (2, {})} | custom-call | flops 1000 | bytes 1000 | tf_op jit(solution)/shard_map/d_tokens/pallas_call | solution.py:152
  (90 shorter events, 9.4 us)
Async XLA Ops:
  0.6 11.7 %copy-start.8 = (s32[768]{0:T(1024)S(1)}, s32[768]{0:T(1024)}, u32[]{:S(2)}) copy-start(s32[768]{0:T(1024)} %param.8) | copy-start | bytes 9220
  1.6 10.7 %collective-permute-start.2 = (bf16[16,768]{1,0:T(8,128)(2,1)S(1)}, bf16[16,768]{1,0:T(8,128)(2,1)S(1)}, u32[]{:S(2)}, u32[]{:S(2)}) collective-permute-start(bf16[16,768]{1,0:T(8,128)(2,1)S(1)} %get-tuple-element.80), channel_id=1, source_target_pairs={{0,96},{32,64},{64,32},{96,0},{1,97},{33,65},{65,33},{97,1},{2,98}... | collective-permute-start | bytes 73736 | tf_op jit(solution)/shard_map/weights/ppermute | solution.py:247
  5.8 6.5 %collective-permute-start = (bf16[16,768]{1,0:T(8,128)(2,1)S(1)}, bf16[16,768]{1,0:T(8,128)(2,1)S(1)}, u32[]{:S(2)}, u32[]{:S(2)}) collective-permute-start(bf16[16,768]{1,0:T(8,128)(2,1)S(1)} %get-tuple-element.81), channel_id=1, source_target_pairs={{0,32},{32,0},{64,96},{96,64},{1,33},{33,1},{65,97},{97,65},{2,34}... | collective-permute-start | bytes 73736 | tf_op jit(solution)/shard_map/weights/ppermute | solution.py:245
  6.5 5.7 %collective-permute-start.1 = (bf16[19,768]{1,0:T(8,128)(2,1)S(1)}, bf16[19,768]{1,0:T(8,128)(2,1)S(1)}, u32[]{:S(2)}, u32[]{:S(2)}) collective-permute-start(bf16[19,768]{1,0:T(8,128)(2,1)S(1)} %pad_maximum_fusion.3), channel_id=1, source_target_pairs={{0,64},{32,96},{64,0},{96,32},{1,65},{33,97},{65,1},{97,33},{2,66}... | collective-permute-start | bytes 87560 | tf_op jit(solution)/shard_map/weights/ppermute | solution.py:242
  10.2 17.6 %collective-permute-start.5 = (bf16[256,1024]{1,0:T(8,128)(2,1)S(1)}, bf16[256,1024]{1,0:T(8,128)(2,1)}, u32[]{:S(2)}, u32[]{:S(2)}) collective-permute-start(bf16[256,1024]{1,0:T(8,128)(2,1)S(1)} %get-tuple-element.57), channel_id=1, source_target_pairs={{0,64},{64,0},{1,65},{65,1},{2,66},{66,2},{3,67},{67,3},{4,68},{68... | collective-permute-start | bytes 1572872 | tf_op jit(solution)/shard_map/tokens/ppermute | solution.py:15
  12.4 14.2 %copy-start.9 = (f32[8]{0:T(128)S(1)}, f32[8]{0:T(128)}, u32[]{:S(2)}) copy-start(f32[8]{0:T(128)} %param.9) | copy-start | bytes 100
  12.4 8.3 %collective-permute-start.3 = (bf16[4,1,16,768]{3,2,0,1:T(8,128)(2,1)S(1)}, bf16[4,1,16,768]{3,2,0,1:T(8,128)(2,1)S(1)}, u32[]{:S(2)}, u32[]{:S(2)}) collective-permute-start(bf16[4,1,16,768]{3,2,0,1:T(8,128)(2,1)S(1)} %bitcast.102), channel_id=1, source_target_pairs={{0,16},{16,0},{1,17},{17,1},{2,18},{18,2},{3,19},{19,3},{4,20},{20... | collective-permute-start | bytes 294920 | tf_op jit(solution)/shard_map/weights/ppermute | solution.py:15
  20.7 7.1 %collective-permute-start.4 = (bf16[8,16,768]{2,1,0:T(8,128)(2,1)S(1)}, bf16[8,16,768]{2,1,0:T(8,128)(2,1)S(1)}, u32[]{:S(2)}, u32[]{:S(2)}) collective-permute-start(bf16[8,16,768]{2,1,0:T(8,128)(2,1)S(1)} %bitcast.104), channel_id=1, source_target_pairs={{0,4},{4,0},{8,12},{12,8},{1,5},{5,1},{9,13},{13,9},{2,6},{6,2},{1... | collective-permute-start | bytes 589832 | tf_op jit(solution)/shard_map/weights/ppermute | solution.py:259
  22.3 10.9 %collective-permute-start.9 = (bf16[8,16,768]{2,1,0:T(8,128)(2,1)S(1)}, bf16[8,16,768]{2,1,0:T(8,128)(2,1)S(1)}, u32[]{:S(2)}, u32[]{:S(2)}) collective-permute-start(bf16[8,16,768]{2,1,0:T(8,128)(2,1)S(1)} %bitcast.105), channel_id=1, source_target_pairs={{0,12},{4,8},{8,4},{12,0},{1,13},{5,9},{9,5},{13,1},{2,14},{6,10},... | collective-permute-start | bytes 589832 | tf_op jit(solution)/shard_map/weights/ppermute | solution.py:259
  24.4 8.8 %collective-permute-start.8 = (bf16[8,16,768]{2,1,0:T(8,128)(2,1)S(1)}, bf16[8,16,768]{2,1,0:T(8,128)(2,1)S(1)}, u32[]{:S(2)}, u32[]{:S(2)}) collective-permute-start(bf16[8,16,768]{2,1,0:T(8,128)(2,1)S(1)} %bitcast.106), channel_id=1, source_target_pairs={{0,8},{4,12},{8,0},{12,4},{1,9},{5,13},{9,1},{13,5},{2,10},{6,14},... | collective-permute-start | bytes 589832 | tf_op jit(solution)/shard_map/weights/ppermute | solution.py:259
  25.0 14.8 %collective-permute-start.7 = (bf16[256,1024]{1,0:T(8,128)(2,1)}, bf16[256,1024]{1,0:T(8,128)(2,1)}, u32[]{:S(2)}, u32[]{:S(2)}) collective-permute-start(bf16[256,1024]{1,0:T(8,128)(2,1)} %get-tuple-element.56), channel_id=1, source_target_pairs={{0,64},{64,0},{1,65},{65,1},{2,66},{66,2},{3,67},{67,3},{4,68},{68... | collective-permute-start | bytes 1572872 | tf_op jit(solution)/shard_map/tokens/ppermute | solution.py:15
  27.9 10.8 %collective-permute-start.6 = (bf16[256,1024]{1,0:T(8,128)(2,1)}, bf16[256,1024]{1,0:T(8,128)(2,1)}, u32[]{:S(2)}, u32[]{:S(2)}) collective-permute-start(bf16[256,1024]{1,0:T(8,128)(2,1)} %collective-permute-done.5), channel_id=1, source_target_pairs={{0,1},{1,0},{2,3},{3,2},{4,5},{5,4},{6,7},{7,6},{8,9},{9,8},{10,11... | collective-permute-start | bytes 1572872 | tf_op jit(solution)/shard_map/weights/ppermute | solution.py:15
  33.3 1.1 copy-start.4
  33.4 7.5 %collective-permute-start.10 = (bf16[8,4,16,768]{3,2,1,0:T(8,128)(2,1)S(1)}, bf16[8,4,16,768]{3,2,1,0:T(8,128)(2,1)S(1)}, u32[]{:S(2)}, u32[]{:S(2)}) collective-permute-start(bf16[8,4,16,768]{3,2,1,0:T(8,128)(2,1)S(1)} %get-tuple-element.34), channel_id=1, source_target_pairs={{0,2},{2,0},{1,3},{3,1},{4,6},{6,4},{5,7},{7,5},{8,10},{10,8},{9,1... | collective-permute-start | bytes 2359304 | tf_op jit(solution)/shard_map/weights/ppermute | solution.py:15
  34.6 13.6 %collective-permute-start.11 = (bf16[768,256]{1,0:T(8,128)(2,1)S(1)}, bf16[768,256]{1,0:T(8,128)(2,1)S(1)}, u32[]{:S(2)}, u32[]{:S(2)}) collective-permute-start(bf16[768,256]{1,0:T(8,128)(2,1)S(1)} %get-tuple-element.61), channel_id=1, source_target_pairs={{0,64},{64,0},{1,65},{65,1},{2,66},{66,2},{3,67},{67,3},{4,68},{68... | collective-permute-start | bytes 1179656 | tf_op jit(solution)/shard_map/bias/ppermute | solution.py:15
  40.9 1.4 copy-start
  43.7 24.3 %collective-permute-start.12 = (bf16[8,4,16,768]{3,2,1,0:T(8,128)(2,1)S(1)}, bf16[8,4,16,768]{3,2,1,0:T(8,128)(2,1)S(1)}, u32[]{:S(2)}, u32[]{:S(2)}) collective-permute-start(bf16[8,4,16,768]{3,2,1,0:T(8,128)(2,1)S(1)} %get-tuple-element.34), channel_id=1, source_target_pairs={{0,64},{64,0},{1,65},{65,1},{2,66},{66,2},{3,67},{67,3},{4,68},{68... | collective-permute-start | bytes 2359304 | tf_op jit(solution)/shard_map/attention/ppermute | solution.py:15
  66.8 23.0 %collective-permute-start.13 = (bf16[768,384]{1,0:T(8,128)(2,1)S(1)}, bf16[768,384]{1,0:T(8,128)(2,1)S(1)}, u32[]{:S(2)}, u32[]{:S(2)}) collective-permute-start(bf16[768,384]{1,0:T(8,128)(2,1)S(1)} %get-tuple-element.36.refs_1_), channel_id=1, source_target_pairs={{0,64},{64,0},{1,65},{65,1},{2,66},{66,2},{3,67},{67,3},{4,68},{68... | collective-permute-start | bytes 1769480 | tf_op jit(solution)/shard_map/d_tokens/ppermute | solution.py:15
  68.0 21.2 %collective-permute-start.14 = (bf16[8,4,16,768]{3,2,1,0:T(8,128)(2,1)S(1)}, bf16[8,4,16,768]{3,2,1,0:T(8,128)(2,1)S(1)}, u32[]{:S(2)}, u32[]{:S(2)}) collective-permute-start(bf16[8,4,16,768]{3,2,1,0:T(8,128)(2,1)S(1)} %collective-permute-done.12), channel_id=1, source_target_pairs={{0,2},{2,0},{1,3},{3,1},{4,6},{6,4},{5,7},{7,5},{8,10},{10,8},{9,1... | collective-permute-start | bytes 2359304 | tf_op jit(solution)/shard_map/d_tokens/ppermute | solution.py:15
  86.6 8.9 %collective-permute-start.15 = (bf16[256,384]{1,0:T(8,128)(2,1)S(1)}, bf16[256,384]{1,0:T(8,128)(2,1)S(1)}, u32[]{:S(2)}, u32[]{:S(2)}) collective-permute-start(bf16[256,384]{1,0:T(8,128)(2,1)S(1)} %get-tuple-element.40), channel_id=1, source_target_pairs={{0,64},{64,0},{1,65},{65,1},{2,66},{66,2},{3,67},{67,3},{4,68},{68... | collective-permute-start | bytes 589832 | tf_op jit(solution)/shard_map/d_tokens/ppermute | solution.py:15
  96.0 8.0 %copy-start.1 = (bf16[256,1024]{1,0:T(8,128)(2,1)}, bf16[256,1024]{1,0:T(8,128)(2,1)S(1)}, u32[]{:S(2)}) copy-start(bf16[256,1024]{1,0:T(8,128)(2,1)S(1)} %fusion.12.mine_ref) | copy-start | bytes 1572868
  101.4 17.1 %collective-permute-start.16 = (f32[512,768]{1,0:T(8,128)S(1)}, f32[512,768]{1,0:T(8,128)S(1)}, u32[]{:S(2)}, u32[]{:S(2)}) collective-permute-start(f32[512,768]{1,0:T(8,128)S(1)} %get-tuple-element.45), channel_id=1, source_target_pairs={{0,2},{2,0},{1,3},{3,1},{4,6},{6,4},{5,7},{7,5},{8,10},{10,8},{9,1... | collective-permute-start | bytes 4718600 | tf_op jit(solution)/shard_map/d_weight/ppermute | solution.py:15
  101.5 13.0 %collective-permute-start.21 = (bf16[512,384]{1,0:T(8,128)(2,1)S(1)}, bf16[512,384]{1,0:T(8,128)(2,1)S(1)}, u32[]{:S(2)}, u32[]{:S(2)}) collective-permute-start(bf16[512,384]{1,0:T(8,128)(2,1)S(1)} %get-tuple-element.41), channel_id=1, source_target_pairs={{0,64},{64,0},{1,65},{65,1},{2,66},{66,2},{3,67},{67,3},{4,68},{68... | collective-permute-start | bytes 1179656 | tf_op jit(solution)/shard_map/d_tokens/ppermute | solution.py:15
  103.9 14.5 %collective-permute-start.17 = (bf16[256,1024]{1,0:T(8,128)(2,1)S(1)}, bf16[256,1024]{1,0:T(8,128)(2,1)S(1)}, u32[]{:S(2)}, u32[]{:S(2)}) collective-permute-start(bf16[256,1024]{1,0:T(8,128)(2,1)S(1)} %fusion.12.mine_ref), channel_id=1, source_target_pairs={{0,1},{1,0},{2,3},{3,2},{4,5},{5,4},{6,7},{7,6},{8,9},{9,8},{10,11... | collective-permute-start | bytes 1572872 | tf_op jit(solution)/shard_map/d_weight/ppermute | solution.py:15
  115.0 3.7 %copy-start.3 = (bf16[256,1024]{1,0:T(8,128)(2,1)}, bf16[256,1024]{1,0:T(8,128)(2,1)S(1)}, u32[]{:S(2)}) copy-start(bf16[256,1024]{1,0:T(8,128)(2,1)S(1)} %fusion.11.mine_ref) | copy-start | bytes 1572868
  115.0 16.7 %collective-permute-start.22 = (bf16[256,1024]{1,0:T(8,128)(2,1)S(1)}, bf16[256,1024]{1,0:T(8,128)(2,1)S(1)}, u32[]{:S(2)}, u32[]{:S(2)}) collective-permute-start(bf16[256,1024]{1,0:T(8,128)(2,1)S(1)} %fusion.11.mine_ref), channel_id=1, source_target_pairs={{0,1},{1,0},{2,3},{3,2},{4,5},{5,4},{6,7},{7,6},{8,9},{9,8},{10,11... | collective-permute-start | bytes 1572872 | tf_op jit(solution)/shard_map/d_weight/ppermute | solution.py:15
  118.5 0.8 copy-start.5
  119.3 8.4 %collective-permute-start.20 = (bf16[8,16,768]{2,1,0:T(8,128)(2,1)S(1)}, bf16[8,16,768]{2,1,0:T(8,128)(2,1)S(1)}, u32[]{:S(2)}, u32[]{:S(2)}) collective-permute-start(bf16[8,16,768]{2,1,0:T(8,128)(2,1)S(1)} %bitcast.115), channel_id=1, source_target_pairs={{0,12},{4,8},{8,4},{12,0},{1,13},{5,9},{9,5},{13,1},{2,14},{6,10},... | collective-permute-start | bytes 589832 | tf_op jit(solution)/shard_map/d_weight/ppermute | solution.py:306
  121.1 7.8 %collective-permute-start.18 = (bf16[8,16,768]{2,1,0:T(8,128)(2,1)S(1)}, bf16[8,16,768]{2,1,0:T(8,128)(2,1)S(1)}, u32[]{:S(2)}, u32[]{:S(2)}) collective-permute-start(bf16[8,16,768]{2,1,0:T(8,128)(2,1)S(1)} %bitcast.114), channel_id=1, source_target_pairs={{0,4},{4,0},{8,12},{12,8},{1,5},{5,1},{9,13},{13,9},{2,6},{6,2},{1... | collective-permute-start | bytes 589832 | tf_op jit(solution)/shard_map/d_weight/ppermute | solution.py:306
  122.1 9.5 %collective-permute-start.19 = (bf16[8,16,768]{2,1,0:T(8,128)(2,1)S(1)}, bf16[8,16,768]{2,1,0:T(8,128)(2,1)S(1)}, u32[]{:S(2)}, u32[]{:S(2)}) collective-permute-start(bf16[8,16,768]{2,1,0:T(8,128)(2,1)S(1)} %bitcast.113), channel_id=1, source_target_pairs={{0,8},{4,12},{8,0},{12,4},{1,9},{5,13},{9,1},{13,5},{2,10},{6,14},... | collective-permute-start | bytes 589832 | tf_op jit(solution)/shard_map/d_weight/ppermute | solution.py:306
  124.6 10.5 %copy-start.2 = (bf16[256,1024]{1,0:T(8,128)(2,1)}, bf16[256,1024]{1,0:T(8,128)(2,1)S(1)}, u32[]{:S(2)}) copy-start(bf16[256,1024]{1,0:T(8,128)(2,1)S(1)} %fusion.10.mine_ref) | copy-start | bytes 1572868
  131.7 4.2 %copy-start.6 = (bf16[256,1024]{1,0:T(8,128)(2,1)}, bf16[256,1024]{1,0:T(8,128)(2,1)S(1)}, u32[]{:S(2)}) copy-start(bf16[256,1024]{1,0:T(8,128)(2,1)S(1)} %collective-permute-done.22.theirs_ref) | copy-start | bytes 1572868
  131.7 7.2 %collective-permute-start.24 = (bf16[2,2,16,768]{3,2,1,0:T(8,128)(2,1)S(1)}, bf16[2,2,16,768]{3,2,1,0:T(8,128)(2,1)S(1)}, u32[]{:S(2)}, u32[]{:S(2)}) collective-permute-start(bf16[2,2,16,768]{3,2,1,0:T(8,128)(2,1)S(1)} %fusion.29), channel_id=1, source_target_pairs={{0,16},{16,0},{1,17},{17,1},{2,18},{18,2},{3,19},{19,3},{4,20},{20... | collective-permute-start | bytes 294920 | tf_op jit(solution)/shard_map/d_weight/ppermute | solution.py:15
  135.1 12.6 %collective-permute-start.23 = (bf16[256,1024]{1,0:T(8,128)(2,1)S(1)}, bf16[256,1024]{1,0:T(8,128)(2,1)S(1)}, u32[]{:S(2)}, u32[]{:S(2)}) collective-permute-start(bf16[256,1024]{1,0:T(8,128)(2,1)S(1)} %fusion.10.mine_ref), channel_id=1, source_target_pairs={{0,1},{1,0},{2,3},{3,2},{4,5},{5,4},{6,7},{7,6},{8,9},{9,8},{10,11... | collective-permute-start | bytes 1572872 | tf_op jit(solution)/shard_map/d_weight/ppermute | solution.py:15
  139.0 4.3 %collective-permute-start.25 = (f32[16,768]{1,0:T(8,128)S(1)}, f32[16,768]{1,0:T(8,128)S(1)}, u32[]{:S(2)}, u32[]{:S(2)}) collective-permute-start(f32[16,768]{1,0:T(8,128)S(1)} %select_bitcast_fusion.6), channel_id=1, source_target_pairs={{0,32},{32,0},{64,96},{96,64},{1,33},{33,1},{65,97},{97,65},{2,34}... | collective-permute-start | bytes 147464 | tf_op jit(solution)/shard_map/d_weight/ppermute | solution.py:321
  140.9 5.9 %collective-permute-start.27 = (f32[16,768]{1,0:T(8,128)S(1)}, f32[16,768]{1,0:T(8,128)S(1)}, u32[]{:S(2)}, u32[]{:S(2)}) collective-permute-start(f32[16,768]{1,0:T(8,128)S(1)} %get-tuple-element.78), channel_id=1, source_target_pairs={{0,96},{32,64},{64,32},{96,0},{1,97},{33,65},{65,33},{97,1},{2,98}... | collective-permute-start | bytes 147464 | tf_op jit(solution)/shard_map/d_weight/ppermute | solution.py:321
  141.0 5.8 %collective-permute-start.26 = (f32[16,768]{1,0:T(8,128)S(1)}, f32[16,768]{1,0:T(8,128)S(1)}, u32[]{:S(2)}, u32[]{:S(2)}) collective-permute-start(f32[16,768]{1,0:T(8,128)S(1)} %get-tuple-element.79), channel_id=1, source_target_pairs={{0,64},{32,96},{64,0},{96,32},{1,65},{33,97},{65,1},{97,33},{2,66}... | collective-permute-start | bytes 147464 | tf_op jit(solution)/shard_map/d_weight/ppermute | solution.py:320
  147.7 0.8 copy-start.7

commit v4 on v3

--- a/solution.py
+++ b/solution.py
@@ -295,11 +295,10 @@
 
     with jax.named_scope("d_weight"):
         far1 = jnp.concatenate(far1, 0)
-        far1, back0, mine[0] = lax.optimization_barrier((far1, back0, mine[0]))
+        far1, back0 = lax.optimization_barrier((far1, back0))
         keep, send = weight_terms(jnp.stack([core, x, head]), tokens, far_tokens, [near0, far0, near1, far1])
         other = swap(send, "c")
         theirs = [swap(mine[0], "h")]
-        other, theirs[0] = lax.optimization_barrier((other, theirs[0]))
         term = (keep + other).reshape(4, 8, 16, 768)
         total = term[0]
         for j in range(1, 4):
@@ -307,10 +306,11 @@
             total = total + piece.astype(F32)
         total = total.reshape(2, 2, 2, 16, 768)
         theirs.append(swap(mine[1], "h"))
-        total, theirs[1], mine[2] = lax.optimization_barrier((total, theirs[1], mine[2]))
+        total, theirs[0] = lax.optimization_barrier((total, theirs[0]))
         theirs.append(swap(mine[2], "h"))
         mine_w, their_w = pick(total, y_hi, 2)
         total = mine_w + swap(their_w.astype(BF), "yh").astype(F32)
+        total, theirs[1] = lax.optimization_barrier((total, theirs[1]))
         halves = []
         for a in range(2):
             part = total if a == 0 else total[::-1]

time: 151 us -> 144 us (0.954)
  waiting for transfers between devices: 35.6 us -> 27.8 us
    ppermute x2, waiting for transfers between devices: 3.52 us -> 0.01 us  [on_device(): lax.ppermute(their_w, ('zh', 'zl'), [(i, i ^ 2 * a + 1) for i in range(4)])]
    ppermute x3, waiting for transfers between devices: 6.96 us -> 4.15 us  [on_device(): lax.ppermute(term[j].astype(BF), 'x', [(i, i ^ j) for i in range(4)])]
  transfers between devices with their start and end apart: 28 -> 28, of which waited for: 12 -> 12; matrix products, arithmetic and copies ran while one was open for 13% -> 14% of each run, Pallas kernels for 28% -> 34%
where the time goes in v4:
time: 144 us; the launch traced here: 143 us
  Pallas kernels  49 us (34%)
  starting transfers between devices  40.9 us (28%)
  waiting for transfers between devices  27.8 us (19%)
  local copies, waits for them, and re-layouts  10.6 us (7%)
  other arithmetic  7.24 us (5%)
  matrix products  6.43 us (4%)
    pallas_call x2, Pallas kernels, attention(): pl.pallas_call(attention_kernel, grid=(total // TILE,), in_specs=[pl.Bloc...  37.2 us
    ppermute x16, starting transfers between devices, swap(): return lax.ppermute(value, axis, [(0, 1), (1, 0)])  21.6 us
    ppermute x16, waiting for transfers between devices, swap(): return lax.ppermute(value, axis, [(0, 1), (1, 0)])  17.8 us
    dot_general x6, matrix products, dot(): return lax.dot_general(a, b, (dims, ((), ())), preferred_element_type=F32)  6.43 us
    pallas_call x3, Pallas kernels, add_rows(): pl.pallas_call(add_kernel, grid=(1,), in_specs=[pl.BlockSpec((rows, width...  6.34 us
    ppermute x3, waiting for transfers between devices, on_device(): lax.ppermute(w, 'x', [(i, i ^ j) for i in range(4)])  5.84 us
    pallas_call x1, Pallas kernels, weight_terms(): pl.pallas_call(weight_kernel, grid=(width // tile,), in_specs=[pl.BlockSp...  5.39 us
    log x1, other arithmetic, on_device(): logd = jnp.log((1 + jnp.abs(pos[:, None] - pos[None, :])).astype(F32))  5.01 us
  transfers between devices with their start and end apart: 28, of which 12 were waited for; matrix products, arithmetic and copies ran while one was open for 14% of the time, Pallas kernels for 34%

profile of v4, /device:TPU:0, one launch (start us, length us, event | category | flops | bytes accessed | tf_op | source)
XLA Modules:
  0.0 143.1 jit_solution(2086163736616439627)
XLA Ops:
  0.6 0.8 reshape.96
  1.6 4.2 %collective-permute-start.2 = (bf16[16,768]{1,0:T(8,128)(2,1)S(1)}, bf16[16,768]{1,0:T(8,128)(2,1)S(1)}, u32[]{:S(2)}, u32[]{:S(2)}) collective-permute-start(bf16[16,768]{1,0:T(8,128)(2,1)S(1)} %get-tuple-element.76), channel_id=1, source_target_pairs={{0,96},{32,64},{64,32},{96,0},{1,97},{33,65},{65,33},{97,1},{2,98}... | collective-permute-start | bytes 73736 | tf_op jit(solution)/shard_map/weights/ppermute | solution.py:247
  6.5 1.6 %collective-permute-start.1 = (bf16[19,768]{1,0:T(8,128)(2,1)S(1)}, bf16[19,768]{1,0:T(8,128)(2,1)S(1)}, u32[]{:S(2)}, u32[]{:S(2)}) collective-permute-start(bf16[19,768]{1,0:T(8,128)(2,1)S(1)} %pad_maximum_fusion.2), channel_id=1, source_target_pairs={{0,64},{32,96},{64,0},{96,32},{1,65},{33,97},{65,1},{97,33},{2,66}... | collective-permute-start | bytes 87560 | tf_op jit(solution)/shard_map/weights/ppermute | solution.py:242
  8.2 2.1 %fusion.35 = (bf16[256,1024]{1,0:T(8,128)(2,1)}, bf16[256,1024]{1,0:T(8,128)(2,1)S(1)}) fusion(bf16[768,1024]{1,0:T(8,128)(2,1)} %near_ref.1, s32[]{:T(128)S(6)} %select_n.238), kind=kLoop, calls=%fused_computation.89 | loop fusion | bytes 2097156 | tf_op jit(solution)/shard_map/tokens/slice | solution.py:235
  10.2 2.0 %collective-permute-start.5 = (bf16[256,1024]{1,0:T(8,128)(2,1)S(1)}, bf16[256,1024]{1,0:T(8,128)(2,1)}, u32[]{:S(2)}, u32[]{:S(2)}) collective-permute-start(bf16[256,1024]{1,0:T(8,128)(2,1)S(1)} %get-tuple-element.53), channel_id=1, source_target_pairs={{0,64},{64,0},{1,65},{65,1},{2,66},{66,2},{3,67},{67,3},{4,68},{68... | collective-permute-start | bytes 1572872 | tf_op jit(solution)/shard_map/tokens/ppermute | solution.py:15
  12.4 3.3 %collective-permute-start.3 = (bf16[4,1,16,768]{3,2,1,0:T(8,128)(2,1)S(1)}, bf16[4,1,16,768]{3,2,1,0:T(8,128)(2,1)S(1)}, u32[]{:S(2)}, u32[]{:S(2)}) collective-permute-start(bf16[4,1,16,768]{3,2,1,0:T(8,128)(2,1)S(1)} %maximum_bitcast_fusion), channel_id=1, source_target_pairs={{0,16},{16,0},{1,17},{17,1},{2,18},{18,2},{3,19},{19,3},{4,20},{20... | collective-permute-start | bytes 294920 | tf_op jit(solution)/shard_map/weights/ppermute | solution.py:15
  15.7 5.0 %convert_log_fusion.logd_ref = f32[1536,1536]{1,0:T(8,128)} fusion(s32[1536]{0:T(1024)S(1)} %pad_add_fusion), kind=kLoop, calls=%fused_computation | loop fusion | flops 9437184 | bytes 9443328 | tf_op jit(solution)/shard_map/weights/log | solution.py:252
  20.7 1.6 %collective-permute-start.4 = (bf16[8,16,768]{2,1,0:T(8,128)(2,1)S(1)}, bf16[8,16,768]{2,1,0:T(8,128)(2,1)S(1)}, u32[]{:S(2)}, u32[]{:S(2)}) collective-permute-start(bf16[8,16,768]{2,1,0:T(8,128)(2,1)S(1)} %bitcast.93), channel_id=1, source_target_pairs={{0,4},{4,0},{8,12},{12,8},{1,5},{5,1},{9,13},{13,9},{2,6},{6,2},{1... | collective-permute-start | bytes 589832 | tf_op jit(solution)/shard_map/weights/ppermute | solution.py:259
  22.3 2.1 %collective-permute-start.7 = (bf16[8,16,768]{2,1,0:T(8,128)(2,1)S(1)}, bf16[8,16,768]{2,1,0:T(8,128)(2,1)S(1)}, u32[]{:S(2)}, u32[]{:S(2)}) collective-permute-start(bf16[8,16,768]{2,1,0:T(8,128)(2,1)S(1)} %bitcast.94), channel_id=1, source_target_pairs={{0,12},{4,8},{8,4},{12,0},{1,13},{5,9},{9,5},{13,1},{2,14},{6,10},... | collective-permute-start | bytes 589832 | tf_op jit(solution)/shard_map/weights/ppermute | solution.py:259
  25.0 1.6 %collective-permute-start.10 = (bf16[256,1024]{1,0:T(8,128)(2,1)}, bf16[256,1024]{1,0:T(8,128)(2,1)}, u32[]{:S(2)}, u32[]{:S(2)}) collective-permute-start(bf16[256,1024]{1,0:T(8,128)(2,1)} %get-tuple-element.52), channel_id=1, source_target_pairs={{0,64},{64,0},{1,65},{65,1},{2,66},{66,2},{3,67},{67,3},{4,68},{68... | collective-permute-start | bytes 1572872 | tf_op jit(solution)/shard_map/tokens/ppermute | solution.py:15
  26.6 1.2 collective-permute-done.4
  28.5 4.6 %collective-permute-done.7 = bf16[8,16,768]{2,1,0:T(8,128)(2,1)S(1)} collective-permute-done((bf16[8,16,768]{2,1,0:T(8,128)(2,1)S(1)}, bf16[8,16,768]{2,1,0:T(8,128)(2,1)S(1)}, u32[]{:S(2)}, u32[]{:S(2)}) %collective-permute-start.7) | collective-permute-done | bytes 196640 | tf_op jit(solution)/shard_map/weights/ppermute | solution.py:259
  34.5 1.7 %collective-permute-start.11 = (bf16[768,256]{1,0:T(8,128)(2,1)S(1)}, bf16[768,256]{1,0:T(8,128)(2,1)S(1)}, u32[]{:S(2)}, u32[]{:S(2)}) collective-permute-start(bf16[768,256]{1,0:T(8,128)(2,1)S(1)} %get-tuple-element.57), channel_id=1, source_target_pairs={{0,64},{64,0},{1,65},{65,1},{2,66},{66,2},{3,67},{67,3},{4,68},{68... | collective-permute-start | bytes 1179656 | tf_op jit(solution)/shard_map/bias/ppermute | solution.py:15
  36.2 1.1 constant_dynamic-update-slice_fusion.2
  37.3 1.4 collective-permute-done.9
  38.7 1.1 constant_dynamic-update-slice_fusion.1
  39.8 1.1 constant_dynamic-update-slice_fusion.far_ref
  41.3 1.2 copy-done
  42.5 1.4 fusion.9.qo.ko.vo
  44.0 2.2 %collective-permute-start.12 = (bf16[8,4,16,768]{3,2,0,1:T(8,128)(2,1)S(1)}, bf16[8,4,16,768]{3,2,0,1:T(8,128)(2,1)S(1)}, u32[]{:S(2)}, u32[]{:S(2)}) collective-permute-start(bf16[8,4,16,768]{3,2,0,1:T(8,128)(2,1)S(1)} %get-tuple-element.32), channel_id=1, source_target_pairs={{0,64},{64,0},{1,65},{65,1},{2,66},{66,2},{3,67},{67,3},{4,68},{68... | collective-permute-start | bytes 2359304 | tf_op jit(solution)/shard_map/attention/ppermute | solution.py:15
  46.2 1.4 convolution_convert_fusion.1.qf.kf.vf
  47.8 18.6 %attention.2 = (bf16[768,384]{1,0:T(8,128)(2,1)S(1)}, bf16[768,384]{1,0:T(8,128)(2,1)S(1)}) custom-call(s32[1]{0:T(128)} %bitcast.8.place_ref, f32[2]{0:T(128)S(1)} %get-tuple-element.85.slopes_ref, bf16[768,768]{1,0:T(8,128)(2,1)S(1)} %fusion.9.qo.ko.vo, bf16[768,768]{1,0:T(8,128)(2,1)S(1)} %convolution_convert_fusion.1.qf.kf.vf, ...), custom_call_target="tpu_custom_call" | custom-call | flops 12079595520 | bytes 9437184 | tf_op jit(solution)/shard_map/attention/pallas_call | solution.py:126
  66.4 1.4 %collective-permute-start.13 = (bf16[768,384]{1,0:T(8,128)(2,1)S(1)}, bf16[768,384]{1,0:T(8,128)(2,1)S(1)}, u32[]{:S(2)}, u32[]{:S(2)}) collective-permute-start(bf16[768,384]{1,0:T(8,128)(2,1)S(1)} %get-tuple-element.37.refs_1_), channel_id=1, source_target_pairs={{0,64},{64,0},{1,65},{65,1},{2,66},{66,2},{3,67},{67,3},{4,68},{68... | collective-permute-start | bytes 1769480 | tf_op jit(solution)/shard_map/d_tokens/ppermute | solution.py:15
  67.9 18.6 %attention.3 = (bf16[768,384]{1,0:T(8,128)(2,1)S(1)}, bf16[256,384]{1,0:T(8,128)(2,1)S(1)}, bf16[512,384]{1,0:T(8,128)(2,1)S(1)}) custom-call(s32[1]{0:T(128)} %bitcast.8.place_ref, f32[2]{0:T(128)S(1)} %get-tuple-element.84.slopes_ref, bf16[768,768]{1,0:T(8,128)(2,1)S(1)} %fusion.9.qo.ko.vo, bf16[768,768]{1,0:T(8,128)(2,1)S(1)} %convolution_convert_fusion.1.qf.kf.vf, ...), custom_call_target="tpu_custom_call" | custom-call | flops 12079595520 | bytes 9437184 | tf_op jit(solution)/shard_map/attention/pallas_call | solution.py:126
  86.6 5.4 %d_weight.1 = (f32[512,768]{1,0:T(8,128)S(1)}, f32[512,768]{1,0:T(8,128)S(1)}) custom-call(s32[3]{0:T(128)S(1)} %pad_add_fusion.1.place_ref, bf16[768,1024]{1,0:T(8,128)(2,1)S(1)} %copy-done, bf16[768,1024]{1,0:T(8,128)(2,1)S(1)} %constant_dynamic-update-slice_fusion.far_ref, bf16[768,384]{1,0:T(8,128)(2,1)S(1)} %get-tuple-element.33.refs_0_, ...), custom_call_target="tpu_custom_call" | custom-call | flops 1000 | bytes 1000 | tf_op jit(solution)/shard_map/d_weight/pallas_call | solution.py:195
  92.6 2.2 %collective-permute-start.21 = (bf16[256,384]{1,0:T(8,128)(2,1)S(1)}, bf16[256,384]{1,0:T(8,128)(2,1)S(1)}, u32[]{:S(2)}, u32[]{:S(2)}) collective-permute-start(bf16[256,384]{1,0:T(8,128)(2,1)S(1)} %get-tuple-element.40), channel_id=1, source_target_pairs={{0,64},{64,0},{1,65},{65,1},{2,66},{66,2},{3,67},{67,3},{4,68},{68... | collective-permute-start | bytes 589832 | tf_op jit(solution)/shard_map/d_tokens/ppermute | solution.py:15
  94.7 1.4 collective-permute-start.15
  96.7 2.2 %fusion = f32[768,1024]{1,0:T(8,128)S(1)} fusion(bf16[1024,384]{1,0:T(8,128)(2,1)S(1)} %slice.169, bf16[1024,768]{1,0:T(8,128)(2,1)S(1)} %bitcast.91, bf16[768,384]{1,0:T(8,128)(2,1)S(1)} %collective-permute-done.13, bf16[768,384]{1,0:T(8,128)(2,1)S(1)} %get-tuple-element.36.refs_2_, bf16[768,384]{1,0:T(8,128)(2,1)S(1)} %get-tuple-element.33.refs_0_), kind=kOutput, calls=%fused_computation.1 | convolution fusion | flops 1821966336 | bytes 7274496 | tf_op jit(solution)/shard_map/d_tokens/dot_general | solution.py:19
  98.9 2.9 %collective-permute-done.21 = bf16[256,384]{1,0:T(8,128)(2,1)S(1)} collective-permute-done((bf16[256,384]{1,0:T(8,128)(2,1)S(1)}, bf16[256,384]{1,0:T(8,128)(2,1)S(1)}, u32[]{:S(2)}, u32[]{:S(2)}) %collective-permute-start.21) | collective-permute-done | bytes 196640 | tf_op jit(solution)/shard_map/d_tokens/ppermute | solution.py:15
  102.3 0.8 collective-permute-start.22
  103.3 2.7 %collective-permute-start.20 = (bf16[8,16,768]{2,1,0:T(8,128)(2,1)S(1)}, bf16[8,16,768]{2,1,0:T(8,128)(2,1)S(1)}, u32[]{:S(2)}, u32[]{:S(2)}) collective-permute-start(bf16[8,16,768]{2,1,0:T(8,128)(2,1)S(1)} %bitcast.103), channel_id=1, source_target_pairs={{0,12},{4,8},{8,4},{12,0},{1,13},{5,9},{9,5},{13,1},{2,14},{6,10},... | collective-permute-start | bytes 589832 | tf_op jit(solution)/shard_map/d_weight/ppermute | solution.py:305
  106.0 0.9 collective-permute-start.18
  107.0 1.1 collective-permute-start.19
  108.1 1.3 collective-permute-done.15
  109.9 1.0 collective-permute-start.24
  110.9 1.5 %collective-permute-done.20 = bf16[8,16,768]{2,1,0:T(8,128)(2,1)S(1)} collective-permute-done((bf16[8,16,768]{2,1,0:T(8,128)(2,1)S(1)}, bf16[8,16,768]{2,1,0:T(8,128)(2,1)S(1)}, u32[]{:S(2)}, u32[]{:S(2)}) %collective-permute-start.20) | collective-permute-done | bytes 196640 | tf_op jit(solution)/shard_map/d_weight/ppermute | solution.py:305
  113.0 2.1 %collective-permute-done.19 = bf16[8,16,768]{2,1,0:T(8,128)(2,1)S(1)} collective-permute-done((bf16[8,16,768]{2,1,0:T(8,128)(2,1)S(1)}, bf16[8,16,768]{2,1,0:T(8,128)(2,1)S(1)}, u32[]{:S(2)}, u32[]{:S(2)}) %collective-permute-start.19) | collective-permute-done | bytes 196640 | tf_op jit(solution)/shard_map/d_weight/ppermute | solution.py:305
  115.2 1.9 %collective-permute-done.22.theirs_ref = bf16[256,1024]{1,0:T(8,128)(2,1)S(1)} collective-permute-done((bf16[256,1024]{1,0:T(8,128)(2,1)S(1)}, bf16[256,1024]{1,0:T(8,128)(2,1)S(1)}, u32[]{:S(2)}, u32[]{:S(2)}) %collective-permute-start.22) | collective-permute-done | bytes 524320 | tf_op jit(solution)/shard_map/d_weight/ppermute | solution.py:15
  117.1 2.1 %collective-permute-start.23 = (bf16[2,2,16,768]{3,2,1,0:T(8,128)(2,1)S(1)}, bf16[2,2,16,768]{3,2,1,0:T(8,128)(2,1)S(1)}, u32[]{:S(2)}, u32[]{:S(2)}) collective-permute-start(bf16[2,2,16,768]{3,2,1,0:T(8,128)(2,1)S(1)} %fusion.29), channel_id=1, source_target_pairs={{0,16},{16,0},{1,17},{17,1},{2,18},{18,2},{3,19},{19,3},{4,20},{20... | collective-permute-start | bytes 294920 | tf_op jit(solution)/shard_map/d_weight/ppermute | solution.py:15
  120.4 2.1 %d_tokens.3.refs_0_ = bf16[768,1024]{1,0:T(8,128)(2,1)} custom-call(bf16[256,1024]{1,0:T(8,128)(2,1)} %copy-done.1, bf16[256,1024]{1,0:T(8,128)(2,1)} %copy-done.5), custom_call_target="tpu_custom_call" | custom-call | flops 1000 | bytes 1000 | tf_op jit(solution)/shard_map/d_tokens/pallas_call | solution.py:152
  122.6 9.1 %collective-permute-done.23 = bf16[2,2,16,768]{3,2,1,0:T(8,128)(2,1)S(1)} collective-permute-done((bf16[2,2,16,768]{3,2,1,0:T(8,128)(2,1)S(1)}, bf16[2,2,16,768]{3,2,1,0:T(8,128)(2,1)S(1)}, u32[]{:S(2)}, u32[]{:S(2)}) %collective-permute-start.23) | collective-permute-done | bytes 98336 | tf_op jit(solution)/shard_map/d_weight/ppermute | solution.py:15
  131.8 0.9 collective-permute-start.25
  132.7 1.9 %collective-permute-start.27 = (f32[16,768]{1,0:T(8,128)S(1)}, f32[16,768]{1,0:T(8,128)S(1)}, u32[]{:S(2)}, u32[]{:S(2)}) collective-permute-start(f32[16,768]{1,0:T(8,128)S(1)} %get-tuple-element.74), channel_id=1, source_target_pairs={{0,96},{32,64},{64,32},{96,0},{1,97},{33,65},{65,33},{97,1},{2,98}... | collective-permute-start | bytes 147464 | tf_op jit(solution)/shard_map/d_weight/ppermute | solution.py:321
  134.6 1.5 %collective-permute-start.26 = (f32[16,768]{1,0:T(8,128)S(1)}, f32[16,768]{1,0:T(8,128)S(1)}, u32[]{:S(2)}, u32[]{:S(2)}) collective-permute-start(f32[16,768]{1,0:T(8,128)S(1)} %get-tuple-element.75), channel_id=1, source_target_pairs={{0,64},{32,96},{64,0},{96,32},{1,65},{33,97},{65,1},{97,33},{2,66}... | collective-permute-start | bytes 147464 | tf_op jit(solution)/shard_map/d_weight/ppermute | solution.py:320
  136.2 2.1 %d_tokens.4.refs_0_ = bf16[768,1024]{1,0:T(8,128)(2,1)} custom-call(bf16[256,1024]{1,0:T(8,128)(2,1)} %copy-done.2, bf16[256,1024]{1,0:T(8,128)(2,1)} %copy-done.6, bf16[768,1024]{1,0:T(8,128)(2,1)} %d_tokens.3.refs_0_), custom_call_target="tpu_custom_call", output_to_operand_aliasing={{}: (2, {})} | custom-call | flops 1000 | bytes 1000 | tf_op jit(solution)/shard_map/d_tokens/pallas_call | solution.py:152
  138.3 0.9 collective-permute-done.16.theirs_ref
  139.2 0.8 copy-done.7
  140.0 2.1 %d_tokens.5 = bf16[768,1024]{1,0:T(8,128)(2,1)} custom-call(bf16[256,1024]{1,0:T(8,128)(2,1)} %copy-done.3, bf16[256,1024]{1,0:T(8,128)(2,1)} %copy-done.7, bf16[768,1024]{1,0:T(8,128)(2,1)} %d_tokens.4.refs_0_), custom_call_target="tpu_custom_call", output_to_operand_aliasing={{}: (2, {})} | custom-call | flops 1000 | bytes 1000 | tf_op jit(solution)/shard_map/d_tokens/pallas_call | solution.py:152
  (91 shorter events, 9.6 us)
Async XLA Ops:
  0.6 11.7 %copy-start.8 = (s32[768]{0:T(1024)S(1)}, s32[768]{0:T(1024)}, u32[]{:S(2)}) copy-start(s32[768]{0:T(1024)} %param.8) | copy-start | bytes 9220
  1.6 10.7 %collective-permute-start.2 = (bf16[16,768]{1,0:T(8,128)(2,1)S(1)}, bf16[16,768]{1,0:T(8,128)(2,1)S(1)}, u32[]{:S(2)}, u32[]{:S(2)}) collective-permute-start(bf16[16,768]{1,0:T(8,128)(2,1)S(1)} %get-tuple-element.76), channel_id=1, source_target_pairs={{0,96},{32,64},{64,32},{96,0},{1,97},{33,65},{65,33},{97,1},{2,98}... | collective-permute-start | bytes 73736 | tf_op jit(solution)/shard_map/weights/ppermute | solution.py:247
  5.8 6.5 %collective-permute-start = (bf16[16,768]{1,0:T(8,128)(2,1)S(1)}, bf16[16,768]{1,0:T(8,128)(2,1)S(1)}, u32[]{:S(2)}, u32[]{:S(2)}) collective-permute-start(bf16[16,768]{1,0:T(8,128)(2,1)S(1)} %get-tuple-element.77), channel_id=1, source_target_pairs={{0,32},{32,0},{64,96},{96,64},{1,33},{33,1},{65,97},{97,65},{2,34}... | collective-permute-start | bytes 73736 | tf_op jit(solution)/shard_map/weights/ppermute | solution.py:245
  6.5 5.7 %collective-permute-start.1 = (bf16[19,768]{1,0:T(8,128)(2,1)S(1)}, bf16[19,768]{1,0:T(8,128)(2,1)S(1)}, u32[]{:S(2)}, u32[]{:S(2)}) collective-permute-start(bf16[19,768]{1,0:T(8,128)(2,1)S(1)} %pad_maximum_fusion.2), channel_id=1, source_target_pairs={{0,64},{32,96},{64,0},{96,32},{1,65},{33,97},{65,1},{97,33},{2,66}... | collective-permute-start | bytes 87560 | tf_op jit(solution)/shard_map/weights/ppermute | solution.py:242
  10.2 17.6 %collective-permute-start.5 = (bf16[256,1024]{1,0:T(8,128)(2,1)S(1)}, bf16[256,1024]{1,0:T(8,128)(2,1)}, u32[]{:S(2)}, u32[]{:S(2)}) collective-permute-start(bf16[256,1024]{1,0:T(8,128)(2,1)S(1)} %get-tuple-element.53), channel_id=1, source_target_pairs={{0,64},{64,0},{1,65},{65,1},{2,66},{66,2},{3,67},{67,3},{4,68},{68... | collective-permute-start | bytes 1572872 | tf_op jit(solution)/shard_map/tokens/ppermute | solution.py:15
  12.4 14.2 %copy-start.9 = (f32[8]{0:T(128)S(1)}, f32[8]{0:T(128)}, u32[]{:S(2)}) copy-start(f32[8]{0:T(128)} %param.9) | copy-start | bytes 100
  12.4 8.3 %collective-permute-start.3 = (bf16[4,1,16,768]{3,2,1,0:T(8,128)(2,1)S(1)}, bf16[4,1,16,768]{3,2,1,0:T(8,128)(2,1)S(1)}, u32[]{:S(2)}, u32[]{:S(2)}) collective-permute-start(bf16[4,1,16,768]{3,2,1,0:T(8,128)(2,1)S(1)} %maximum_bitcast_fusion), channel_id=1, source_target_pairs={{0,16},{16,0},{1,17},{17,1},{2,18},{18,2},{3,19},{19,3},{4,20},{20... | collective-permute-start | bytes 294920 | tf_op jit(solution)/shard_map/weights/ppermute | solution.py:15
  20.7 7.1 %collective-permute-start.4 = (bf16[8,16,768]{2,1,0:T(8,128)(2,1)S(1)}, bf16[8,16,768]{2,1,0:T(8,128)(2,1)S(1)}, u32[]{:S(2)}, u32[]{:S(2)}) collective-permute-start(bf16[8,16,768]{2,1,0:T(8,128)(2,1)S(1)} %bitcast.93), channel_id=1, source_target_pairs={{0,4},{4,0},{8,12},{12,8},{1,5},{5,1},{9,13},{13,9},{2,6},{6,2},{1... | collective-permute-start | bytes 589832 | tf_op jit(solution)/shard_map/weights/ppermute | solution.py:259
  22.3 10.9 %collective-permute-start.7 = (bf16[8,16,768]{2,1,0:T(8,128)(2,1)S(1)}, bf16[8,16,768]{2,1,0:T(8,128)(2,1)S(1)}, u32[]{:S(2)}, u32[]{:S(2)}) collective-permute-start(bf16[8,16,768]{2,1,0:T(8,128)(2,1)S(1)} %bitcast.94), channel_id=1, source_target_pairs={{0,12},{4,8},{8,4},{12,0},{1,13},{5,9},{9,5},{13,1},{2,14},{6,10},... | collective-permute-start | bytes 589832 | tf_op jit(solution)/shard_map/weights/ppermute | solution.py:259
  24.4 8.8 %collective-permute-start.6 = (bf16[8,16,768]{2,1,0:T(8,128)(2,1)S(1)}, bf16[8,16,768]{2,1,0:T(8,128)(2,1)S(1)}, u32[]{:S(2)}, u32[]{:S(2)}) collective-permute-start(bf16[8,16,768]{2,1,0:T(8,128)(2,1)S(1)} %bitcast.95), channel_id=1, source_target_pairs={{0,8},{4,12},{8,0},{12,4},{1,9},{5,13},{9,1},{13,5},{2,10},{6,14},... | collective-permute-start | bytes 589832 | tf_op jit(solution)/shard_map/weights/ppermute | solution.py:259
  25.0 14.8 %collective-permute-start.10 = (bf16[256,1024]{1,0:T(8,128)(2,1)}, bf16[256,1024]{1,0:T(8,128)(2,1)}, u32[]{:S(2)}, u32[]{:S(2)}) collective-permute-start(bf16[256,1024]{1,0:T(8,128)(2,1)} %get-tuple-element.52), channel_id=1, source_target_pairs={{0,64},{64,0},{1,65},{65,1},{2,66},{66,2},{3,67},{67,3},{4,68},{68... | collective-permute-start | bytes 1572872 | tf_op jit(solution)/shard_map/tokens/ppermute | solution.py:15
  27.9 10.8 %collective-permute-start.9 = (bf16[256,1024]{1,0:T(8,128)(2,1)}, bf16[256,1024]{1,0:T(8,128)(2,1)}, u32[]{:S(2)}, u32[]{:S(2)}) collective-permute-start(bf16[256,1024]{1,0:T(8,128)(2,1)} %collective-permute-done.5), channel_id=1, source_target_pairs={{0,1},{1,0},{2,3},{3,2},{4,5},{5,4},{6,7},{7,6},{8,9},{9,8},{10,11... | collective-permute-start | bytes 1572872 | tf_op jit(solution)/shard_map/weights/ppermute | solution.py:15
  33.2 1.1 copy-start.4
  33.4 7.5 %collective-permute-start.8 = (bf16[8,4,16,768]{3,2,0,1:T(8,128)(2,1)S(1)}, bf16[8,4,16,768]{3,2,0,1:T(8,128)(2,1)S(1)}, u32[]{:S(2)}, u32[]{:S(2)}) collective-permute-start(bf16[8,4,16,768]{3,2,0,1:T(8,128)(2,1)S(1)} %get-tuple-element.32), channel_id=1, source_target_pairs={{0,2},{2,0},{1,3},{3,1},{4,6},{6,4},{5,7},{7,5},{8,10},{10,8},{9,1... | collective-permute-start | bytes 2359304 | tf_op jit(solution)/shard_map/weights/ppermute | solution.py:15
  34.5 13.3 %collective-permute-start.11 = (bf16[768,256]{1,0:T(8,128)(2,1)S(1)}, bf16[768,256]{1,0:T(8,128)(2,1)S(1)}, u32[]{:S(2)}, u32[]{:S(2)}) collective-permute-start(bf16[768,256]{1,0:T(8,128)(2,1)S(1)} %get-tuple-element.57), channel_id=1, source_target_pairs={{0,64},{64,0},{1,65},{65,1},{2,66},{66,2},{3,67},{67,3},{4,68},{68... | collective-permute-start | bytes 1179656 | tf_op jit(solution)/shard_map/bias/ppermute | solution.py:15
  41.1 1.4 copy-start
  44.0 23.9 %collective-permute-start.12 = (bf16[8,4,16,768]{3,2,0,1:T(8,128)(2,1)S(1)}, bf16[8,4,16,768]{3,2,0,1:T(8,128)(2,1)S(1)}, u32[]{:S(2)}, u32[]{:S(2)}) collective-permute-start(bf16[8,4,16,768]{3,2,0,1:T(8,128)(2,1)S(1)} %get-tuple-element.32), channel_id=1, source_target_pairs={{0,64},{64,0},{1,65},{65,1},{2,66},{66,2},{3,67},{67,3},{4,68},{68... | collective-permute-start | bytes 2359304 | tf_op jit(solution)/shard_map/attention/ppermute | solution.py:15
  66.4 20.2 %collective-permute-start.13 = (bf16[768,384]{1,0:T(8,128)(2,1)S(1)}, bf16[768,384]{1,0:T(8,128)(2,1)S(1)}, u32[]{:S(2)}, u32[]{:S(2)}) collective-permute-start(bf16[768,384]{1,0:T(8,128)(2,1)S(1)} %get-tuple-element.37.refs_1_), channel_id=1, source_target_pairs={{0,64},{64,0},{1,65},{65,1},{2,66},{66,2},{3,67},{67,3},{4,68},{68... | collective-permute-start | bytes 1769480 | tf_op jit(solution)/shard_map/d_tokens/ppermute | solution.py:15
  67.9 28.2 %collective-permute-start.14 = (bf16[8,4,16,768]{3,2,0,1:T(8,128)(2,1)S(1)}, bf16[8,4,16,768]{3,2,0,1:T(8,128)(2,1)S(1)}, u32[]{:S(2)}, u32[]{:S(2)}) collective-permute-start(bf16[8,4,16,768]{3,2,0,1:T(8,128)(2,1)S(1)} %collective-permute-done.12), channel_id=1, source_target_pairs={{0,2},{2,0},{1,3},{3,1},{4,6},{6,4},{5,7},{7,5},{8,10},{10,8},{9,1... | collective-permute-start | bytes 2359304 | tf_op jit(solution)/shard_map/d_tokens/ppermute | solution.py:15
  92.0 11.1 %collective-permute-start.17 = (f32[512,768]{1,0:T(8,128)S(1)}, f32[512,768]{1,0:T(8,128)S(1)}, u32[]{:S(2)}, u32[]{:S(2)}) collective-permute-start(f32[512,768]{1,0:T(8,128)S(1)} %get-tuple-element.43), channel_id=1, source_target_pairs={{0,2},{2,0},{1,3},{3,1},{4,6},{6,4},{5,7},{7,5},{8,10},{10,8},{9,1... | collective-permute-start | bytes 4718600 | tf_op jit(solution)/shard_map/d_weight/ppermute | solution.py:15
  92.6 9.3 %collective-permute-start.21 = (bf16[256,384]{1,0:T(8,128)(2,1)S(1)}, bf16[256,384]{1,0:T(8,128)(2,1)S(1)}, u32[]{:S(2)}, u32[]{:S(2)}) collective-permute-start(bf16[256,384]{1,0:T(8,128)(2,1)S(1)} %get-tuple-element.40), channel_id=1, source_target_pairs={{0,64},{64,0},{1,65},{65,1},{2,66},{66,2},{3,67},{67,3},{4,68},{68... | collective-permute-start | bytes 589832 | tf_op jit(solution)/shard_map/d_tokens/ppermute | solution.py:15
  94.7 14.7 %collective-permute-start.15 = (bf16[512,384]{1,0:T(8,128)(2,1)S(1)}, bf16[512,384]{1,0:T(8,128)(2,1)S(1)}, u32[]{:S(2)}, u32[]{:S(2)}) collective-permute-start(bf16[512,384]{1,0:T(8,128)(2,1)S(1)} %get-tuple-element.39), channel_id=1, source_target_pairs={{0,64},{64,0},{1,65},{65,1},{2,66},{66,2},{3,67},{67,3},{4,68},{68... | collective-permute-start | bytes 1179656 | tf_op jit(solution)/shard_map/d_tokens/ppermute | solution.py:15
  102.3 1.0 copy-start.1
  102.3 14.8 %collective-permute-start.22 = (bf16[256,1024]{1,0:T(8,128)(2,1)S(1)}, bf16[256,1024]{1,0:T(8,128)(2,1)S(1)}, u32[]{:S(2)}, u32[]{:S(2)}) collective-permute-start(bf16[256,1024]{1,0:T(8,128)(2,1)S(1)} %fusion.10.mine_ref), channel_id=1, source_target_pairs={{0,1},{1,0},{2,3},{3,2},{4,5},{5,4},{6,7},{7,6},{8,9},{9,8},{10,11... | collective-permute-start | bytes 1572872 | tf_op jit(solution)/shard_map/d_weight/ppermute | solution.py:15
  103.3 9.1 %collective-permute-start.20 = (bf16[8,16,768]{2,1,0:T(8,128)(2,1)S(1)}, bf16[8,16,768]{2,1,0:T(8,128)(2,1)S(1)}, u32[]{:S(2)}, u32[]{:S(2)}) collective-permute-start(bf16[8,16,768]{2,1,0:T(8,128)(2,1)S(1)} %bitcast.103), channel_id=1, source_target_pairs={{0,12},{4,8},{8,4},{12,0},{1,13},{5,9},{9,5},{13,1},{2,14},{6,10},... | collective-permute-start | bytes 589832 | tf_op jit(solution)/shard_map/d_weight/ppermute | solution.py:305
  106.0 6.9 %collective-permute-start.18 = (bf16[8,16,768]{2,1,0:T(8,128)(2,1)S(1)}, bf16[8,16,768]{2,1,0:T(8,128)(2,1)S(1)}, u32[]{:S(2)}, u32[]{:S(2)}) collective-permute-start(bf16[8,16,768]{2,1,0:T(8,128)(2,1)S(1)} %bitcast.102), channel_id=1, source_target_pairs={{0,4},{4,0},{8,12},{12,8},{1,5},{5,1},{9,13},{13,9},{2,6},{6,2},{1... | collective-permute-start | bytes 589832 | tf_op jit(solution)/shard_map/d_weight/ppermute | solution.py:305
  107.0 8.1 %collective-permute-start.19 = (bf16[8,16,768]{2,1,0:T(8,128)(2,1)S(1)}, bf16[8,16,768]{2,1,0:T(8,128)(2,1)S(1)}, u32[]{:S(2)}, u32[]{:S(2)}) collective-permute-start(bf16[8,16,768]{2,1,0:T(8,128)(2,1)S(1)} %bitcast.101), channel_id=1, source_target_pairs={{0,8},{4,12},{8,0},{12,4},{1,9},{5,13},{9,1},{13,5},{2,10},{6,14},... | collective-permute-start | bytes 589832 | tf_op jit(solution)/shard_map/d_weight/ppermute | solution.py:305
  109.9 9.8 %copy-start.2 = (bf16[256,1024]{1,0:T(8,128)(2,1)}, bf16[256,1024]{1,0:T(8,128)(2,1)S(1)}, u32[]{:S(2)}) copy-start(bf16[256,1024]{1,0:T(8,128)(2,1)S(1)} %fusion.11.mine_ref) | copy-start | bytes 1572868
  109.9 21.8 %collective-permute-start.24 = (bf16[256,1024]{1,0:T(8,128)(2,1)S(1)}, bf16[256,1024]{1,0:T(8,128)(2,1)S(1)}, u32[]{:S(2)}, u32[]{:S(2)}) collective-permute-start(bf16[256,1024]{1,0:T(8,128)(2,1)S(1)} %fusion.11.mine_ref), channel_id=1, source_target_pairs={{0,1},{1,0},{2,3},{3,2},{4,5},{5,4},{6,7},{7,6},{8,9},{9,8},{10,11... | collective-permute-start | bytes 1572872 | tf_op jit(solution)/shard_map/d_weight/ppermute | solution.py:15
  117.1 3.4 %copy-start.5 = (bf16[256,1024]{1,0:T(8,128)(2,1)}, bf16[256,1024]{1,0:T(8,128)(2,1)S(1)}, u32[]{:S(2)}) copy-start(bf16[256,1024]{1,0:T(8,128)(2,1)S(1)} %collective-permute-done.22.theirs_ref) | copy-start | bytes 1572868
  117.1 14.6 %collective-permute-start.23 = (bf16[2,2,16,768]{3,2,1,0:T(8,128)(2,1)S(1)}, bf16[2,2,16,768]{3,2,1,0:T(8,128)(2,1)S(1)}, u32[]{:S(2)}, u32[]{:S(2)}) collective-permute-start(bf16[2,2,16,768]{3,2,1,0:T(8,128)(2,1)S(1)} %fusion.29), channel_id=1, source_target_pairs={{0,16},{16,0},{1,17},{17,1},{2,18},{18,2},{3,19},{19,3},{4,20},{20... | collective-permute-start | bytes 294920 | tf_op jit(solution)/shard_map/d_weight/ppermute | solution.py:15
  119.7 12.0 %copy-start.3 = (bf16[256,1024]{1,0:T(8,128)(2,1)}, bf16[256,1024]{1,0:T(8,128)(2,1)S(1)}, u32[]{:S(2)}) copy-start(bf16[256,1024]{1,0:T(8,128)(2,1)S(1)} %fusion.12.mine_ref) | copy-start | bytes 1572868
  119.7 19.5 %collective-permute-start.16 = (bf16[256,1024]{1,0:T(8,128)(2,1)S(1)}, bf16[256,1024]{1,0:T(8,128)(2,1)S(1)}, u32[]{:S(2)}, u32[]{:S(2)}) collective-permute-start(bf16[256,1024]{1,0:T(8,128)(2,1)S(1)} %fusion.12.mine_ref), channel_id=1, source_target_pairs={{0,1},{1,0},{2,3},{3,2},{4,5},{5,4},{6,7},{7,6},{8,9},{9,8},{10,11... | collective-permute-start | bytes 1572872 | tf_op jit(solution)/shard_map/d_weight/ppermute | solution.py:15
  131.7 4.4 %copy-start.6 = (bf16[256,1024]{1,0:T(8,128)(2,1)}, bf16[256,1024]{1,0:T(8,128)(2,1)S(1)}, u32[]{:S(2)}) copy-start(bf16[256,1024]{1,0:T(8,128)(2,1)S(1)} %collective-permute-done.24.theirs_ref) | copy-start | bytes 1572868
  131.8 10.3 %collective-permute-start.25 = (f32[16,768]{1,0:T(8,128)S(1)}, f32[16,768]{1,0:T(8,128)S(1)}, u32[]{:S(2)}, u32[]{:S(2)}) collective-permute-start(f32[16,768]{1,0:T(8,128)S(1)} %select_bitcast_fusion.6), channel_id=1, source_target_pairs={{0,32},{32,0},{64,96},{96,64},{1,33},{33,1},{65,97},{97,65},{2,34}... | collective-permute-start | bytes 147464 | tf_op jit(solution)/shard_map/d_weight/ppermute | solution.py:321
  132.7 9.4 %collective-permute-start.27 = (f32[16,768]{1,0:T(8,128)S(1)}, f32[16,768]{1,0:T(8,128)S(1)}, u32[]{:S(2)}, u32[]{:S(2)}) collective-permute-start(f32[16,768]{1,0:T(8,128)S(1)} %get-tuple-element.74), channel_id=1, source_target_pairs={{0,96},{32,64},{64,32},{96,0},{1,97},{33,65},{65,33},{97,1},{2,98}... | collective-permute-start | bytes 147464 | tf_op jit(solution)/shard_map/d_weight/ppermute | solution.py:321
  134.6 7.6 %collective-permute-start.26 = (f32[16,768]{1,0:T(8,128)S(1)}, f32[16,768]{1,0:T(8,128)S(1)}, u32[]{:S(2)}, u32[]{:S(2)}) collective-permute-start(f32[16,768]{1,0:T(8,128)S(1)} %get-tuple-element.75), channel_id=1, source_target_pairs={{0,64},{32,96},{64,0},{96,32},{1,65},{33,97},{65,1},{97,33},{2,66}... | collective-permute-start | bytes 147464 | tf_op jit(solution)/shard_map/d_weight/ppermute | solution.py:320
  139.2 0.8 copy-start.7
